TPU v7x, 32 devices: a whole 2x2x4 slice. The times are simulated.
32 devices in a mesh: dp: 4 (over y, core), fsdp: 8 (over z, x).
Axes of the slice: x: 2, y: 2, z: 4, core: 2. Of those that a mesh axis runs over, the one named last changes fastest.
Arguments:
- patches: bfloat16 [32, 8, 196, 768], P(('dp', 'fsdp')), may hold values from -10 to 10
- patch_keep_mask: int32 [32, 8, 196], P(('dp', 'fsdp')), may hold values from 0 to 1, as said below
- partner: int32 [32], replicated, may hold values from 0 to 31, as said below
- matrices: float32 [18, 768, 768], P(None, 'fsdp'), may hold values from -3 to 3
- matrix_first: float32 [18, 768, 768], P(None, 'fsdp'), may hold values from -9.536743e-06 to 9.536743e-06
- matrix_second: float32 [18, 768, 768], P(None, 'fsdp'), may hold values from 1.201335e-11 to 4.787138e-11
- matrix_average: float32 [18, 768, 768], P(None, 'fsdp'), may hold values from -0.21875 to 0.21875
- head_weight: float32 [768, 256], P('fsdp'), may hold values from -0.21875 to 0.21875
- head_first: float32 [768, 256], P('fsdp'), may hold values from -3.8146973e-05 to 3.8146973e-05
- head_second: float32 [768, 256], P('fsdp'), may hold values from 1.9112148e-10 to 7.644859e-10
- head_average: float32 [768, 256], P('fsdp'), may hold values from -0.21875 to 0.21875
- vectors: float32 [227, 768], P(None, 'fsdp'), may hold values from -3 to 3
- array_running_mean: float32 [227, 768], P(None, 'fsdp'), may hold values from -3.8146973e-05 to 3.8146973e-05
- vector_second: float32 [227, 768], P(None, 'fsdp'), may hold values from 1.9112148e-11 to 7.644859e-11
- vector_average: float32 [227, 768], P(None, 'fsdp'), may hold values from -1.75 to 1.75
Outputs:
- contrastive_loss: float32 [], replicated
- squared_norm: float32 [], replicated
- new_matrices: float32 [18, 768, 768], P(None, 'fsdp')
- new_matrix_first: float32 [18, 768, 768], P(None, 'fsdp')
- revised_grid_variance: float32 [18, 768, 768], P(None, 'fsdp')
- new_matrix_average: float32 [18, 768, 768], P(None, 'fsdp')
- new_head_weight: float32 [768, 256], P('fsdp')
- new_head_first: float32 [768, 256], P('fsdp')
- new_head_second: float32 [768, 256], P('fsdp')
- new_head_average: float32 [768, 256], P('fsdp')
- new_vectors: float32 [227, 768], P(None, 'fsdp')
- new_vector_first: float32 [227, 768], P(None, 'fsdp')
- new_vector_second: float32 [227, 768], P(None, 'fsdp')
- new_vector_average: float32 [227, 768], P(None, 'fsdp')
Inputs may be any that keep to these rules, and one draw needn't show every extreme that they name: `patch_keep_mask`: frame 0 of every clip keeps all 196 patches; the other frames keep shares that differ from frame to frame. partner[partner[i]] = i and partner[i] != i for every clip i.
All inputs are finite; a program needn't handle non-finite values.
Results may differ from a plain program's by a relative error of at most 0.0055.
The roundings to bfloat16 on the way count: a program that leaves them out, or rounds other values in their place, can miss the bound.
Values may be sent and summed in bfloat16 or wider, within the bound.
A program may use at most 448 MiB of HBM per device.

v0:
```python
import jax
import jax.numpy as jnp
from jax import lax
from jax.sharding import PartitionSpec as P

D = 768
H = 12
HD = 64
F = 8
S = 196
STEP = 10


NORM_EPS = 1e-06
SCORE_SHARPNESS = 0.07
CLIP_AT = 0.05
RATE = 0.01
VECTOR_RATE = 0.1
BETA_ONE = 0.9
BETA_TWO = 0.95
ADAM_EPSILON = 1e-08
DECAY = 0.05
AVERAGE_KEEP = 0.9


def layer_norm(inputs, gain, shift):
    centred = inputs - jnp.mean(inputs, -1, keepdims=True)
    spread = jnp.mean(centred * centred, -1, keepdims=True)
    return centred * lax.rsqrt(spread + NORM_EPS) * gain + shift


def gelu_exact(values):
    return jax.nn.gelu(values, approximate=False)


def project(inputs, weight):
    return jnp.einsum("...a,ab->...b", inputs, weight, preferred_element_type=jnp.float32)


def project_back(inputs, weight, cotangent):
    rounded = cotangent.astype(jnp.bfloat16)
    back_in = jnp.einsum("...b,ab->...a", rounded, weight, preferred_element_type=jnp.float32)
    flat_in = inputs.reshape(-1, inputs.shape[-1])
    flat_back = rounded.reshape(-1, rounded.shape[-1])
    grad_weight = jnp.einsum("na,nb->ab", flat_in, flat_back, preferred_element_type=jnp.float32)
    return (back_in, grad_weight, jnp.sum(flat_back, 0, dtype=jnp.float32))


def project_many(inputs, weights):
    return jnp.einsum("...a,kab->k...b", inputs, weights, preferred_element_type=jnp.float32)


def project_many_back(inputs, weights, cotangent):
    rounded = cotangent.astype(jnp.bfloat16)
    back_in = jnp.einsum("k...b,kab->...a", rounded, weights, preferred_element_type=jnp.float32)
    flat_in = inputs.reshape(-1, inputs.shape[-1])
    flat_back = rounded.reshape(rounded.shape[0], -1, rounded.shape[-1])
    grad_weight = jnp.einsum("na,knb->kab", flat_in, flat_back, preferred_element_type=jnp.float32)
    return (back_in, grad_weight, jnp.sum(flat_back, 1, dtype=jnp.float32))


def stacked_bias(first_row, last_row, rank):
    rows = jnp.stack([first_row, jnp.zeros_like(first_row), last_row])
    return rows.reshape((3,) + (1,) * (rank - 2) + (first_row.shape[-1],))


def scores_of(query, keys, allowed):
    raw_scores = jnp.einsum(
        "blhd,bmhd->bhlm", query, keys, preferred_element_type=jnp.float32
    ) * HD ** (-0.5)
    return jnp.where(allowed[:, None, None, :], raw_scores, -1000000000.0)


def attend(query, keys, values, allowed):
    scores = scores_of(query, keys, allowed)
    highest = jnp.max(scores, -1, keepdims=True)
    expanded = jnp.exp(scores - highest)
    summed = jnp.sum(expanded, -1, keepdims=True)
    probabilities = (expanded / summed).astype(jnp.bfloat16)
    mixed = jnp.einsum("bhlm,bmhd->blhd", probabilities, values, preferred_element_type=jnp.float32)
    return (mixed, (highest + jnp.log(summed))[..., 0])


def attend_back(query, keys, values, allowed, logsum, back_out):
    scores = scores_of(query, keys, allowed)
    probabilities = jnp.exp(scores - logsum[..., None])
    back_probs = jnp.einsum("blhd,bmhd->bhlm", back_out, values, preferred_element_type=jnp.float32)
    inner = jnp.sum(back_probs * probabilities, -1, keepdims=True)
    back_scores = (probabilities * (back_probs - inner)).astype(jnp.bfloat16)
    factor = HD ** (-0.5)
    back_query = (
        jnp.einsum("bhlm,bmhd->blhd", back_scores, keys, preferred_element_type=jnp.float32)
        * factor
    )
    back_keys = (
        jnp.einsum("bhlm,blhd->bmhd", back_scores, query, preferred_element_type=jnp.float32)
        * factor
    )
    back_values = jnp.einsum(
        "bhlm,blhd->bmhd",
        probabilities.astype(jnp.bfloat16),
        back_out,
        preferred_element_type=jnp.float32,
    )
    return (back_query, back_keys, back_values)


def per_patch(tensor, clip_count):
    return (
        tensor.reshape(clip_count, F, S, H, HD)
        .transpose(0, 2, 1, 3, 4)
        .reshape(clip_count * S, F, H, HD)
    )


def from_patch(tensor, clip_count):
    return (
        tensor.reshape(clip_count, S, F, H, HD)
        .transpose(0, 2, 1, 3, 4)
        .reshape(clip_count, F, S, H * HD)
    )


def per_frame(tensor, clip_count):
    width = tensor.shape[-1]
    leading = jnp.broadcast_to(tensor[:, None, :1], (clip_count, F, 1, width))
    framed = jnp.concatenate([leading, tensor[:, 1:].reshape(clip_count, F, S, width)], 2)
    return framed.reshape(clip_count * F, S + 1, H, HD)


def from_frame(tensor, clip_count):
    framed = tensor.reshape(clip_count, F, S + 1, H * HD)
    return jnp.concatenate(
        [jnp.sum(framed[:, :, :1], 1), framed[:, :, 1:].reshape(clip_count, F * S, H * HD)], 1
    )


def forward(mats16, head16, vectors, patches, patch_keep_mask):
    clip_count = patches.shape[0]
    alive = patch_keep_mask > 0
    embedded = project(patches, mats16[0]) + vectors[9]
    start_rows = embedded + vectors[31 : 31 + S][None, None] + vectors[1 : 1 + F][None, :, None]
    normed_time = layer_norm(start_rows, vectors[22], vectors[23]).astype(jnp.bfloat16)
    triple_time = (
        project_many(normed_time, mats16[1:4]) + stacked_bias(vectors[10], vectors[11], 5)
    ).astype(jnp.bfloat16)
    live_time = alive.transpose(0, 2, 1).reshape(clip_count * S, F)
    mixed_time, logsum_time = attend(
        per_patch(triple_time[0], clip_count),
        per_patch(triple_time[1], clip_count),
        per_patch(triple_time[2], clip_count),
        live_time,
    )
    mixed_time = from_patch(mixed_time, clip_count).astype(jnp.bfloat16)
    moved_time = (project(mixed_time, mats16[4]) + vectors[12]).astype(jnp.bfloat16)
    after_time = start_rows + project(moved_time, mats16[5]) + vectors[13]
    leading = jnp.broadcast_to(vectors[0] + vectors[30], (clip_count, 1, D))
    joined = jnp.concatenate([leading, after_time.reshape(clip_count, F * S, D)], 1)
    normed_space = layer_norm(joined, vectors[24], vectors[25]).astype(jnp.bfloat16)
    triple_space = (
        project_many(normed_space, mats16[6:9]) + stacked_bias(vectors[14], vectors[15], 4)
    ).astype(jnp.bfloat16)
    live_space = jnp.concatenate([jnp.ones((clip_count, F, 1), jnp.bool_), alive], 2).reshape(
        clip_count * F, S + 1
    )
    mixed_space, logsum_space = attend(
        per_frame(triple_space[0], clip_count),
        per_frame(triple_space[1], clip_count),
        per_frame(triple_space[2], clip_count),
        live_space,
    )
    mixed_space = mixed_space.reshape(clip_count, F, S + 1, D)
    mixed_space = jnp.concatenate(
        [jnp.mean(mixed_space[:, :, :1], 1), mixed_space[:, :, 1:].reshape(clip_count, F * S, D)], 1
    ).astype(jnp.bfloat16)
    after_space = joined + project(mixed_space, mats16[9]) + vectors[16]
    normed_mlp = layer_norm(after_space, vectors[26], vectors[27]).astype(jnp.bfloat16)
    hidden = project_many(normed_mlp, mats16[10:14]) + vectors[17:21][:, None, None, :]
    activated = gelu_exact(hidden).astype(jnp.bfloat16)
    after_mlp = (
        after_space
        + jnp.einsum("kcna,kab->cnb", activated, mats16[14:18], preferred_element_type=jnp.float32)
        + vectors[21]
    )
    pooled = jnp.mean(layer_norm(after_mlp, vectors[28], vectors[29]), 1).astype(jnp.bfloat16)
    projected = project(pooled, head16)
    saved = (
        start_rows,
        normed_time,
        triple_time,
        live_time,
        logsum_time,
        mixed_time,
        moved_time,
        joined,
        normed_space,
        triple_space,
        live_space,
        logsum_space,
        mixed_space,
        after_space,
        normed_mlp,
        hidden,
        activated,
        after_mlp,
        pooled,
    )
    return (projected, saved)


def backward(mats16, head16, vectors, patches, saved, back_projected):
    (
        start_rows,
        normed_time,
        triple_time,
        live_time,
        logsum_time,
        mixed_time,
        moved_time,
        joined,
        normed_space,
        triple_space,
        live_space,
        logsum_space,
        mixed_space,
        after_space,
        normed_mlp,
        hidden,
        activated,
        after_mlp,
        pooled,
    ) = saved
    clip_count = start_rows.shape[0]
    rows_clip = joined.shape[1]
    back_pooled, grad_head, unused_bias = project_back(pooled, head16, back_projected)
    unused_out, norm_back = jax.vjp(layer_norm, after_mlp, vectors[28], vectors[29])
    reverse_perceptron, gain_final, shift_final = norm_back(
        jnp.broadcast_to(back_pooled[:, None] / rows_clip, after_mlp.shape)
    )
    rounded = reverse_perceptron.astype(jnp.bfloat16)
    back_activated = jnp.einsum(
        "cnb,kab->kcna", rounded, mats16[14:18], preferred_element_type=jnp.float32
    )
    grad_down = jnp.einsum("kcna,cnb->kab", activated, rounded, preferred_element_type=jnp.float32)
    bias_down = jnp.sum(rounded, (0, 1), dtype=jnp.float32)
    unused_out, gelu_back = jax.vjp(gelu_exact, hidden)
    (back_hidden,) = gelu_back(back_activated)
    back_normed, grad_up, bias_up = project_many_back(normed_mlp, mats16[10:14], back_hidden)
    unused_out, norm_back = jax.vjp(layer_norm, after_space, vectors[26], vectors[27])
    back_norm_in, gain_mlp, shift_mlp = norm_back(back_normed)
    back_space = reverse_perceptron + back_norm_in
    back_mixed, grad_proj_space, bias_proj_space = project_back(mixed_space, mats16[9], back_space)
    back_mixed = back_mixed.astype(jnp.bfloat16)
    head_rows = (back_mixed[:, None, :1].astype(jnp.float32) / F).astype(jnp.bfloat16)
    back_frames = jnp.concatenate(
        [
            jnp.broadcast_to(head_rows, (clip_count, F, 1, D)),
            back_mixed[:, 1:].reshape(clip_count, F, S, D),
        ],
        2,
    ).reshape(clip_count * F, S + 1, H, HD)
    back_query, back_keys, back_values = attend_back(
        per_frame(triple_space[0], clip_count),
        per_frame(triple_space[1], clip_count),
        per_frame(triple_space[2], clip_count),
        live_space,
        logsum_space,
        back_frames,
    )
    back_triple = jnp.stack(
        [
            from_frame(back_query, clip_count),
            from_frame(back_keys, clip_count),
            from_frame(back_values, clip_count),
        ]
    )
    back_normed, grad_triple_space, bias_triple_space = project_many_back(
        normed_space, mats16[6:9], back_triple
    )
    unused_out, norm_back = jax.vjp(layer_norm, joined, vectors[24], vectors[25])
    back_norm_in, gain_space, shift_space = norm_back(back_normed)
    back_joined = back_space + back_norm_in
    back_class = jnp.sum(back_joined[:, 0], 0)
    back_after = back_joined[:, 1:].reshape(clip_count, F, S, D)
    back_moved, grad_fc_time, bias_fc_time = project_back(moved_time, mats16[5], back_after)
    back_mixed, grad_proj_time, bias_proj_time = project_back(mixed_time, mats16[4], back_moved)
    back_mixed = per_patch(back_mixed.astype(jnp.bfloat16), clip_count)
    back_query, back_keys, back_values = attend_back(
        per_patch(triple_time[0], clip_count),
        per_patch(triple_time[1], clip_count),
        per_patch(triple_time[2], clip_count),
        live_time,
        logsum_time,
        back_mixed,
    )
    back_triple = jnp.stack(
        [
            from_patch(back_query, clip_count),
            from_patch(back_keys, clip_count),
            from_patch(back_values, clip_count),
        ]
    )
    back_normed, grad_triple_time, bias_triple_time = project_many_back(
        normed_time, mats16[1:4], back_triple
    )
    unused_out, norm_back = jax.vjp(layer_norm, start_rows, vectors[22], vectors[23])
    back_norm_in, gain_time, shift_time = norm_back(back_normed)
    back_start = back_after + back_norm_in
    rounded = back_start.astype(jnp.bfloat16).reshape(-1, D)
    grad_embed = jnp.einsum(
        "na,nb->ab",
        patches.reshape(-1, patches.shape[-1]),
        rounded,
        preferred_element_type=jnp.float32,
    )
    embedding_bias = jnp.sum(rounded, 0, dtype=jnp.float32)
    grad_mats = jnp.concatenate(
        [
            grad_embed[None],
            grad_triple_time,
            grad_proj_time[None],
            grad_fc_time[None],
            grad_triple_space,
            grad_proj_space[None],
            grad_up,
            grad_down,
        ],
        0,
    )
    grad_vecs = jnp.concatenate(
        [
            back_class[None],
            jnp.sum(back_start, (0, 2)),
            embedding_bias[None],
            bias_triple_time[0][None],
            bias_triple_time[2][None],
            bias_proj_time[None],
            bias_fc_time[None],
            bias_triple_space[0][None],
            bias_triple_space[2][None],
            bias_proj_space[None],
            bias_up,
            bias_down[None],
            jnp.stack(
                [
                    gain_time,
                    shift_time,
                    gain_space,
                    shift_space,
                    gain_mlp,
                    shift_mlp,
                    gain_final,
                    shift_final,
                ]
            ),
            back_class[None],
            jnp.sum(back_start, (0, 1)),
        ],
        0,
    )
    return (grad_mats, grad_head, grad_vecs)


def normalize(projected):
    return projected * lax.rsqrt(jnp.sum(projected * projected, -1, keepdims=True) + 1e-06)


def adamw_step(weight, first, second, average, gradient, factor, rate):
    clipped = gradient * factor
    first = BETA_ONE * first + (1.0 - BETA_ONE) * clipped
    second = BETA_TWO * second + (1.0 - BETA_TWO) * clipped * clipped
    first_hat = first / (1.0 - BETA_ONE**STEP)
    second_hat = second / (1.0 - BETA_TWO**STEP)
    weight = weight - rate * (first_hat / (jnp.sqrt(second_hat) + ADAM_EPSILON) + DECAY * weight)
    average = AVERAGE_KEEP * average + (1.0 - AVERAGE_KEEP) * weight
    return (weight, first, second, average)


def local(
    patches,
    patch_keep_mask,
    partner,
    matrices,
    matrix_first,
    matrix_second,
    matrix_average,
    head_weight,
    head_first,
    head_second,
    head_average,
    vectors,
    array_running_mean,
    vector_second,
    vector_average,
):
    shards = (
        matrices.astype(jnp.bfloat16),
        head_weight.astype(jnp.bfloat16),
        vectors.astype(jnp.bfloat16),
    )
    mats16, head16, vecs16 = (
        lax.all_gather(shards[0], "fsdp", axis=1, tiled=True),
        lax.all_gather(shards[1], "fsdp", axis=0, tiled=True),
        lax.all_gather(shards[2], "fsdp", axis=1, tiled=True),
    )
    projected, saved = forward(mats16, head16, vecs16.astype(jnp.float32), patches, patch_keep_mask)
    unit_length_lines, unit_back = jax.vjp(normalize, projected)
    gathered = lax.all_gather(unit_length_lines, ("dp", "fsdp"), axis=0, tiled=True)

    def contrast(gathered_rows):
        pairwise_affinity_scores_raw = (
            jnp.dot(gathered_rows, gathered_rows.T, precision=lax.Precision.HIGHEST)
            / SCORE_SHARPNESS
        )
        clip_total = pairwise_affinity_scores_raw.shape[0]
        column = jnp.arange(clip_total)[None, :]
        pairwise_affinity_scores_raw = jnp.where(
            jnp.arange(clip_total)[:, None] == column, -1000000000.0, pairwise_affinity_scores_raw
        )
        positive = jnp.sum(
            jnp.where(column == partner[:, None], pairwise_affinity_scores_raw, 0.0), -1
        )
        return jnp.mean(jax.nn.logsumexp(pairwise_affinity_scores_raw, -1) - positive)

    contrastive_loss, objective_cotangent_flow = jax.vjp(contrast, gathered)
    (back_gathered,) = objective_cotangent_flow(jnp.ones_like(contrastive_loss))
    clip_count = projected.shape[0]
    offset = lax.axis_index(("dp", "fsdp")) * clip_count
    back_unit = lax.dynamic_slice_in_dim(back_gathered, offset, clip_count, 0)
    (back_projected,) = unit_back(back_unit)
    back_weights = (
        lax.all_gather(shards[0], "fsdp", axis=1, tiled=True),
        lax.all_gather(shards[1], "fsdp", axis=0, tiled=True),
        lax.all_gather(shards[2], "fsdp", axis=1, tiled=True),
    )
    grad_mats, grad_head, grad_vecs = backward(
        back_weights[0],
        back_weights[1],
        back_weights[2].astype(jnp.float32),
        patches,
        saved,
        back_projected,
    )
    grad_mats, grad_head, grad_vecs = (
        lax.psum_scatter(grad_mats, "fsdp", scatter_dimension=1, tiled=True),
        lax.psum_scatter(grad_head, "fsdp", scatter_dimension=0, tiled=True),
        lax.psum_scatter(grad_vecs, "fsdp", scatter_dimension=1, tiled=True),
    )
    grad_mats, grad_head, grad_vecs = lax.psum((grad_mats, grad_head, grad_vecs), "dp")
    partial_squares = (
        jnp.sum(grad_mats * grad_mats)
        + jnp.sum(grad_head * grad_head)
        + jnp.sum(grad_vecs * grad_vecs)
    )
    squared_norm = lax.psum(partial_squares, "fsdp")
    factor = CLIP_AT / jnp.maximum(jnp.sqrt(squared_norm), CLIP_AT)
    mats_out = adamw_step(
        matrices, matrix_first, matrix_second, matrix_average, grad_mats, factor, RATE
    )
    head_out = adamw_step(
        head_weight, head_first, head_second, head_average, grad_head, factor, RATE
    )
    vecs_out = adamw_step(
        vectors, array_running_mean, vector_second, vector_average, grad_vecs, factor, VECTOR_RATE
    )
    return (
        contrastive_loss,
        squared_norm,
        mats_out[0],
        mats_out[1],
        mats_out[2],
        mats_out[3],
        head_out[0],
        head_out[1],
        head_out[2],
        head_out[3],
        vecs_out[0],
        vecs_out[1],
        vecs_out[2],
        vecs_out[3],
    )


def solution(mesh):
    placed = (
        P(("dp", "fsdp"), None, None, None),
        P(("dp", "fsdp"), None, None),
        P(),
        P(None, "fsdp", None),
        P(None, "fsdp", None),
        P(None, "fsdp", None),
        P(None, "fsdp", None),
        P("fsdp", None),
        P("fsdp", None),
        P("fsdp", None),
        P("fsdp", None),
        P(None, "fsdp"),
        P(None, "fsdp"),
        P(None, "fsdp"),
        P(None, "fsdp"),
    )
    return jax.shard_map(
        local,
        mesh=mesh,
        in_specs=placed,
        out_specs=(
            P(),
            P(),
            P(None, "fsdp", None),
            P(None, "fsdp", None),
            P(None, "fsdp", None),
            P(None, "fsdp", None),
            P("fsdp", None),
            P("fsdp", None),
            P("fsdp", None),
            P("fsdp", None),
            P(None, "fsdp"),
            P(None, "fsdp"),
            P(None, "fsdp"),
            P(None, "fsdp"),
        ),
        check_vma=False,
    )
```

profile of v0, /device:TPU:0, one launch (start us, length us, event | category | flops | bytes accessed | tf_op | source)
XLA Modules:
  0.0 2339.3 jit_solution(5097292605749882801)
XLA Ops:
  11.7 64.1 %all_gather.15 = bf16[227,768]{0,1:T(8,128)(2,1)S(1)} all-gather(bf16[227,96]{0,1:T(8,128)(2,1)S(1)} %convert_element_type.207), channel_id=1, replica_groups=mesh['dp'=4,'fsdp'=8] {'fsdp'}, dimensions={1}, use_global_device_ids=true | all-gather | bytes 392256 | tf_op jit(solution)/shard_map/all_gather | solution.py:404
  76.9 48.1 %all_gather.17 = bf16[768,256]{1,0:T(8,128)(2,1)} all-gather(bf16[96,256]{1,0:T(8,128)(2,1)S(1)} %convert_element_type.227), channel_id=1, replica_groups=mesh['dp'=4,'fsdp'=8] {'fsdp'}, dimensions={0}, use_global_device_ids=true | all-gather | bytes 442368 | tf_op jit(solution)/shard_map/all_gather | solution.py:403
  125.8 308.8 %all-gather.4.cloned.1.call-done = bf16[18,768,768]{2,1,0:T(8,128)(2,1)} async-done(((bf16[18,96,768]{2,1,0:T(8,128)(2,1)}), bf16[18,768,768]{2,1,0:T(8,128)(2,1)}) %all-gather.4.cloned.1.call-update) | async-done | bytes 21233680 | tf_op jit(solution)/shard_map/all_gather | solution.py:402
  611.9 12.0 fusion.179
  623.9 11.5 fusion.24
  668.5 13.3 fusion.63
  681.8 43.4 %fusion.160.clone.5 = bf16[4,1569,768]{2,1,0:T(8,128)(2,1)} fusion(f32[1569,4,768]{2,0,1:T(8,128)S(1)} %fusion.63, f32[4,768]{1,0:T(4,128)S(1)} %copy-done.94), kind=kLoop, calls=%fused_computation.52.clone.1.clone.clone.clone.2 | loop fusion | flops 318117888 | bytes 28932096 | tf_op jit(solution)/shard_map/reduce_sum | solution.py:27
  725.3 19.8 fusion.181
  749.1 66.8 %all-gather.1 = f32[32,1,256]{2,1,0:T(1,128)S(1)} all-gather(f32[1,1,256]{2,1,0:T(1,128)S(1)} %bitcast.500), channel_id=2, replica_groups=mesh['dp'=4,'fsdp'=8] {'dp','fsdp'}, dimensions={0}, use_global_device_ids=true | all-gather | bytes 33792 | tf_op jit(solution)/shard_map/all_gather | solution.py:408
  827.8 56.8 %convert_reduce_fusion = (f32[4,768]{1,0:T(4,128)}, bf16[4,1,1569,768]{3,2,0,1:T(8,128)(2,1)}) fusion(bf16[18,768,768]{2,1,0:T(8,128)(2,1)} %all-gather.4.cloned.1.call-done, bf16[1569,768]{1,0:T(8,128)(2,1)S(1)} %get-tuple-element.117, f32[4,768]{1,0:T(4,128)S(1)} %copy-done.94, f32[1569,4,768]{2,0,1:T(8,128)} %copy-done.11), kind=kOutput, calls=%fused_computation.26 | convolution fusion | flops 7764965376 | bytes 36158976 | tf_op jit(solution)/shard_map/cnb,kab->kcna/dot_general | solution.py:241
  884.6 15.1 fusion.44
  924.6 15.6 multiply_reduce_fusion
  940.2 14.1 multiply_convert_fusion
  1023.8 13.2 bitcast_reduce_fusion.1
  1215.4 15.1 bitcast_dynamic-update-slice_fusion
  1230.5 55.9 %convolution_dynamic-update-slice_fusion = f32[18,768,768]{1,2,0:T(8,128)} fusion(f32[18,768,768]{1,2,0:T(8,128)} %bitcast_dynamic-update-slice_fusion, bf16[1569,768]{1,0:T(8,128)(2,1)S(1)} %copy-done.43, f32[1569,4,768]{2,0,1:T(8,128)S(1)} %bitcast.475, f32[4,768]{1,0:T(4,128)S(1)} %copy-done.95), kind=kOutput, calls=%fused_computation.136 | convolution fusion | flops 7721588736 | bytes 31139328 | tf_op jit(solution)/shard_map/kcna,cnb->kab/dot_general | solution.py:244
  1286.4 50.3 %copy.397 = f32[18,768,768]{2,0,1:T(8,128)} copy(f32[18,768,768]{1,2,0:T(8,128)} %convolution_dynamic-update-slice_fusion) | data formatting | bytes 84934656
  1336.7 34.3 %copy.407 = f32[96,8,18,768]{3,1,2,0:T(8,128)} copy(f32[96,8,18,768]{3,2,1,0:T(8,128)} %bitcast.455) | data formatting | bytes 84934656
  1423.6 616.9 %reduce-scatter.10.cloned.1.call-done = f32[96,13824]{1,0:T(8,128)} async-done(((f32[768,13824]{1,0:T(8,128)}), f32[96,13824]{1,0:T(8,128)}) %reduce-scatter.10.cloned.1.call-update) | async-done | bytes 5308432
  2053.8 52.6 %reduce-scatter.12.cloned.1.call-done = f32[96,227]{1,0:T(8,128)} async-done(((f32[768,227]{1,0:T(8,128)}), f32[96,227]{1,0:T(8,128)}) %reduce-scatter.12.cloned.1.call-update) | async-done | bytes 87184
  2106.3 65.2 %reduce-scatter.8.cloned.1.call-done = f32[96,256]{1,0:T(8,128)} async-done(((f32[768,256]{1,0:T(8,128)}), f32[96,256]{1,0:T(8,128)}) %reduce-scatter.8.cloned.1.call-update) | async-done | bytes 98320 | tf_op jit(solution)/shard_map/reduce_scatter | solution.py:446
  2171.6 109.1 %all-reduce.4.cloned.1.call-done = (f32[18,96,768]{2,1,0:T(8,128)}, f32[96,256]{1,0:T(8,128)}, f32[227,96]{0,1:T(8,128)}) async-done(((f32[18,96,768]{2,1,0:T(8,128)}, f32[96,256]{1,0:T(8,128)}, f32[227,96]{0,1:T(8,128)}), (f32[18,96,768]{2,1,0:T(8,128)}, f32[96,256]{1,0:T(8,128)}, f32[227,96]{0,1:T(8,128)})) %all-reduce.4.cloned.1.call-update) | async-done | bytes 5493904 | tf_op jit(solution)/shard_map/psum | solution.py:449
  2289.1 21.9 psum.31
  2313.3 18.2 multiply_add_fusion
  (560 shorter events, 575.4 us)
Async XLA Ops:
  7.2 427.4 %all-gather.4.cloned.1.call-start = ((), (), s32[]{:S(2)}) async-start(), calls=%async_computation.3 | async-start | bytes 23887872 | tf_op jit(solution)/shard_map/all_gather | solution.py:402
  11.6 2028.8 %reduce-scatter.10.cloned.1.call-start = ((), (), s32[]{:S(2)}) async-start(), calls=%async_computation.5 | async-start | bytes 47775744
  125.0 363.7 %copy-start.105 = (pred[196,8]{0,1:T(8,128)(4,1)}, pred[196,8]{0,1:T(8,128)(4,1)S(1)}, u32[]{:S(2)}) copy-start(pred[196,8]{0,1:T(8,128)(4,1)S(1)} %fusion.205) | copy-start | bytes 4708
  125.8 315.5 %copy-start.96 = (f32[768]{0:T(1024)}, f32[768]{0:T(1024)S(1)}, u32[]{:S(2)}) copy-start(f32[768]{0:T(1024)S(1)} %get-tuple-element.96) | copy-start | bytes 9220
  125.8 315.5 %copy-start.132 = (f32[768]{0:T(1024)}, f32[768]{0:T(1024)S(1)}, u32[]{:S(2)}) copy-start(f32[768]{0:T(1024)S(1)} %get-tuple-element.95) | copy-start | bytes 9220
  125.8 423.2 %copy-start.99 = (f32[768]{0:T(1024)}, f32[768]{0:T(1024)S(1)}, u32[]{:S(2)}) copy-start(f32[768]{0:T(1024)S(1)} %get-tuple-element.92) | copy-start | bytes 9220
  125.8 423.2 %copy-start.130 = (f32[768]{0:T(1024)}, f32[768]{0:T(1024)S(1)}, u32[]{:S(2)}) copy-start(f32[768]{0:T(1024)S(1)} %get-tuple-element.91) | copy-start | bytes 9220
  125.8 534.3 %copy-start.77 = (f32[1,768]{1,0:T(1,128)}, f32[1,768]{1,0:T(1,128)S(1)}, u32[]{:S(2)}) copy-start(f32[1,768]{1,0:T(1,128)S(1)} %get-tuple-element.138) | copy-start | bytes 9220
  745.1 80.1 %copy-start.50 = (f32[1569]{0:T(1024)}, f32[1569]{0:T(1024)S(1)}, u32[]{:S(2)}) copy-start(f32[1569]{0:T(1024)S(1)} %broadcast_multiply_fusion.3) | copy-start | bytes 18832
  745.8 79.4 %copy-start.60 = (f32[1569]{0:T(1024)}, f32[1569]{0:T(1024)S(1)}, u32[]{:S(2)}) copy-start(f32[1569]{0:T(1024)S(1)} %fusion.122) | copy-start | bytes 18832
  1004.4 195.6 %copy-start.119 = (bf16[1,1,768]{2,1,0:T(2,128)(2,1)}, bf16[1,1,768]{2,1,0:T(2,128)(2,1)S(1)}, u32[]{:S(2)}) copy-start(bf16[1,1,768]{2,1,0:T(2,128)(2,1)S(1)} %reduce_sum.489) | copy-start | bytes 4612
  1016.0 184.1 %copy-start.121 = (bf16[1,1,768]{2,1,0:T(2,128)(2,1)}, bf16[1,1,768]{2,1,0:T(2,128)(2,1)S(1)}, u32[]{:S(2)}) copy-start(bf16[1,1,768]{2,1,0:T(2,128)(2,1)S(1)} %reduce_sum.491) | copy-start | bytes 4612
  1023.8 176.2 %copy-start.123 = (bf16[1,1,768]{2,1,0:T(2,128)(2,1)}, bf16[1,1,768]{2,1,0:T(2,128)(2,1)S(1)}, u32[]{:S(2)}) copy-start(bf16[1,1,768]{2,1,0:T(2,128)(2,1)S(1)} %reduce_sum.496) | copy-start | bytes 4612
  1371.0 735.4 %reduce-scatter.12.cloned.1.call-start = ((), (), s32[]{:S(2)}) async-start(), calls=%async_computation.6 | async-start | bytes 884736
  1422.3 749.2 %reduce-scatter.8.cloned.1.call-start = ((), (), s32[]{:S(2)}) async-start(), calls=%async_computation.4 | async-start | bytes 884736 | tf_op jit(solution)/shard_map/reduce_scatter | solution.py:446
  1423.5 857.2 %all-reduce.4.cloned.1.call-start = ((), (), s32[]{:S(2)}) async-start(), calls=%async_computation.7 | async-start | bytes 11010048 | tf_op jit(solution)/shard_map/psum | solution.py:449
  2171.5 140.2 %copy-start.55 = (f32[227,96]{0,1:T(8,128)S(1)}, f32[227,96]{0,1:T(8,128)}, u32[]{:S(2)}) copy-start(f32[227,96]{0,1:T(8,128)} %param.26) | copy-start | bytes 261508
  2171.5 140.2 %copy-start.71 = (f32[227,96]{0,1:T(8,128)S(1)}, f32[227,96]{0,1:T(8,128)}, u32[]{:S(2)}) copy-start(f32[227,96]{0,1:T(8,128)} %param.29) | copy-start | bytes 261508
  2171.5 140.2 %copy-start.72 = (f32[227,96]{0,1:T(8,128)S(1)}, f32[227,96]{0,1:T(8,128)}, u32[]{:S(2)}) copy-start(f32[227,96]{0,1:T(8,128)} %param.27) | copy-start | bytes 261508
  2171.5 140.2 %copy-start.73 = (f32[227,96]{0,1:T(8,128)S(1)}, f32[227,96]{0,1:T(8,128)}, u32[]{:S(2)}) copy-start(f32[227,96]{0,1:T(8,128)} %param.28) | copy-start | bytes 261508
  2171.5 141.0 %copy-start.57 = (f32[96,256]{1,0:T(8,128)S(1)}, f32[96,256]{1,0:T(8,128)}, u32[]{:S(2)}) copy-start(f32[96,256]{1,0:T(8,128)} %param.22) | copy-start | bytes 294916
  2171.5 141.0 %copy-start.74 = (f32[96,256]{1,0:T(8,128)S(1)}, f32[96,256]{1,0:T(8,128)}, u32[]{:S(2)}) copy-start(f32[96,256]{1,0:T(8,128)} %param.25) | copy-start | bytes 294916
  2171.5 141.0 %copy-start.75 = (f32[96,256]{1,0:T(8,128)S(1)}, f32[96,256]{1,0:T(8,128)}, u32[]{:S(2)}) copy-start(f32[96,256]{1,0:T(8,128)} %param.23) | copy-start | bytes 294916
  2171.6 141.0 %copy-start.76 = (f32[96,256]{1,0:T(8,128)S(1)}, f32[96,256]{1,0:T(8,128)}, u32[]{:S(2)}) copy-start(f32[96,256]{1,0:T(8,128)} %param.24) | copy-start | bytes 294916
  (150 other events, 1898.7 us)
Sparse Core Ops, SparseCore 0:
  11.7 422.8 all-gather.3
  1371.1 669.3 reduce-scatter.9
  2044.7 61.6 reduce-scatter.11
  2110.1 61.4 reduce-scatter.7
  2174.6 106.0 all-reduce.3
where the time goes:
time: 2350 us; the launch traced here: 2340 us
  waiting for transfers between devices  1150 us (49%)
  matrix products  413 us (18%)
  local copies, waits for them, and re-layouts  394 us (17%)
  blocking collectives  201 us (9%)
  other arithmetic  156 us (7%)
    unnamed x7, waiting for transfers between devices  670 us
    all_gather x1, waiting for transfers between devices, local(): lax.all_gather(shards[0], 'fsdp', axis=1, tiled=True)  309 us
    unnamed x346, local copies, waits for them, and re-layouts  113 us
    psum x1, waiting for transfers between devices, local(): lax.psum((grad_mats, grad_head, grad_vecs), 'dp')  109 us
    all_gather x1, blocking collectives, local(): lax.all_gather(unit_length_lines, ('dp', 'fsdp'), axis=0, tiled=True)  66.8 us
    reduce_scatter x1, waiting for transfers between devices, local(): lax.psum_scatter(grad_head, 'fsdp', scatter_dimension=0, tiled=True)  65.2 us
    all_gather x1, blocking collectives, local(): lax.all_gather(shards[2], 'fsdp', axis=1, tiled=True)  64.1 us
    dot_general x1, matrix products, backward(): jnp.einsum('cnb,kab->kcna', rounded, mats16[14:18], preferred_element_typ...  56.8 us
  transfers between devices with their start and end apart: 5, of which 5 were waited for; matrix products, arithmetic and copies ran while one was open for 3% of the time, Pallas kernels for 0%

commit v1 on v0

--- a/solution.py
+++ b/solution.py
@@ -1,6 +1,9 @@
+import functools
 import jax
 import jax.numpy as jnp
 from jax import lax
+from jax.experimental import pallas as pl
+from jax.experimental.pallas import tpu as pltpu
 from jax.sharding import PartitionSpec as P
 
 D = 768
@@ -8,6 +11,7 @@
 HD = 64
 F = 8
 S = 196
+NVEC = 227
 STEP = 10
 
 
@@ -22,6 +26,408 @@
 DECAY = 0.05
 AVERAGE_KEEP = 0.9
 
+
+NMAT = 18
+MESH = pl.DeviceIdType.MESH
+ANY = pl.BlockSpec(memory_space=pl.ANY)
+
+
+class Layout:
+    def __init__(self, dp, fsdp, split):
+        self.dp, self.n = dp, fsdp
+        self.outer = 4 if fsdp % 4 == 0 else 1
+        self.inner = fsdp // self.outer
+        self.planes = dp // 2
+        self.half = NMAT // 2
+        self.split = split
+        self.common = self.half - split * self.planes
+        self.handled = self.common + split
+        self.rows = D // fsdp
+
+    def place(self):
+        i = lax.axis_index("fsdp")
+        d = lax.axis_index("dp")
+        return i, lax.div(i, self.inner), lax.rem(i, self.inner), lax.div(d, 2), lax.rem(d, 2)
+
+    def peer(self, i, y, c):
+        return {"fsdp": i, "dp": y * 2 + c}
+
+    def matrix(self, c, y, k):
+        if k < self.common:
+            return c * self.half + k
+        return c * self.half + self.common + y * self.split + (k - self.common)
+
+
+def turn(x, t, size):
+    return lax.rem(x + t + size, size)
+
+
+def greet(lay, i, a, b, y, c):
+    barrier = pltpu.get_barrier_semaphore()
+    others = [lay.peer(turn(a, t, lay.outer) * lay.inner + b, y, c) for t in range(1, lay.outer)]
+    others += [lay.peer(a * lay.inner + turn(b, u, lay.inner), y, c) for u in range(1, lay.inner)]
+    others += [lay.peer(i, turn(y, v, lay.planes), c) for v in range(1, lay.planes)]
+    others += [lay.peer(i, y, 1 - c)]
+    for other in others:
+        pl.semaphore_signal(barrier, inc=1, device_id=other, device_id_type=MESH)
+    pl.semaphore_wait(barrier, len(others))
+
+
+def gather_kernel(lay, w_ref, s_ref, ow_ref, os_ref, own_sem, zs, zr, xs, xr, ys, yr, cs, cr, small):
+    i, a, b, y, c = lay.place()
+    A, B = lay.outer, lay.inner
+    greet(lay, i, a, b, y, c)
+    pending = []
+
+    def remote(src, dst, ssem, rsem, dev):
+        copy = pltpu.make_async_remote_copy(
+            src_ref=src, dst_ref=dst, send_sem=ssem, recv_sem=rsem, device_id=dev, device_id_type=MESH
+        )
+        copy.start()
+        pending.append(copy)
+        return copy
+
+    def landed(dst, ssem, rsem, dev):
+        pltpu.make_async_remote_copy(
+            src_ref=dst, dst_ref=dst, send_sem=ssem, recv_sem=rsem, device_id=dev, device_id_type=MESH
+        ).wait_recv()
+
+    K = lay.handled
+    here = lay.peer(i, y, 1 - c)
+    local_small = pltpu.make_async_copy(s_ref, os_ref.at[i], own_sem.at[0])
+    local_small.start()
+    for k in [-1] + list(range(lay.common, K)) + list(range(lay.common)):
+        src = s_ref if k < 0 else w_ref.at[lay.matrix(c, y, k)]
+        dst = os_ref.at[i] if k < 0 else ow_ref.at[lay.matrix(c, y, k), i]
+        for t in range(1, A):
+            remote(src, dst, zs.at[k + 1, t], zr.at[k + 1, t], lay.peer(turn(a, t, A) * B + b, y, c))
+        for u in range(1, B):
+            remote(src, dst, xs.at[k + 1, u, 0], xr.at[k + 1, u, 0], lay.peer(a * B + turn(b, u, B), y, c))
+    locals_ = []
+    for first, count in ((lay.matrix(c, y, 0), lay.common), (lay.matrix(c, y, lay.common), lay.split)):
+        if count:
+            span = pl.ds(first, count)
+            locals_.append(pltpu.make_async_copy(w_ref.at[span], ow_ref.at[span, i], own_sem.at[1 + len(locals_)]))
+            locals_[-1].start()
+    order = [-1] + list(range(lay.common, K)) + list(range(lay.common))
+
+    def at(k, j):
+        return os_ref.at[j] if k < 0 else ow_ref.at[lay.matrix(c, y, k), j]
+
+    def cross(k):
+        for t in range(1, A):
+            j = turn(a, -t, A) * B + b
+            landed(at(k, j), zs.at[k + 1, t], zr.at[k + 1, t], here)
+            for u in range(1, B):
+                remote(at(k, j), at(k, j), xs.at[k + 1, u, t], xr.at[k + 1, u, t], lay.peer(a * B + turn(b, u, B), y, c))
+
+    def share(k):
+        for u in range(1, B):
+            for t in range(A):
+                j = turn(a, -t, A) * B + turn(b, -u, B)
+                landed(at(k, j), xs.at[k + 1, u, t], xr.at[k + 1, u, t], here)
+        if k >= 0:
+            m = lay.matrix(c, y, k)
+            if k >= lay.common:
+                for v in range(1, lay.planes):
+                    q = k - lay.common
+                    remote(ow_ref.at[m], ow_ref.at[m], ys.at[q, v], yr.at[q, v], lay.peer(i, turn(y, v, lay.planes), c))
+            remote(ow_ref.at[m], ow_ref.at[m], cs.at[k], cr.at[k], here)
+
+    for step in range(len(order) + 1):
+        if step < len(order):
+            cross(order[step])
+        if step == 2:
+            for local in locals_:
+                local.wait()
+        if step >= 1:
+            share(order[step - 1])
+    slot = K
+    for v in range(1, lay.planes):
+        for q in range(lay.split):
+            m = lay.matrix(c, turn(y, -v, lay.planes), lay.common + q)
+            landed(ow_ref.at[m], ys.at[q, v], yr.at[q, v], here)
+            remote(ow_ref.at[m], ow_ref.at[m], cs.at[slot], cr.at[slot], here)
+            slot += 1
+    slot = K
+    for k in range(K):
+        m = lay.matrix(1 - c, y, k)
+        landed(ow_ref.at[m], cs.at[k], cr.at[k], here)
+    for v in range(1, lay.planes):
+        for q in range(lay.split):
+            m = lay.matrix(1 - c, turn(y, -v, lay.planes), lay.common + q)
+            landed(ow_ref.at[m], cs.at[slot], cr.at[slot], here)
+            slot += 1
+    local_small.wait()
+    for copy in pending:
+        copy.wait_send()
+
+
+def gather(lay, shard, small):
+    A, B, K = lay.outer, lay.inner, lay.handled
+    dma = pltpu.SemaphoreType.DMA
+    kept = max(lay.split, 1)
+    return pl.pallas_call(
+        functools.partial(gather_kernel, lay),
+        out_shape=(
+            jax.ShapeDtypeStruct((NMAT, lay.n) + shard.shape[1:], shard.dtype),
+            jax.ShapeDtypeStruct((lay.n,) + small.shape, small.dtype),
+        ),
+        in_specs=[ANY, ANY],
+        out_specs=(ANY, ANY),
+        scratch_shapes=[
+            dma((3,)), dma((K + 1, A)), dma((K + 1, A)), dma((K + 1, B, A)), dma((K + 1, B, A)),
+            dma((kept, lay.planes)), dma((kept, lay.planes)), dma((lay.half,)), dma((lay.half,)),
+            dma((1,)),
+        ],
+        compiler_params=pltpu.CompilerParams(collective_id=0, has_side_effects=True),
+    )(shard, small)
+
+
+def reduce_kernel(lay, g_ref, s_ref, og_ref, os_ref, *scratch):
+    i, a, b, y, c = lay.place()
+    A, B, Y = lay.outer, lay.inner, lay.planes
+    greet(lay, i, a, b, y, c)
+    big, little, out_sem = scratch[:20], scratch[20:40], scratch[40]
+    pending = []
+    here = lay.peer(i, y, 1 - c)
+
+    def remote(src, dst, ssem, rsem, dev):
+        copy = pltpu.make_async_remote_copy(
+            src_ref=src, dst_ref=dst, send_sem=ssem, recv_sem=rsem, device_id=dev, device_id_type=MESH
+        )
+        copy.start()
+        pending.append(copy.wait_send)
+
+    def landed(dst, sems, *at):
+        pltpu.make_async_remote_copy(
+            src_ref=dst, dst_ref=dst, send_sem=sems.at[at], recv_sem=sems.at[at], device_id=here, device_id_type=MESH
+        ).wait_recv()
+
+    class Set:
+        def __init__(self, refs, common, split, source, target):
+            (self.g, self.r, self.ys, self.yr, self.xs, self.xr, self.zs, self.zr, self.fin, self.all_) = refs[:10]
+            (self.lsem, self.rs, self.rr, self.yss, self.yrs, self.xss, self.xrs, self.zss, self.zrs, self.fsem) = refs[10:]
+            self.common, self.split = common, split
+            self.source, self.target = source, target
+            self.blocks = self.g.shape[1]
+
+        def slots(self):
+            found = [(v, q) for v in range(1, Y) for q in range(self.split)]
+            return found + [(None, k) for k in range(self.common)] + [(0, q) for q in range(self.split)]
+
+        def slot(self, v, q):
+            return self.slots().index((v, q))
+
+    def big_at(core, v, q):
+        if v is None:
+            return core * lay.half + q
+        return core * lay.half + lay.common + turn(y, v, Y) * lay.split + q
+
+    mats = Set(big, lay.common, lay.split, lambda core, v, q: g_ref.at[big_at(core, v, q)], lambda core, v, q: og_ref.at[big_at(core, v, q)])
+    rest = Set(little, 1, 0, lambda core, v, q: s_ref.at[core], lambda core, v, q: os_ref.at[core])
+
+    work = [(rest, None, 0)] + [(mats, None, k) for k in range(mats.common)] + [(mats, 0, q) for q in range(mats.split)]
+    starts = [(mats, v, q) for v in range(1, Y) for q in range(mats.split)] + work
+    for st, v, q in starts:
+        n = st.slot(v, q)
+        remote(st.source(1 - c, v, q), st.r.at[n], st.rs.at[n], st.rr.at[n], here)
+        pltpu.make_async_copy(st.source(c, v, q), st.g.at[n], st.lsem.at[n]).start()
+
+    def ready(st, v, q):
+        n = st.slot(v, q)
+        pltpu.make_async_copy(st.source(c, v, q), st.g.at[n], st.lsem.at[n]).wait()
+        landed(st.r.at[n], st.rr, n)
+
+    def base(st, n, v, q, j):
+        total = st.g[n, j].astype(jnp.float32) + st.r[n, j].astype(jnp.float32)
+        if v == 0:
+            for w in range(1, Y):
+                total = total + st.yr[w - 1, q, j].astype(jnp.float32)
+        return total
+
+    def pass_on(st, v, q):
+        n = st.slot(v, q)
+        ready(st, v, q)
+
+        @pl.loop(0, st.blocks)
+        def _(j):
+            st.ys[v - 1, q, j] = base(st, n, None, q, j).astype(jnp.bfloat16)
+
+        remote(st.ys.at[v - 1, q], st.yr.at[v - 1, q], st.yss.at[v - 1, q], st.yrs.at[v - 1, q], lay.peer(i, turn(y, v, Y), c))
+
+    def item(st, v, q):
+        return q if v is None else st.common + q
+
+    def cross(st, v, q):
+        n, k = st.slot(v, q), item(st, v, q)
+        ready(st, v, q)
+        if v == 0:
+            for w in range(1, Y):
+                landed(st.yr.at[w - 1, q], st.yrs, w - 1, q)
+        for u in range(1, B):
+            other = turn(b, u, B)
+
+            @pl.loop(0, A)
+            def _(e):
+                st.xs[k, u - 1, e] = base(st, n, v, q, e * B + other).astype(jnp.bfloat16)
+
+            remote(st.xs.at[k, u - 1], st.xr.at[k, u - 1], st.xss.at[k, u - 1], st.xrs.at[k, u - 1], lay.peer(a * B + other, y, c))
+
+    def along(st, v, q):
+        n, k = st.slot(v, q), item(st, v, q)
+        for u in range(1, B):
+            landed(st.xr.at[k, u - 1], st.xrs, k, u - 1)
+
+        def total(e):
+            value = base(st, n, v, q, e * B + b)
+            for u in range(1, B):
+                value = value + st.xr[k, u - 1, e].astype(jnp.float32)
+            return value
+
+        for t in range(1, A):
+            e = turn(a, t, A)
+            st.zs[k, t - 1] = total(e).astype(jnp.bfloat16)
+            remote(st.zs.at[k, t - 1], st.zr.at[k, t - 1], st.zss.at[k, t - 1], st.zrs.at[k, t - 1], lay.peer(e * B + b, y, c))
+        st.fin[k] = total(a)
+
+    def close(st, v, q):
+        k = item(st, v, q)
+        for t in range(1, A):
+            landed(st.zr.at[k, t - 1], st.zrs, k, t - 1)
+        value = st.fin[k]
+        for t in range(1, A):
+            value = value + st.zr[k, t - 1].astype(jnp.float32)
+        st.fin[k] = value
+        if v is None:
+            st.all_[y, k] = value
+            for w in range(1, Y):
+                remote(st.all_.at[y, k], st.all_.at[y, k], st.fsem.at[0, k, w], st.fsem.at[1, k, w], lay.peer(i, turn(y, w, Y), c))
+        else:
+            target = st.target(c, v, q)
+            for w in range(1, Y):
+                remote(st.fin.at[k], target, st.fsem.at[0, k, w], st.fsem.at[1, k, w], lay.peer(i, turn(y, w, Y), c))
+            finish(st, k, target)
+
+    def finish(st, k, target):
+        copy = pltpu.make_async_copy(st.fin.at[k], target, st.fsem.at[2, k, 0])
+        copy.start()
+        pending.append(copy.wait)
+        remote(st.fin.at[k], target, st.fsem.at[3, k, 0], st.fsem.at[4, k, 0], here)
+
+    def merge(st, v, q):
+        k = item(st, v, q)
+        if v is None:
+            for w in range(1, Y):
+                landed(st.all_.at[turn(y, -w, Y), k], st.fsem, 1, k, w)
+            value = st.all_[0, k]
+            for w in range(1, Y):
+                value = value + st.all_[w, k]
+            st.fin[k] = value
+            finish(st, k, st.target(c, v, q))
+        else:
+            for w in range(1, Y):
+                back = st.target(c, -w, q)
+                landed(back, st.fsem, 1, k, w)
+                remote(back, back, st.fsem.at[3, k, w], st.fsem.at[4, k, w], here)
+
+    others = [(mats, v, q) for v in range(1, Y) for q in range(mats.split)]
+    for job in others:
+        pass_on(*job)
+    for step in range(len(work) + 3):
+        if step < len(work):
+            cross(*work[step])
+        if 0 <= step - 1 < len(work):
+            along(*work[step - 1])
+        if 0 <= step - 2 < len(work):
+            close(*work[step - 2])
+        if 0 <= step - 3 < len(work):
+            merge(*work[step - 3])
+    for st, v, q in work:
+        k = item(st, v, q)
+        landed(st.target(1 - c, v, q), st.fsem, 4, k, 0)
+        if v is not None:
+            for w in range(1, Y):
+                landed(st.target(1 - c, -w, q), st.fsem, 4, k, w)
+    for wait in pending:
+        wait()
+
+
+def reduce_scratch(lay, rows, common, split):
+    A, B, Y, n = lay.outer, lay.inner, lay.planes, lay.n
+    slots, kept, passed, K = common + split * Y, max(split, 1), max(Y - 1, 1), common + split
+    half = jnp.bfloat16
+    dma = pltpu.SemaphoreType.DMA
+    width = rows if split else 16
+    depth = n if split else 1
+    crossed, along = max(B - 1, 1), max(A - 1, 1)
+    return [
+        pltpu.VMEM((slots, n, rows, D), half), pltpu.VMEM((slots, n, rows, D), half),
+        pltpu.VMEM((passed, kept, depth, width, D), half), pltpu.VMEM((passed, kept, depth, width, D), half),
+        pltpu.VMEM((K, crossed, A, rows, D), half), pltpu.VMEM((K, crossed, A, rows, D), half),
+        pltpu.VMEM((K, along, rows, D), half), pltpu.VMEM((K, along, rows, D), half),
+        pltpu.VMEM((K, rows, D), jnp.float32), pltpu.VMEM((Y, K if not split else common, rows, D), jnp.float32),
+        dma((slots,)), dma((slots,)), dma((slots,)), dma((passed, kept)), dma((passed, kept)),
+        dma((K, crossed)), dma((K, crossed)), dma((K, along)), dma((K, along)), dma((5, K, Y)),
+    ]
+
+
+def reduce(lay, grads, small):
+    rows, rest = grads.shape[2], small.shape[2]
+    return pl.pallas_call(
+        functools.partial(reduce_kernel, lay),
+        out_shape=(
+            jax.ShapeDtypeStruct((NMAT, rows, D), jnp.float32),
+            jax.ShapeDtypeStruct((2, rest, D), jnp.float32),
+        ),
+        in_specs=[ANY, ANY],
+        out_specs=(ANY, ANY),
+        scratch_shapes=reduce_scratch(lay, rows, lay.common, lay.split) + reduce_scratch(lay, rest, 1, 0) + [pltpu.SemaphoreType.DMA((1,))],
+        compiler_params=pltpu.CompilerParams(collective_id=1, has_side_effects=True, vmem_limit_bytes=58 * 2**20),
+    )(grads, small)
+
+
+def spread_kernel(dp, n, x_ref, o_ref, ssem, rsem):
+    i, d = lax.axis_index("fsdp"), lax.axis_index("dp")
+    me = d * n + i
+    total = dp * n
+    barrier = pltpu.get_barrier_semaphore()
+
+    def other(t):
+        j = lax.rem(me + t, total)
+        return {"fsdp": lax.rem(j, n), "dp": lax.div(j, n)}
+
+    @pl.loop(1, total)
+    def _(t):
+        pl.semaphore_signal(barrier, inc=1, device_id=other(t), device_id_type=MESH)
+
+    pl.semaphore_wait(barrier, total - 1)
+
+    @pl.loop(1, total)
+    def _(t):
+        pltpu.make_async_remote_copy(
+            src_ref=x_ref, dst_ref=o_ref.at[me], send_sem=ssem.at[t], recv_sem=rsem.at[t], device_id=other(t), device_id_type=MESH
+        ).start()
+
+    o_ref[me] = x_ref[...]
+
+    @pl.loop(1, total)
+    def _(t):
+        pltpu.make_async_remote_copy(
+            src_ref=x_ref, dst_ref=o_ref.at[lax.rem(me - t + total, total)], send_sem=ssem.at[t], recv_sem=rsem.at[t], device_id=other(t), device_id_type=MESH
+        ).wait()
+
+
+def spread(dp, n, tile, number):
+    vmem = pl.BlockSpec(memory_space=pltpu.VMEM)
+    return pl.pallas_call(
+        functools.partial(spread_kernel, dp, n),
+        out_shape=jax.ShapeDtypeStruct((dp * n,) + tile.shape, tile.dtype),
+        in_specs=[vmem],
+        out_specs=vmem,
+        scratch_shapes=[pltpu.SemaphoreType.DMA((dp * n,)), pltpu.SemaphoreType.DMA((dp * n,))],
+        compiler_params=pltpu.CompilerParams(collective_id=number, has_side_effects=True),
+    )(tile)
 
 def layer_norm(inputs, gain, shift):
     centred = inputs - jnp.mean(inputs, -1, keepdims=True)
@@ -376,7 +782,42 @@
     return (weight, first, second, average)
 
 
+def pack(head, vecs):
+    rows = head.shape[0] // 3
+    first = jnp.concatenate([head[:rows], head[rows : 2 * rows], head[2 * rows :]], 1)
+    tall = jnp.pad(vecs, ((0, D // 3 - vecs.shape[0]), (0, 0)))
+    second = tall.reshape(D // head.shape[0], rows, head.shape[0]).transpose(1, 0, 2).reshape(rows, D)
+    fill = -rows % 16
+    return jnp.pad(jnp.stack([first, second]), ((0, 0), (0, fill), (0, 0)))
+
+
+def unpack(blocks, rows):
+    n = blocks.shape[0]
+    kept = blocks[:, :, : rows // 3]
+    head = kept[:, 0].reshape(n, rows // 3, 3, D // 3).transpose(0, 2, 1, 3).reshape(D, D // 3)
+    vecs = kept[:, 1].reshape(n, rows // 3, n, rows).transpose(2, 1, 0, 3).reshape(D // 3, D)
+    return head, vecs[:NVEC]
+
+
+def pack_all(head, vecs, n):
+    rows = D // n
+    first = head.reshape(n, 3, rows // 3, D // 3).transpose(0, 2, 1, 3).reshape(n, rows // 3, D)
+    tall = jnp.pad(vecs, ((0, D // 3 - vecs.shape[0]), (0, 0)))
+    second = tall.reshape(n, rows // 3, n, rows).transpose(2, 1, 0, 3).reshape(n, rows // 3, D)
+    fill = -(rows // 3) % 16
+    return jnp.pad(jnp.stack([first, second]), ((0, 0), (0, 0), (0, fill), (0, 0)))
+
+
+def unpack_shard(blocks, n):
+    rows = D // n
+    first, second = blocks[0, : rows // 3], blocks[1, : rows // 3]
+    head = jnp.concatenate([first[:, : D // 3], first[:, D // 3 : 2 * D // 3], first[:, 2 * D // 3 :]], 0)
+    vecs = second.reshape(rows // 3, n, rows).transpose(1, 0, 2).reshape(D // 3, rows)
+    return head, vecs[:NVEC]
+
+
 def local(
+    lay,
     patches,
     patch_keep_mask,
     partner,
@@ -393,19 +834,21 @@
     vector_second,
     vector_average,
 ):
-    shards = (
+    n = lay.n
+    gathered_mats, gathered_small = gather(
+        lay,
         matrices.astype(jnp.bfloat16),
-        head_weight.astype(jnp.bfloat16),
-        vectors.astype(jnp.bfloat16),
-    )
-    mats16, head16, vecs16 = (
-        lax.all_gather(shards[0], "fsdp", axis=1, tiled=True),
-        lax.all_gather(shards[1], "fsdp", axis=0, tiled=True),
-        lax.all_gather(shards[2], "fsdp", axis=1, tiled=True),
-    )
+        pack(head_weight.astype(jnp.bfloat16), vectors.astype(jnp.bfloat16)),
+    )
+    mats16 = gathered_mats.reshape(NMAT, D, D)
+    head16, vecs16 = unpack(gathered_small, lay.rows)
     projected, saved = forward(mats16, head16, vecs16.astype(jnp.float32), patches, patch_keep_mask)
     unit_length_lines, unit_back = jax.vjp(normalize, projected)
-    gathered = lax.all_gather(unit_length_lines, ("dp", "fsdp"), axis=0, tiled=True)
+    clip_count, width = unit_length_lines.shape
+    lines = unit_length_lines.reshape(-1, 128)
+    tile = jnp.pad(lines, ((0, -lines.shape[0] % 8), (0, 0)))
+    everyone = spread(lay.dp, n, tile, 2)
+    gathered = everyone[:, : lines.shape[0]].reshape(-1, width)
 
     def contrast(gathered_rows):
         pairwise_affinity_scores_raw = (
@@ -428,31 +871,27 @@
     offset = lax.axis_index(("dp", "fsdp")) * clip_count
     back_unit = lax.dynamic_slice_in_dim(back_gathered, offset, clip_count, 0)
     (back_projected,) = unit_back(back_unit)
-    back_weights = (
-        lax.all_gather(shards[0], "fsdp", axis=1, tiled=True),
-        lax.all_gather(shards[1], "fsdp", axis=0, tiled=True),
-        lax.all_gather(shards[2], "fsdp", axis=1, tiled=True),
-    )
     grad_mats, grad_head, grad_vecs = backward(
-        back_weights[0],
-        back_weights[1],
-        back_weights[2].astype(jnp.float32),
+        mats16,
+        head16,
+        vecs16.astype(jnp.float32),
         patches,
         saved,
         back_projected,
     )
-    grad_mats, grad_head, grad_vecs = (
-        lax.psum_scatter(grad_mats, "fsdp", scatter_dimension=1, tiled=True),
-        lax.psum_scatter(grad_head, "fsdp", scatter_dimension=0, tiled=True),
-        lax.psum_scatter(grad_vecs, "fsdp", scatter_dimension=1, tiled=True),
-    )
-    grad_mats, grad_head, grad_vecs = lax.psum((grad_mats, grad_head, grad_vecs), "dp")
+    grad_mats, grad_small = reduce(
+        lay,
+        grad_mats.astype(jnp.bfloat16).reshape(NMAT, n, lay.rows, D),
+        pack_all(grad_head, grad_vecs, n).astype(jnp.bfloat16),
+    )
+    grad_head, grad_vecs = unpack_shard(grad_small, n)
     partial_squares = (
         jnp.sum(grad_mats * grad_mats)
         + jnp.sum(grad_head * grad_head)
         + jnp.sum(grad_vecs * grad_vecs)
     )
-    squared_norm = lax.psum(partial_squares, "fsdp")
+    squares = spread(lay.dp, n, jnp.broadcast_to(partial_squares, (8, 128)), 3)
+    squared_norm = jnp.sum(squares[:, 0, 0]) / lay.dp
     factor = CLIP_AT / jnp.maximum(jnp.sqrt(squared_norm), CLIP_AT)
     mats_out = adamw_step(
         matrices, matrix_first, matrix_second, matrix_average, grad_mats, factor, RATE
@@ -482,6 +921,7 @@
 
 
 def solution(mesh):
+    lay = Layout(mesh.shape["dp"], mesh.shape["fsdp"], 2)
     placed = (
         P(("dp", "fsdp"), None, None, None),
         P(("dp", "fsdp"), None, None),
@@ -500,7 +940,7 @@
         P(None, "fsdp"),
     )
     return jax.shard_map(
-        local,
+        functools.partial(local, lay),
         mesh=mesh,
         in_specs=placed,
         out_specs=(

time: 2350 us -> 1300 us (0.55)
  waiting for transfers between devices: 1150 us -> 0 us
  Pallas kernels: 0 us -> 287 us
  blocking collectives: 201 us -> 0 us
  local copies, waits for them, and re-layouts: 394 us -> 425 us
    unnamed x7 -> x0, waiting for transfers between devices: 670 us -> none
    all_gather x1 -> x0, waiting for transfers between devices: 309 us -> none  [local(): lax.all_gather(shards[0], 'fsdp', axis=1, tiled=True)]
    pallas_call x0 -> x4, Pallas kernels: none -> 287 us  [the longest x1 135 us: reduce(): pl.pallas_call(functools.partial(reduce_kernel, lay), out_shape=(jax.Shap...]
    all_gather x3 -> x0, blocking collectives: 179 us -> none  [the longest x1 66.8 us: local(): lax.all_gather(unit_length_lines, ('dp', 'fsdp'), axis=0, tiled=True)]
    psum x1 -> x0, waiting for transfers between devices: 109 us -> none  [local(): lax.psum((grad_mats, grad_head, grad_vecs), 'dp')]
    unnamed x346 -> x263, local copies, waits for them, and re-layouts: 113 us -> 38.7 us
    reduce_scatter x1 -> x0, waiting for transfers between devices: 65.2 us -> none  [local(): lax.psum_scatter(grad_head, 'fsdp', scatter_dimension=0, tiled=True)]
    dot_general x1, matrix products: 55.9 us -> 10.3 us  [backward(): jnp.einsum('kcna,cnb->kab', activated, rounded, preferred_element_type=jn...]
  transfers between devices with their start and end apart: 5 -> 0, of which waited for: 5 -> 0; matrix products, arithmetic and copies ran while one was open for 3% -> 0% of each run, Pallas kernels for 0% -> 0%
where the time goes in v1:
time: 1300 us; the launch traced here: 1290 us
  local copies, waits for them, and re-layouts  425 us (33%)
  matrix products  394 us (30%)
  Pallas kernels  287 us (22%)
  other arithmetic  171 us (13%)
    pallas_call x1, Pallas kernels, reduce(): pl.pallas_call(functools.partial(reduce_kernel, lay), out_shape=(jax.Shap...  135 us
    pallas_call x1, Pallas kernels, gather(): pl.pallas_call(functools.partial(gather_kernel, lay), out_shape=(jax.Shap...  126 us
    dot_general x1, matrix products, forward(): jnp.einsum('kcna,kab->cnb', activated, mats16[14:18], preferred_element_t...  56.5 us
    dot_general x1, matrix products, backward(): jnp.einsum('cnb,kab->kcna', rounded, mats16[14:18], preferred_element_typ...  55.7 us
    another operation x10, local copies, waits for them, and re-layouts  53.8 us
    concatenate x6, local copies, waits for them, and re-layouts, per_frame(): jnp.concatenate([leading, tensor[:, 1:].reshape(clip_count, F, S, width)]...  50.7 us
    dot_general x1, other arithmetic, backward(): jnp.einsum('kcna,cnb->kab', activated, rounded, preferred_element_type=jn...  43.7 us
    unnamed x263, local copies, waits for them, and re-layouts  38.7 us

profile of v1, /device:TPU:0, one launch (start us, length us, event | category | flops | bytes accessed | tf_op | source)
XLA Modules:
  0.0 1287.4 jit_solution(2550208043643154518)
XLA Ops:
  11.0 125.9 %shard_map.254 = (bf16[18,8,96,768]{3,2,1,0:T(8,128)(2,1)}, bf16[8,2,32,768]{3,2,1,0:T(8,128)(2,1)}) custom-call(bf16[18,96,768]{2,1,0:T(8,128)(2,1)} %convert_element_type.229.w_ref, bf16[2,32,768]{2,1,0:T(8,128)(2,1)} %pad_maximum_fusion.28.s_ref), custom_call_target="tpu_custom_call" | custom-call | tf_op jit(solution)/shard_map/pallas_call | solution.py:170
  215.8 10.2 fusion.52
  375.3 12.4 fusion.237
  387.7 11.3 fusion.24
  399.6 13.4 %fusion.31 = f32[8,12,64,197]{3,2,1,0:T(8,128)} fusion(f32[8,12,197,197]{2,3,1,0:T(8,128)} %get-tuple-element.150, f32[8,12,197]{2,1,0:T(8,128)S(1)} %fusion.24, f32[8,12,197]{2,1,0:T(8,128)S(1)} %get-tuple-element.149, bf16[8,196,12,64]{1,3,2,0:T(8,128)(2,1)} %copy.201, bf16[8,1,12,64]{1,3,2,0:T(8,128)(2,1)} %broadcast_in_dim.112), kind=kOutput, calls=%fused_computation.48 | convolution fusion | flops 492903456 | bytes 22316160 | tf_op jit(solution)/shard_map/bhlm,bmhd->blhd/dot_general | solution.py:486
  442.2 11.5 fusion.207
  453.7 56.5 %fusion.239 = (f32[1569]{0:T(1024)S(1)}, f32[1569,768]{1,0:T(8,128)S(1)}) fusion(f32[768]{0:T(1024)S(1)} %copy-done.94, f32[1569,768]{1,0:T(8,128)S(1)} %get-tuple-element.152, bf16[4,768,768]{2,1,0:T(8,128)(2,1)S(1)} %bitcast.556, f32[4,768]{1,0:T(4,128)S(1)} %copy-done.67, f32[4,768,1569]{1,2,0:T(8,128)} %fusion.207), kind=kOutput, calls=%fused_computation.382 | convolution fusion | flops 7725202432 | bytes 33660036 | tf_op jit(solution)/shard_map/kcna,kab->cnb/dot_general | solution.py:588
  514.7 13.5 %shard_map.255 = f32[32,8,128]{2,1,0:T(8,128)} custom-call(f32[8,128]{1,0:T(8,128)} %pad.15.x_ref), custom_call_target="tpu_custom_call" | custom-call | tf_op jit(solution)/shard_map/pallas_call | solution.py:423
  544.8 55.7 %fusion.242 = (bf16[4,768]{1,0:T(4,128)(2,1)}, bf16[4,1,1569,768]{3,2,0,1:T(8,128)(2,1)}) fusion(bf16[4,768,768]{2,1,0:T(8,128)(2,1)} %bitcast.553, bf16[1569,768]{1,0:T(8,128)(2,1)S(1)} %get-tuple-element.81, f32[4,768]{1,0:T(4,128)S(1)} %copy-done.67, f32[4,768,1569]{1,2,0:T(8,128)} %fusion.207), kind=kOutput, calls=%fused_computation.385 | convolution fusion | flops 7760145408 | bytes 36066816 | tf_op jit(solution)/shard_map/cnb,kab->kcna/dot_general | solution.py:647
  600.6 43.7 %fusion.116 = bf16[4,768,1569]{1,2,0:T(8,128)(2,1)} fusion(f32[4,768]{1,0:T(4,128)S(1)} %copy-done.67, f32[4,768,1569]{1,2,0:T(8,128)S(1)} %bitcast.533), kind=kLoop, calls=%fused_computation.179 | loop fusion | flops 318117888 | bytes 28932096 | tf_op jit(solution)/shard_map/kcna,cnb->kab/dot_general | solution.py:650
  644.4 13.2 %fusion.46 = (bf16[768]{0:T(1024)(128)(2,1)S(1)}, f32[1569]{0:T(1024)S(1)}, bf16[768]{0:T(1024)(128)(2,1)S(1)}, f32[1569,768,1]{1,0,2:T(8,128)S(1)}) fusion(f32[1569,768]{1,0:T(8,128)S(1)} %copy-done.9, f32[1569]{0:T(1024)S(1)} %copy-done.74, f32[1569]{0:T(1024)S(1)} %copy-done.60, f32[768]{0:T(1024)S(1)} %copy-done.79, ...), kind=kOutput, calls=%fused_computation.98 | convolution fusion | flops 7413107712 | bytes 24023436 | tf_op jit(solution)/shard_map/k...b,kab->...a/dot_general | solution.py:461
  657.6 14.6 %fusion.76 = bf16[4,768,768]{1,2,0:T(8,128)(2,1)} fusion(bf16[4,1,1569,768]{3,2,0,1:T(8,128)(2,1)} %get-tuple-element.165, f32[1569,768]{1,0:T(8,128)S(1)} %copy-done.9, f32[768]{0:T(1024)S(1)} %copy-done.93, f32[768]{0:T(1024)S(1)} %copy-done.79, f32[1569]{0:T(1024)S(1)} %copy-done.74, f32[1569]{0:T(1024)S(1)} %copy-done.60), kind=kOutput, calls=%fused_computation.149 | convolution fusion | flops 7411855360 | bytes 19197192 | tf_op jit(solution)/shard_map/na,knb->kab/dot_general | solution.py:464
  681.4 13.3 %copy.242 = bf16[4,768,1569]{2,1,0:T(8,128)(2,1)} copy(bf16[4,768,1569]{1,2,0:T(8,128)(2,1)} %fusion.116) | data formatting | bytes 19279872 | tf_op jit(solution)/shard_map/kcna,cnb->kab/dot_general | solution.py:650
  720.3 10.0 fusion.28
  746.0 16.6 %multiply_reduce_fusion = (f32[8,12,197]{2,1,0:T(8,128)S(1)}, f32[8,12,197,197]{2,3,1,0:T(8,128)}) fusion(f32[8,12,197,197]{2,3,1,0:T(8,128)} %get-tuple-element.150, f32[8,12,197]{2,1,0:T(8,128)S(1)} %copy-done.25, bf16[8,196,12,64]{1,3,2,0:T(8,128)(2,1)} %copy.201, bf16[8,1,12,64]{1,3,2,0:T(8,128)(2,1)} %broadcast_in_dim.112, ...), kind=kOutput, calls=%fused_computation.3 | convolution fusion | flops 497726016 | bytes 34798080 | tf_op jit(solution)/shard_map/blhd,bmhd->bhlm/dot_general | solution.py:493
  762.6 18.1 %multiply_convert_fusion = bf16[8,12,197,197]{2,3,1,0:T(8,128)(2,1)} fusion(f32[8,12,197,197]{2,3,1,0:T(8,128)} %get-tuple-element.159, f32[8,12,197,197]{2,3,1,0:T(8,128)} %get-tuple-element.150, f32[8,12,197]{2,1,0:T(8,128)S(1)} %get-tuple-element.158, f32[8,12,197]{2,1,0:T(8,128)S(1)} %copy-done.25), kind=kLoop, calls=%fused_computation.2 | loop fusion | flops 14902656 | bytes 37407936 | tf_op jit(solution)/shard_map/convert_element_type | solution.py:495
  780.7 11.1 broadcast_multiply_fusion
  791.8 10.2 broadcast_multiply_fusion.1
  1038.3 11.4 bitcast_reduce_fusion
  1049.8 12.3 bitcast_convert_fusion
  1095.1 10.3 convert_dynamic-update-slice_fusion.g_ref
  1105.4 134.6 %shard_map.256 = (f32[18,96,768]{2,1,0:T(8,128)}, f32[2,32,768]{2,1,0:T(8,128)}) custom-call(bf16[18,8,96,768]{3,2,1,0:T(8,128)(2,1)} %convert_dynamic-update-slice_fusion.g_ref, bf16[2,8,32,768]{3,2,1,0:T(8,128)(2,1)} %pad_maximum_fusion.27.s_ref), custom_call_target="tpu_custom_call" | custom-call | tf_op jit(solution)/shard_map/pallas_call | solution.py:377
  1248.7 12.9 %shard_map.257 = f32[32,8,128]{2,1,0:T(8,128)} custom-call(f32[8,128]{1,0:T(8,128)} %broadcast_in_dim.237.x_ref), custom_call_target="tpu_custom_call" | custom-call | tf_op jit(solution)/shard_map/pallas_call | solution.py:423
  1266.5 18.2 %multiply_add_fusion = (f32[18,96,768]{2,1,0:T(8,128)}, f32[18,96,768]{2,1,0:T(8,128)}, f32[18,96,768]{2,1,0:T(8,128)}, f32[18,96,768]{2,1,0:T(8,128)}) fusion(f32[18,96,768]{2,1,0:T(8,128)} %param.21, f32[18,96,768]{2,1,0:T(8,128)} %param.18, f32[18,96,768]{2,1,0:T(8,128)} %get-tuple-element.20, f32[]{:T(128)S(6)} %div.228, f32[18,96,768]{2,1,0:T(8,128)} %param.19, ...), kind=kLoop, calls=%fused_computation.73 | loop fusion | flops 25214976 | bytes 47775748 | tf_op jit(solution)/shard_map/add | solution.py:781
  (499 shorter events, 616.0 us)
Async XLA Ops:
  3.1 229.8 %copy-start.75 = (pred[196,8]{0,1:T(8,128)(4,1)}, pred[196,8]{0,1:T(8,128)(4,1)S(1)}, u32[]{:S(2)}) copy-start(pred[196,8]{0,1:T(8,128)(4,1)S(1)} %fusion.279) | copy-start | bytes 4708
  143.9 156.0 %copy-start.71 = (f32[768]{0:T(1024)}, f32[768]{0:T(1024)S(1)}, u32[]{:S(2)}) copy-start(f32[768]{0:T(1024)S(1)} %get-tuple-element.119) | copy-start | bytes 9220
  143.9 156.0 %copy-start.90 = (f32[768]{0:T(1024)}, f32[768]{0:T(1024)S(1)}, u32[]{:S(2)}) copy-start(f32[768]{0:T(1024)S(1)} %get-tuple-element.120) | copy-start | bytes 9220
  143.9 289.9 %copy-start.51 = (f32[1,768]{1,0:T(1,128)}, f32[1,768]{1,0:T(1,128)S(1)}, u32[]{:S(2)}) copy-start(f32[1,768]{1,0:T(1,128)S(1)} %get-tuple-element.127) | copy-start | bytes 9220
  453.7 57.3 %copy-start.68 = (f32[768]{0:T(1024)S(1)}, f32[768]{0:T(1024)}, u32[]{:S(2)}) copy-start(f32[768]{0:T(1024)} %get-tuple-element.125) | copy-start | bytes 9220
  453.7 57.3 %copy-start.77 = (f32[768]{0:T(1024)S(1)}, f32[768]{0:T(1024)}, u32[]{:S(2)}) copy-start(f32[768]{0:T(1024)} %get-tuple-element.113) | copy-start | bytes 9220
  510.3 30.4 %copy-start.28 = (f32[1569]{0:T(1024)}, f32[1569]{0:T(1024)S(1)}, u32[]{:S(2)}) copy-start(f32[1569]{0:T(1024)S(1)} %broadcast_multiply_fusion.2) | copy-start | bytes 18832
  511.0 29.6 %copy-start.35 = (f32[1569]{0:T(1024)}, f32[1569]{0:T(1024)S(1)}, u32[]{:S(2)}) copy-start(f32[1569]{0:T(1024)S(1)} %fusion.144) | copy-start | bytes 18832
  539.1 61.4 %copy-start.53 = (f32[1569]{0:T(1024)}, f32[1569]{0:T(1024)S(1)}, u32[]{:S(2)}) copy-start(f32[1569]{0:T(1024)S(1)} %negate_multiply_fusion.4) | copy-start | bytes 18832
  540.7 59.8 %slice-start.12 = ((s8[19365888]{0:T(1024)(128)(4,1)}), s8[4194304]{0:T(1024)(128)(4,1)S(1)}, s32[]{:S(2)}) async-start(s8[19365888]{0:T(1024)(128)(4,1)} %bitcast.532), calls=%async_computation.12 | async-start | bytes 8388608
  544.2 56.3 %copy-start.22 = (bf16[1569,768]{1,0:T(8,128)(2,1)}, bf16[1569,768]{1,0:T(8,128)(2,1)S(1)}, u32[]{:S(2)}) copy-start(bf16[1569,768]{1,0:T(8,128)(2,1)S(1)} %get-tuple-element.81) | copy-start | bytes 7229956
  544.8 55.7 %slice-start.13 = ((s8[19365888]{0:T(1024)(128)(4,1)}), s8[4194304]{0:T(1024)(128)(4,1)S(1)}, s32[]{:S(2)}) async-start(s8[19365888]{0:T(1024)(128)(4,1)} %bitcast.532), calls=%async_computation.13 | async-start | bytes 8388608
  544.8 55.7 %slice-start.14 = ((s8[19365888]{0:T(1024)(128)(4,1)}), s8[4194304]{0:T(1024)(128)(4,1)S(1)}, s32[]{:S(2)}) async-start(s8[19365888]{0:T(1024)(128)(4,1)} %bitcast.532), calls=%async_computation.14 | async-start | bytes 8388608
  544.8 55.7 %slice-start.15 = ((s8[19365888]{0:T(1024)(128)(4,1)}), s8[4194304]{0:T(1024)(128)(4,1)S(1)}, s32[]{:S(2)}) async-start(s8[19365888]{0:T(1024)(128)(4,1)} %bitcast.532), calls=%async_computation.15 | async-start | bytes 8388608
  544.8 55.7 %slice-start.16 = ((s8[19365888]{0:T(1024)(128)(4,1)}), s8[2588672]{0:T(1024)(128)(4,1)S(1)}, s32[]{:S(2)}) async-start(s8[19365888]{0:T(1024)(128)(4,1)} %bitcast.532), calls=%async_computation.16 | async-start | bytes 5177344
  600.5 43.8 %copy-start.9 = (f32[1569,768]{1,0:T(8,128)S(1)}, f32[1569,768]{1,0:T(8,128)}, u32[]{:S(2)}) copy-start(f32[1569,768]{1,0:T(8,128)} %copy-done.8) | copy-start | bytes 14459908
  600.5 43.8 %copy-start.13 = (bf16[4,8,96,768]{3,2,1,0:T(8,128)(2,1)S(1)}, bf16[4,8,96,768]{3,2,1,0:T(8,128)(2,1)}, u32[]{:S(2)}) copy-start(bf16[4,8,96,768]{3,2,1,0:T(8,128)(2,1)} %get-tuple-element.92) | copy-start | bytes 14155780
  600.6 43.8 %copy-start.60 = (f32[1569]{0:T(1024)S(1)}, f32[1569]{0:T(1024)}, u32[]{:S(2)}) copy-start(f32[1569]{0:T(1024)} %copy-done.59) | copy-start | bytes 18832
  600.6 43.8 %copy-start.74 = (f32[1569]{0:T(1024)S(1)}, f32[1569]{0:T(1024)}, u32[]{:S(2)}) copy-start(f32[1569]{0:T(1024)} %copy-done.73) | copy-start | bytes 18832
  600.6 43.8 %copy-start.79 = (f32[768]{0:T(1024)S(1)}, f32[768]{0:T(1024)}, u32[]{:S(2)}) copy-start(f32[768]{0:T(1024)} %get-tuple-element.122) | copy-start | bytes 9220
  644.4 29.8 %slice-start = ((s8[4841472]{0:T(1024)(128)(4,1)}), s8[647168]{0:T(1024)(128)(4,1)S(1)}, s32[]{:S(2)}) async-start(s8[4841472]{0:T(1024)(128)(4,1)} %bitcast.514), calls=%async_computation | async-start | bytes 1294336
  1038.3 26.2 %slice-start.8 = ((s8[4915200]{0:T(1024)(128)(4,1)}), s8[4194304]{0:T(1024)(128)(4,1)S(1)}, s32[]{:S(2)}) async-start(s8[4915200]{0:T(1024)(128)(4,1)} %bitcast.528), calls=%async_computation.8 | async-start | bytes 8388608
  1240.0 24.8 %copy-start.34 = (f32[96,256]{1,0:T(8,128)S(1)}, f32[96,256]{1,0:T(8,128)}, u32[]{:S(2)}) copy-start(f32[96,256]{1,0:T(8,128)} %param.22) | copy-start | bytes 294916
  1240.0 24.8 %copy-start.49 = (f32[96,256]{1,0:T(8,128)S(1)}, f32[96,256]{1,0:T(8,128)}, u32[]{:S(2)}) copy-start(f32[96,256]{1,0:T(8,128)} %param.25) | copy-start | bytes 294916
  (102 other events, 895.4 us)

commit v2 on v1

--- a/solution.py
+++ b/solution.py
@@ -11,11 +11,11 @@
 HD = 64
 F = 8
 S = 196
+SP = 208
+NMAT = 18
 NVEC = 227
 STEP = 10
 
-
-NORM_EPS = 1e-06
 SCORE_SHARPNESS = 0.07
 CLIP_AT = 0.05
 RATE = 0.01
@@ -26,8 +26,6 @@
 DECAY = 0.05
 AVERAGE_KEEP = 0.9
 
-
-NMAT = 18
 MESH = pl.DeviceIdType.MESH
 ANY = pl.BlockSpec(memory_space=pl.ANY)
 
@@ -429,14 +427,413 @@
         compiler_params=pltpu.CompilerParams(collective_id=number, has_side_effects=True),
     )(tile)
 
-def layer_norm(inputs, gain, shift):
-    centred = inputs - jnp.mean(inputs, -1, keepdims=True)
-    spread = jnp.mean(centred * centred, -1, keepdims=True)
-    return centred * lax.rsqrt(spread + NORM_EPS) * gain + shift
-
-
-def gelu_exact(values):
-    return jax.nn.gelu(values, approximate=False)
+
+FB = 2
+GROUP = 16
+HALF = jnp.bfloat16
+FULL = jnp.float32
+NORM_EPS = 1e-06
+MASKED = -1000000000.0
+NEVER = -3e38
+
+
+def dot(a, b):
+    return lax.dot_general(a, b, (((1,), (0,)), ((), ())), preferred_element_type=FULL)
+
+
+def dot_back(a, b):
+    return lax.dot_general(a, b, (((1,), (1,)), ((), ())), preferred_element_type=FULL)
+
+
+def dot_rows(a, b):
+    return lax.dot_general(a, b, (((0,), (0,)), ((), ())), preferred_element_type=FULL)
+
+
+def mean(x):
+    return jnp.sum(x, -1, keepdims=True) * (1.0 / D)
+
+
+def norm(x, gain, shift):
+    centred = x - mean(x)
+    scale = lax.rsqrt(mean(centred * centred) + NORM_EPS)
+    return centred * scale * gain + shift
+
+
+def norm_back(x, gain, back):
+    centred = x - mean(x)
+    scale = lax.rsqrt(mean(centred * centred) + NORM_EPS)
+    unit = centred * scale
+    inner = back * gain
+    return scale * (inner - mean(inner) - unit * mean(inner * unit)), back * unit
+
+
+def normal_cdf(x):
+    size = jnp.abs(x) * 0.7071067811865476
+    t = pl.reciprocal(1.0 + 0.3275911 * size)
+    bell = jnp.exp(-0.5 * x * x)
+    poly = ((((1.061405429 * t - 1.453152027) * t + 1.421413741) * t - 0.284496736) * t + 0.254829592) * t
+    tail = 0.5 * poly * bell
+    return jnp.where(x < 0, tail, 1.0 - tail), bell
+
+
+def gelu(x):
+    return x * normal_cdf(x)[0]
+
+
+def gelu_slope(x):
+    below, bell = normal_cdf(x)
+    return below + x * bell * 0.3989422804014327
+
+
+def column_sum(x):
+    return jnp.sum(x.astype(FULL), 0, keepdims=True)
+
+
+def flat(ref):
+    x = ref[...]
+    return x.reshape(-1, x.shape[-1])
+
+
+def row_of(rows):
+    return lax.rem(lax.broadcasted_iota(jnp.int32, (rows, 1), 0), SP)
+
+
+def first_step():
+    return pl.program_id(0) == 0
+
+
+def add_rows(ref, values):
+    @pl.when(first_step())
+    def _():
+        ref[...] = jnp.zeros_like(ref)
+
+    for k, value in enumerate(values):
+        if value is not None:
+            ref[k : k + 1, :] += value
+
+
+def pair_lanes(x, low):
+    zero = jnp.zeros_like(x)
+    return jnp.concatenate([jnp.where(low, x, zero), jnp.where(low, zero, x)], 0)
+
+
+def attend(q, k, v, fill):
+    rows = q.shape[0]
+    low = lax.broadcasted_iota(jnp.int32, (rows, 128), 1) < HD
+    stacked = pair_lanes(q * jnp.asarray(HD ** (-0.5), HALF), low)
+    scores = dot_back(stacked, k)
+    if fill.shape[0] != 1:
+        fill = jnp.concatenate([fill, fill], 0)
+    scores = jnp.where(fill == 0.0, scores, fill)
+    expanded = jnp.exp(scores - jnp.max(scores, -1, keepdims=True))
+    share = pl.reciprocal(jnp.sum(expanded, -1, keepdims=True))
+    mixed = dot((expanded * share).astype(HALF), v)
+    return jnp.where(low, mixed[:rows], mixed[rows:])
+
+
+def attend_back(q, k, v, back, fill):
+    rows = q.shape[0]
+    low = lax.broadcasted_iota(jnp.int32, (rows, 128), 1) < HD
+    stacked = pair_lanes(q * jnp.asarray(HD ** (-0.5), HALF), low)
+    backs = pair_lanes(back, low)
+    scores = dot_back(k, stacked)
+    scores = jnp.where(fill == 0.0, scores, fill)
+    expanded = jnp.exp(scores - jnp.max(scores, 0, keepdims=True))
+    chances = expanded * pl.reciprocal(jnp.sum(expanded, 0, keepdims=True))
+    back_chances = dot_back(v, backs)
+    inner = jnp.sum(back_chances * chances, 0, keepdims=True)
+    back_scores = (chances * (back_chances - inner)).astype(HALF)
+    back_keys = dot(back_scores, stacked)
+    back_values = dot(chances.astype(HALF), backs)
+    queries = dot_rows(back_scores, k) * HD ** (-0.5)
+    return jnp.where(low, queries[:rows], queries[rows:]), back_keys, back_values
+
+
+def embed_kernel(p_ref, w0, w1, w2, w3, v_ref, pos_ref, time_ref, pad_ref, x_ref, a_ref, q_ref, k_ref, b_ref):
+    pad_ref[:, SP - GROUP :, :] = jnp.zeros((FB, GROUP, D), HALF)
+    for f in range(FB):
+        pad_ref[f, :S, :] = p_ref[0, f]
+    pos = pos_ref[...]
+    here = jnp.concatenate([pos + time_ref[f] for f in range(FB)], 0)
+    x = dot(flat(pad_ref), w0[0]) + v_ref[9:10] + here
+    x_ref[...] = x.reshape(FB, SP, D)
+    a = norm(x, v_ref[22:23], v_ref[23:24]).astype(HALF)
+    a_ref[...] = a.reshape(FB, SP, D)
+    q_ref[...] = (dot(a, w1[0]) + v_ref[10:11]).astype(HALF).reshape(FB, SP, D)
+    k_ref[...] = dot(a, w2[0]).astype(HALF).reshape(FB, SP, D)
+    b_ref[...] = (dot(a, w3[0]) + v_ref[11:12]).astype(HALF).reshape(FB, SP, D)
+
+
+def time_kernel(q_ref, k_ref, v_ref, fill_ref, o_ref):
+    rows = F * GROUP
+    for p in range(H // 2):
+        lanes = slice(128 * p, 128 * p + 128)
+        q, k, v = (ref[:, :, lanes].reshape(rows, 128) for ref in (q_ref, k_ref, v_ref))
+        o_ref[:, :, lanes] = attend(q, k, v, fill_ref[0]).astype(HALF).reshape(F, GROUP, 128)
+
+
+def space_kernel(o_ref, x_ref, w0, w1, w2, w3, w4, v_ref, fill_ref, y_ref, xs_ref, a_ref, q_ref, k_ref, b_ref, os_ref, cls_ref):
+    rows = FB * SP
+    y = (dot(flat(o_ref), w0[0]) + v_ref[12:13]).astype(HALF)
+    y_ref[...] = y.reshape(FB, SP, D)
+    x = flat(x_ref) + dot(y, w1[0]) + v_ref[13:14]
+    x = jnp.where(row_of(rows) == S, v_ref[0:1] + v_ref[30:31], x)
+    xs_ref[...] = x.reshape(FB, SP, D)
+    a = norm(x, v_ref[24:25], v_ref[25:26]).astype(HALF)
+    a_ref[...] = a.reshape(FB, SP, D)
+    q_ref[...] = (dot(a, w2[0]) + v_ref[14:15]).astype(HALF).reshape(FB, SP, D)
+    k_ref[...] = dot(a, w3[0]).astype(HALF).reshape(FB, SP, D)
+    b_ref[...] = (dot(a, w4[0]) + v_ref[15:16]).astype(HALF).reshape(FB, SP, D)
+    for f in range(FB):
+        for p in range(H // 2):
+            lanes = slice(128 * p, 128 * p + 128)
+            mixed = attend(q_ref[f, :, lanes], k_ref[f, :, lanes], b_ref[f, :, lanes], fill_ref[f])
+            os_ref[f, :, lanes] = mixed.astype(HALF)
+            cls_ref[f, :, lanes] = mixed[S : S + 8]
+
+
+def mlp_kernel(o_ref, cls_ref, xs_ref, wp_ref, u0, u1, u2, u3, e0, e1, e2, e3, v_ref, share_ref, of_ref, x2_ref, a_ref, g_ref, e_ref, x3_ref, pool_ref):
+    rows = FB * SP
+    o = jnp.where(row_of(rows) == S, cls_ref[...], flat(o_ref).astype(FULL)).astype(HALF)
+    of_ref[...] = o.reshape(FB, SP, D)
+    x2 = flat(xs_ref) + dot(o, wp_ref[0]) + v_ref[16:17]
+    x2_ref[...] = x2.reshape(FB, SP, D)
+    a = norm(x2, v_ref[26:27], v_ref[27:28]).astype(HALF)
+    a_ref[...] = a.reshape(FB, SP, D)
+    x3 = x2 + v_ref[21:22]
+    for k in range(4):
+        g = dot(a, (u0, u1, u2, u3)[k][0]) + v_ref[17 + k : 18 + k]
+        g_ref[k] = g.reshape(FB, SP, D)
+        e = gelu(g).astype(HALF)
+        e_ref[k] = e.reshape(FB, SP, D)
+        x3 = x3 + dot(e, (e0, e1, e2, e3)[k][0])
+    x3_ref[...] = x3.reshape(FB, SP, D)
+    final = norm(x3, v_ref[28:29], v_ref[29:30]) * share_ref[...]
+    add_rows(pool_ref, [column_sum(final)])
+
+
+def mlp_back_kernel(x3_ref, x2_ref, g_ref, d_ref, wp_ref, u0, u1, u2, u3, e0, e1, e2, e3, v_ref, share_ref, q_ref, k_ref, b_ref, fill_ref,
+                    r3_ref, dg_ref, d2_ref, r2_ref, dq_ref, dk_ref, dv_ref, cq_ref, ck_ref, cv_ref, sum_ref, do_ref):
+    top = d_ref[0:1] * share_ref[...]
+    d3, unit = norm_back(flat(x3_ref), v_ref[28:29], top)
+    sums = [column_sum(unit), column_sum(top)]
+    r3 = d3.astype(HALF)
+    r3_ref[...] = r3.reshape(FB, SP, D)
+    sums.append(column_sum(r3))
+    back = None
+    for k in range(4):
+        dg = (dot_back(r3, (e0, e1, e2, e3)[k][0]) * gelu_slope(flat(g_ref.at[k]))).astype(HALF)
+        dg_ref[k] = dg.reshape(FB, SP, D)
+        sums.append(column_sum(dg))
+        part = dot_back(dg, (u0, u1, u2, u3)[k][0])
+        back = part if back is None else back + part
+    d2, unit = norm_back(flat(x2_ref), v_ref[26:27], back)
+    sums += [column_sum(unit), column_sum(back)]
+    d2 = d2 + d3
+    d2_ref[...] = d2.reshape(FB, SP, D)
+    r2 = d2.astype(HALF)
+    r2_ref[...] = r2.reshape(FB, SP, D)
+    sums.append(column_sum(r2))
+    add_rows(sum_ref, sums)
+    do_ref[...] = dot_back(r2, wp_ref[0]).astype(HALF).reshape(FB, SP, D)
+    for f in range(FB):
+        for p in range(H // 2):
+            lanes = slice(128 * p, 128 * p + 128)
+            outs = attend_back(q_ref[f, :, lanes], k_ref[f, :, lanes], b_ref[f, :, lanes], do_ref[f, :, lanes], fill_ref[f][:, 0:1])
+            for value, ref, cls in zip(outs, (dq_ref, dk_ref, dv_ref), (cq_ref, ck_ref, cv_ref)):
+                ref[f, :, lanes] = value.astype(HALF)
+                cls[f, :, lanes] = value[S : S + 8]
+
+
+def space_back_kernel(dq_ref, dk_ref, dv_ref, cls_ref, xs_ref, d2_ref, w0, w1, w2, w3, w4, v_ref, fq_ref, fk_ref, fv_ref, d1_ref, r1_ref, dy_ref, do_ref, sum_ref):
+    rows = FB * SP
+    is_class = row_of(rows) == S
+    grads = []
+    for k, (ref, out) in enumerate(zip((dq_ref, dk_ref, dv_ref), (fq_ref, fk_ref, fv_ref))):
+        grad = jnp.where(is_class, cls_ref[k : k + 1], flat(ref).astype(FULL)).astype(HALF)
+        out[...] = grad.reshape(FB, SP, D)
+        grads.append(grad)
+    back = dot_back(grads[0], w2[0]) + dot_back(grads[1], w3[0]) + dot_back(grads[2], w4[0])
+    d, unit = norm_back(flat(xs_ref), v_ref[24:25], back)
+    sums = [column_sum(grads[0]), column_sum(grads[2]), column_sum(unit), column_sum(back)]
+    d = d + flat(d2_ref)
+    kept = jnp.where(is_class, d, 0.0)
+    sums.append(column_sum(kept))
+    d = d - kept
+    d1_ref[...] = d.reshape(FB, SP, D)
+    r1 = d.astype(HALF)
+    r1_ref[...] = r1.reshape(FB, SP, D)
+    sums.append(column_sum(r1))
+    dy = dot_back(r1, w1[0]).astype(HALF)
+    dy_ref[...] = dy.reshape(FB, SP, D)
+    sums.append(column_sum(dy))
+    do_ref[...] = dot_back(dy, w0[0]).astype(HALF).reshape(FB, SP, D)
+    add_rows(sum_ref, sums)
+
+
+def time_back_kernel(q_ref, k_ref, v_ref, d_ref, fill_ref, dq_ref, dk_ref, dv_ref):
+    rows = F * GROUP
+    fill = jnp.concatenate([fill_ref[0], fill_ref[0]], 1)
+    for p in range(H // 2):
+        lanes = slice(128 * p, 128 * p + 128)
+        q, k, v, d = (ref[:, :, lanes].reshape(rows, 128) for ref in (q_ref, k_ref, v_ref, d_ref))
+        for value, ref in zip(attend_back(q, k, v, d, fill), (dq_ref, dk_ref, dv_ref)):
+            ref[:, :, lanes] = value.astype(HALF).reshape(F, GROUP, 128)
+
+
+def embed_back_kernel(dq_ref, dk_ref, dv_ref, x_ref, d1_ref, w1, w2, w3, v_ref, r_ref, pos_ref, time_ref, sum_ref):
+    q, v = flat(dq_ref), flat(dv_ref)
+    back = dot_back(q, w1[0]) + dot_back(flat(dk_ref), w2[0]) + dot_back(v, w3[0])
+    d, unit = norm_back(flat(x_ref), v_ref[22:23], back)
+    d = d + flat(d1_ref)
+    rounded = d.astype(HALF)
+    r_ref[...] = rounded.reshape(FB, SP, D)
+    add_rows(sum_ref, [column_sum(q), column_sum(v), column_sum(unit), column_sum(back), column_sum(rounded)])
+
+    @pl.when(first_step())
+    def _():
+        pos_ref[...] = jnp.zeros_like(pos_ref)
+
+    total = jnp.zeros((SP, D), FULL)
+    for f in range(FB):
+        part = d[f * SP : (f + 1) * SP]
+        time_ref[f] = column_sum(part)
+        total = total + part
+    pos_ref[...] += total
+
+
+def shape(*dims, dtype=HALF):
+    return jax.ShapeDtypeStruct(dims, dtype)
+
+
+FRAMES = pl.BlockSpec((FB, SP, D), lambda i: (i, 0, 0))
+HIDDEN = pl.BlockSpec((4, FB, SP, D), lambda i: (0, i, 0, 0))
+SLAB = pl.BlockSpec((F, GROUP, D), lambda i: (0, i, 0))
+ROWS16 = shape(F, SP, D)
+ROWS32 = shape(F, SP, D, dtype=FULL)
+HIDDEN16 = shape(4, F, SP, D)
+HIDDEN32 = shape(4, F, SP, D, dtype=FULL)
+
+
+def whole(*dims):
+    return pl.BlockSpec(dims, lambda i: (0,) * len(dims), pipeline_mode=pl.Buffered(1))
+
+
+def matrix(m):
+    return pl.BlockSpec((1, D, D), lambda i: (m, 0, 0), pipeline_mode=pl.Buffered(1))
+
+
+def matrices(first, count):
+    return [matrix(m) for m in range(first, first + count)]
+
+
+def summed(rows):
+    return pl.BlockSpec((rows, D), lambda i: (0, 0))
+
+
+def call(kernel, steps, in_specs, out_specs, out_shape, scratch=()):
+    return pl.pallas_call(
+        kernel,
+        grid=(steps,),
+        in_specs=in_specs,
+        out_specs=out_specs,
+        out_shape=out_shape,
+        scratch_shapes=list(scratch),
+        compiler_params=pltpu.CompilerParams(vmem_limit_bytes=60 * 2**20),
+    )
+
+
+def per_frame(*tail):
+    return pl.BlockSpec((FB,) + tail, lambda i: (i,) + (0,) * len(tail))
+
+
+def forward(mats, table, patches, mask):
+    alive = jnp.pad(mask[0] > 0, ((0, 0), (0, SP - S)))
+    kept = jnp.where(alive, 0.0, MASKED).astype(FULL)
+    places = jnp.arange(SP)[None]
+    space_fill = jnp.where(places < S, kept, jnp.where(places == S, 0.0, NEVER))
+    time_keys = kept.reshape(F, SP // GROUP, GROUP).transpose(1, 0, 2).reshape(SP // GROUP, F * GROUP)
+    spot = jnp.arange(F * GROUP) % GROUP
+    same = spot[:, None] == spot[None]
+    time_fill = jnp.where(same[None], time_keys[:, None, :], NEVER)
+    time_fill_back = jnp.where(same[None], time_keys[:, :, None], NEVER)
+    table = jnp.pad(table, ((0, -table.shape[0] % 8), (0, 0)))
+    pos = jnp.pad(table[31 : 31 + S], ((0, SP - S), (0, 0)))
+    time = table[1 : 1 + F][:, None]
+    one = jnp.where(places[0] < S, 1.0, jnp.where(places[0] == S, 1.0 / F, 0.0)).astype(FULL)
+    share = jnp.broadcast_to(jnp.tile(one, FB)[:, None], (FB * SP, 1))
+    tab = whole(*table.shape)
+    steps = F // FB
+    padded, x0, at, qt, kt, vt = call(
+        embed_kernel, steps,
+        [pl.BlockSpec((1, FB, S, D), lambda i: (0, i, 0, 0))] + matrices(0, 4) + [tab, whole(SP, D), per_frame(1, D)],
+        [FRAMES] * 6, [ROWS16, ROWS32] + [ROWS16] * 4,
+    )(patches, *[mats] * 4, table, pos, time)
+    ot = call(
+        time_kernel, SP // GROUP, [SLAB] * 3 + [pl.BlockSpec((1, F * GROUP, F * GROUP), lambda i: (i, 0, 0))], SLAB, ROWS16,
+    )(qt, kt, vt, time_fill)
+    yt, xs, as_, qs, ks, vs, os_, cls = call(
+        space_kernel, steps, [FRAMES, FRAMES] + matrices(4, 5) + [tab, per_frame(1, SP)],
+        [FRAMES] * 7 + [per_frame(8, D)], [ROWS16, ROWS32] + [ROWS16] * 5 + [shape(F, 8, D, dtype=FULL)],
+    )(ot, x0, *[mats] * 5, table, space_fill[:, None])
+    cls = jnp.mean(cls[:, 0], 0, keepdims=True)
+    of, x2, a2, g, e, x3, pool = call(
+        mlp_kernel, steps,
+        [FRAMES, whole(1, D), FRAMES] + matrices(9, 9) + [tab, whole(FB * SP, 1)],
+        [FRAMES] * 3 + [HIDDEN] * 2 + [FRAMES, summed(8)],
+        [ROWS16, ROWS32, ROWS16, HIDDEN32, HIDDEN16, ROWS32, shape(8, D, dtype=FULL)],
+    )(os_, cls, xs, *[mats] * 9, table, share)
+    pooled = (pool[:1] / (F * S + 1)).astype(HALF)
+    saved = (table, share, space_fill, time_fill_back, padded, x0, at, qt, kt, vt, ot, yt, xs, as_, qs, ks, vs, of, x2, a2, g, e, x3)
+    return pooled, saved
+
+
+def backward(mats, saved, back_pooled):
+    (table, share, space_fill, time_fill, padded, x0, at, qt, kt, vt, ot, yt, xs, as_, qs, ks, vs, of, x2, a2, g, e, x3) = saved
+    tab = whole(*table.shape)
+    steps = F // FB
+    top = back_pooled / (F * S + 1)
+    column = jnp.broadcast_to(space_fill[:, :, None], (F, SP, 128))
+    r3, dg, d2, r2, dq, dk, dv, cq, ck, cv, sums1 = call(
+        mlp_back_kernel, steps,
+        [FRAMES, FRAMES, HIDDEN, whole(1, D)] + matrices(9, 9) + [tab, whole(FB * SP, 1), FRAMES, FRAMES, FRAMES, per_frame(SP, 128)],
+        [FRAMES, HIDDEN] + [FRAMES] * 5 + [per_frame(8, D)] * 3 + [summed(16)],
+        [ROWS16, HIDDEN16, ROWS32] + [ROWS16] * 4 + [shape(F, 8, D, dtype=FULL)] * 3 + [shape(16, D, dtype=FULL)],
+        [pltpu.VMEM((FB, SP, D), HALF)],
+    )(x3, x2, g, top, *[mats] * 9, table, share, qs, ks, vs, column)
+    cls = jnp.concatenate([jnp.sum(part[:, 0], 0, keepdims=True) for part in (cq, ck, cv)], 0)
+    cls = cls.astype(HALF).astype(FULL) / F
+    fq, fk, fv, d1, r1, dy, do, sums2 = call(
+        space_back_kernel, steps,
+        [FRAMES] * 3 + [whole(3, D), FRAMES, FRAMES] + matrices(4, 5) + [tab],
+        [FRAMES] * 7 + [summed(16)],
+        [ROWS16] * 3 + [ROWS32] + [ROWS16] * 3 + [shape(16, D, dtype=FULL)],
+    )(dq, dk, dv, cls, xs, d2, *[mats] * 5, table)
+    tq, tk, tv = call(
+        time_back_kernel, SP // GROUP, [SLAB] * 4 + [pl.BlockSpec((1, F * GROUP, F * GROUP), lambda i: (i, 0, 0))], [SLAB] * 3, [ROWS16] * 3,
+    )(qt, kt, vt, do, time_fill)
+    rp, pos, time, sums3 = call(
+        embed_back_kernel, steps,
+        [FRAMES] * 5 + matrices(1, 3) + [tab],
+        [FRAMES, summed(SP), per_frame(1, D), summed(16)],
+        [ROWS16, shape(SP, D, dtype=FULL), shape(F, 1, D, dtype=FULL), shape(16, D, dtype=FULL)],
+    )(tq, tk, tv, x0, d1, *[mats] * 3, table)
+
+    def product(a, b):
+        return dot_rows(a.reshape(-1, D), b.reshape(-1, D)).astype(HALF)
+
+    pairs = [(padded, rp), (at, tq), (at, tk), (at, tv), (ot, dy), (yt, r1), (as_, fq), (as_, fk), (as_, fv), (of, r2)]
+    pairs += [(a2, dg[k]) for k in range(4)] + [(e[k], r3) for k in range(4)]
+    grad_mats = jnp.stack([product(*pair) for pair in pairs])
+    class_grad = sums2[4:5]
+    grad_vecs = jnp.concatenate(
+        [
+            class_grad, time[:, 0], sums3[4:5], sums3[0:2], sums2[6:7], sums2[5:6], sums2[0:2], sums1[9:10], sums1[3:7], sums1[2:3],
+            sums3[2:4], sums2[2:4], sums1[7:9], sums1[0:2], class_grad, pos[:S],
+        ],
+        0,
+    )
+    return grad_mats, grad_vecs
 
 
 def project(inputs, weight):
@@ -450,321 +847,6 @@
     flat_back = rounded.reshape(-1, rounded.shape[-1])
     grad_weight = jnp.einsum("na,nb->ab", flat_in, flat_back, preferred_element_type=jnp.float32)
     return (back_in, grad_weight, jnp.sum(flat_back, 0, dtype=jnp.float32))
-
-
-def project_many(inputs, weights):
-    return jnp.einsum("...a,kab->k...b", inputs, weights, preferred_element_type=jnp.float32)
-
-
-def project_many_back(inputs, weights, cotangent):
-    rounded = cotangent.astype(jnp.bfloat16)
-    back_in = jnp.einsum("k...b,kab->...a", rounded, weights, preferred_element_type=jnp.float32)
-    flat_in = inputs.reshape(-1, inputs.shape[-1])
-    flat_back = rounded.reshape(rounded.shape[0], -1, rounded.shape[-1])
-    grad_weight = jnp.einsum("na,knb->kab", flat_in, flat_back, preferred_element_type=jnp.float32)
-    return (back_in, grad_weight, jnp.sum(flat_back, 1, dtype=jnp.float32))
-
-
-def stacked_bias(first_row, last_row, rank):
-    rows = jnp.stack([first_row, jnp.zeros_like(first_row), last_row])
-    return rows.reshape((3,) + (1,) * (rank - 2) + (first_row.shape[-1],))
-
-
-def scores_of(query, keys, allowed):
-    raw_scores = jnp.einsum(
-        "blhd,bmhd->bhlm", query, keys, preferred_element_type=jnp.float32
-    ) * HD ** (-0.5)
-    return jnp.where(allowed[:, None, None, :], raw_scores, -1000000000.0)
-
-
-def attend(query, keys, values, allowed):
-    scores = scores_of(query, keys, allowed)
-    highest = jnp.max(scores, -1, keepdims=True)
-    expanded = jnp.exp(scores - highest)
-    summed = jnp.sum(expanded, -1, keepdims=True)
-    probabilities = (expanded / summed).astype(jnp.bfloat16)
-    mixed = jnp.einsum("bhlm,bmhd->blhd", probabilities, values, preferred_element_type=jnp.float32)
-    return (mixed, (highest + jnp.log(summed))[..., 0])
-
-
-def attend_back(query, keys, values, allowed, logsum, back_out):
-    scores = scores_of(query, keys, allowed)
-    probabilities = jnp.exp(scores - logsum[..., None])
-    back_probs = jnp.einsum("blhd,bmhd->bhlm", back_out, values, preferred_element_type=jnp.float32)
-    inner = jnp.sum(back_probs * probabilities, -1, keepdims=True)
-    back_scores = (probabilities * (back_probs - inner)).astype(jnp.bfloat16)
-    factor = HD ** (-0.5)
-    back_query = (
-        jnp.einsum("bhlm,bmhd->blhd", back_scores, keys, preferred_element_type=jnp.float32)
-        * factor
-    )
-    back_keys = (
-        jnp.einsum("bhlm,blhd->bmhd", back_scores, query, preferred_element_type=jnp.float32)
-        * factor
-    )
-    back_values = jnp.einsum(
-        "bhlm,blhd->bmhd",
-        probabilities.astype(jnp.bfloat16),
-        back_out,
-        preferred_element_type=jnp.float32,
-    )
-    return (back_query, back_keys, back_values)
-
-
-def per_patch(tensor, clip_count):
-    return (
-        tensor.reshape(clip_count, F, S, H, HD)
-        .transpose(0, 2, 1, 3, 4)
-        .reshape(clip_count * S, F, H, HD)
-    )
-
-
-def from_patch(tensor, clip_count):
-    return (
-        tensor.reshape(clip_count, S, F, H, HD)
-        .transpose(0, 2, 1, 3, 4)
-        .reshape(clip_count, F, S, H * HD)
-    )
-
-
-def per_frame(tensor, clip_count):
-    width = tensor.shape[-1]
-    leading = jnp.broadcast_to(tensor[:, None, :1], (clip_count, F, 1, width))
-    framed = jnp.concatenate([leading, tensor[:, 1:].reshape(clip_count, F, S, width)], 2)
-    return framed.reshape(clip_count * F, S + 1, H, HD)
-
-
-def from_frame(tensor, clip_count):
-    framed = tensor.reshape(clip_count, F, S + 1, H * HD)
-    return jnp.concatenate(
-        [jnp.sum(framed[:, :, :1], 1), framed[:, :, 1:].reshape(clip_count, F * S, H * HD)], 1
-    )
-
-
-def forward(mats16, head16, vectors, patches, patch_keep_mask):
-    clip_count = patches.shape[0]
-    alive = patch_keep_mask > 0
-    embedded = project(patches, mats16[0]) + vectors[9]
-    start_rows = embedded + vectors[31 : 31 + S][None, None] + vectors[1 : 1 + F][None, :, None]
-    normed_time = layer_norm(start_rows, vectors[22], vectors[23]).astype(jnp.bfloat16)
-    triple_time = (
-        project_many(normed_time, mats16[1:4]) + stacked_bias(vectors[10], vectors[11], 5)
-    ).astype(jnp.bfloat16)
-    live_time = alive.transpose(0, 2, 1).reshape(clip_count * S, F)
-    mixed_time, logsum_time = attend(
-        per_patch(triple_time[0], clip_count),
-        per_patch(triple_time[1], clip_count),
-        per_patch(triple_time[2], clip_count),
-        live_time,
-    )
-    mixed_time = from_patch(mixed_time, clip_count).astype(jnp.bfloat16)
-    moved_time = (project(mixed_time, mats16[4]) + vectors[12]).astype(jnp.bfloat16)
-    after_time = start_rows + project(moved_time, mats16[5]) + vectors[13]
-    leading = jnp.broadcast_to(vectors[0] + vectors[30], (clip_count, 1, D))
-    joined = jnp.concatenate([leading, after_time.reshape(clip_count, F * S, D)], 1)
-    normed_space = layer_norm(joined, vectors[24], vectors[25]).astype(jnp.bfloat16)
-    triple_space = (
-        project_many(normed_space, mats16[6:9]) + stacked_bias(vectors[14], vectors[15], 4)
-    ).astype(jnp.bfloat16)
-    live_space = jnp.concatenate([jnp.ones((clip_count, F, 1), jnp.bool_), alive], 2).reshape(
-        clip_count * F, S + 1
-    )
-    mixed_space, logsum_space = attend(
-        per_frame(triple_space[0], clip_count),
-        per_frame(triple_space[1], clip_count),
-        per_frame(triple_space[2], clip_count),
-        live_space,
-    )
-    mixed_space = mixed_space.reshape(clip_count, F, S + 1, D)
-    mixed_space = jnp.concatenate(
-        [jnp.mean(mixed_space[:, :, :1], 1), mixed_space[:, :, 1:].reshape(clip_count, F * S, D)], 1
-    ).astype(jnp.bfloat16)
-    after_space = joined + project(mixed_space, mats16[9]) + vectors[16]
-    normed_mlp = layer_norm(after_space, vectors[26], vectors[27]).astype(jnp.bfloat16)
-    hidden = project_many(normed_mlp, mats16[10:14]) + vectors[17:21][:, None, None, :]
-    activated = gelu_exact(hidden).astype(jnp.bfloat16)
-    after_mlp = (
-        after_space
-        + jnp.einsum("kcna,kab->cnb", activated, mats16[14:18], preferred_element_type=jnp.float32)
-        + vectors[21]
-    )
-    pooled = jnp.mean(layer_norm(after_mlp, vectors[28], vectors[29]), 1).astype(jnp.bfloat16)
-    projected = project(pooled, head16)
-    saved = (
-        start_rows,
-        normed_time,
-        triple_time,
-        live_time,
-        logsum_time,
-        mixed_time,
-        moved_time,
-        joined,
-        normed_space,
-        triple_space,
-        live_space,
-        logsum_space,
-        mixed_space,
-        after_space,
-        normed_mlp,
-        hidden,
-        activated,
-        after_mlp,
-        pooled,
-    )
-    return (projected, saved)
-
-
-def backward(mats16, head16, vectors, patches, saved, back_projected):
-    (
-        start_rows,
-        normed_time,
-        triple_time,
-        live_time,
-        logsum_time,
-        mixed_time,
-        moved_time,
-        joined,
-        normed_space,
-        triple_space,
-        live_space,
-        logsum_space,
-        mixed_space,
-        after_space,
-        normed_mlp,
-        hidden,
-        activated,
-        after_mlp,
-        pooled,
-    ) = saved
-    clip_count = start_rows.shape[0]
-    rows_clip = joined.shape[1]
-    back_pooled, grad_head, unused_bias = project_back(pooled, head16, back_projected)
-    unused_out, norm_back = jax.vjp(layer_norm, after_mlp, vectors[28], vectors[29])
-    reverse_perceptron, gain_final, shift_final = norm_back(
-        jnp.broadcast_to(back_pooled[:, None] / rows_clip, after_mlp.shape)
-    )
-    rounded = reverse_perceptron.astype(jnp.bfloat16)
-    back_activated = jnp.einsum(
-        "cnb,kab->kcna", rounded, mats16[14:18], preferred_element_type=jnp.float32
-    )
-    grad_down = jnp.einsum("kcna,cnb->kab", activated, rounded, preferred_element_type=jnp.float32)
-    bias_down = jnp.sum(rounded, (0, 1), dtype=jnp.float32)
-    unused_out, gelu_back = jax.vjp(gelu_exact, hidden)
-    (back_hidden,) = gelu_back(back_activated)
-    back_normed, grad_up, bias_up = project_many_back(normed_mlp, mats16[10:14], back_hidden)
-    unused_out, norm_back = jax.vjp(layer_norm, after_space, vectors[26], vectors[27])
-    back_norm_in, gain_mlp, shift_mlp = norm_back(back_normed)
-    back_space = reverse_perceptron + back_norm_in
-    back_mixed, grad_proj_space, bias_proj_space = project_back(mixed_space, mats16[9], back_space)
-    back_mixed = back_mixed.astype(jnp.bfloat16)
-    head_rows = (back_mixed[:, None, :1].astype(jnp.float32) / F).astype(jnp.bfloat16)
-    back_frames = jnp.concatenate(
-        [
-            jnp.broadcast_to(head_rows, (clip_count, F, 1, D)),
-            back_mixed[:, 1:].reshape(clip_count, F, S, D),
-        ],
-        2,
-    ).reshape(clip_count * F, S + 1, H, HD)
-    back_query, back_keys, back_values = attend_back(
-        per_frame(triple_space[0], clip_count),
-        per_frame(triple_space[1], clip_count),
-        per_frame(triple_space[2], clip_count),
-        live_space,
-        logsum_space,
-        back_frames,
-    )
-    back_triple = jnp.stack(
-        [
-            from_frame(back_query, clip_count),
-            from_frame(back_keys, clip_count),
-            from_frame(back_values, clip_count),
-        ]
-    )
-    back_normed, grad_triple_space, bias_triple_space = project_many_back(
-        normed_space, mats16[6:9], back_triple
-    )
-    unused_out, norm_back = jax.vjp(layer_norm, joined, vectors[24], vectors[25])
-    back_norm_in, gain_space, shift_space = norm_back(back_normed)
-    back_joined = back_space + back_norm_in
-    back_class = jnp.sum(back_joined[:, 0], 0)
-    back_after = back_joined[:, 1:].reshape(clip_count, F, S, D)
-    back_moved, grad_fc_time, bias_fc_time = project_back(moved_time, mats16[5], back_after)
-    back_mixed, grad_proj_time, bias_proj_time = project_back(mixed_time, mats16[4], back_moved)
-    back_mixed = per_patch(back_mixed.astype(jnp.bfloat16), clip_count)
-    back_query, back_keys, back_values = attend_back(
-        per_patch(triple_time[0], clip_count),
-        per_patch(triple_time[1], clip_count),
-        per_patch(triple_time[2], clip_count),
-        live_time,
-        logsum_time,
-        back_mixed,
-    )
-    back_triple = jnp.stack(
-        [
-            from_patch(back_query, clip_count),
-            from_patch(back_keys, clip_count),
-            from_patch(back_values, clip_count),
-        ]
-    )
-    back_normed, grad_triple_time, bias_triple_time = project_many_back(
-        normed_time, mats16[1:4], back_triple
-    )
-    unused_out, norm_back = jax.vjp(layer_norm, start_rows, vectors[22], vectors[23])
-    back_norm_in, gain_time, shift_time = norm_back(back_normed)
-    back_start = back_after + back_norm_in
-    rounded = back_start.astype(jnp.bfloat16).reshape(-1, D)
-    grad_embed = jnp.einsum(
-        "na,nb->ab",
-        patches.reshape(-1, patches.shape[-1]),
-        rounded,
-        preferred_element_type=jnp.float32,
-    )
-    embedding_bias = jnp.sum(rounded, 0, dtype=jnp.float32)
-    grad_mats = jnp.concatenate(
-        [
-            grad_embed[None],
-            grad_triple_time,
-            grad_proj_time[None],
-            grad_fc_time[None],
-            grad_triple_space,
-            grad_proj_space[None],
-            grad_up,
-            grad_down,
-        ],
-        0,
-    )
-    grad_vecs = jnp.concatenate(
-        [
-            back_class[None],
-            jnp.sum(back_start, (0, 2)),
-            embedding_bias[None],
-            bias_triple_time[0][None],
-            bias_triple_time[2][None],
-            bias_proj_time[None],
-            bias_fc_time[None],
-            bias_triple_space[0][None],
-            bias_triple_space[2][None],
-            bias_proj_space[None],
-            bias_up,
-            bias_down[None],
-            jnp.stack(
-                [
-                    gain_time,
-                    shift_time,
-                    gain_space,
-                    shift_space,
-                    gain_mlp,
-                    shift_mlp,
-                    gain_final,
-                    shift_final,
-                ]
-            ),
-            back_class[None],
-            jnp.sum(back_start, (0, 1)),
-        ],
-        0,
-    )
-    return (grad_mats, grad_head, grad_vecs)
 
 
 def normalize(projected):
@@ -842,7 +924,8 @@
     )
     mats16 = gathered_mats.reshape(NMAT, D, D)
     head16, vecs16 = unpack(gathered_small, lay.rows)
-    projected, saved = forward(mats16, head16, vecs16.astype(jnp.float32), patches, patch_keep_mask)
+    pooled, saved = forward(mats16, vecs16.astype(jnp.float32), patches, patch_keep_mask)
+    projected = project(pooled, head16)
     unit_length_lines, unit_back = jax.vjp(normalize, projected)
     clip_count, width = unit_length_lines.shape
     lines = unit_length_lines.reshape(-1, 128)
@@ -871,17 +954,11 @@
     offset = lax.axis_index(("dp", "fsdp")) * clip_count
     back_unit = lax.dynamic_slice_in_dim(back_gathered, offset, clip_count, 0)
     (back_projected,) = unit_back(back_unit)
-    grad_mats, grad_head, grad_vecs = backward(
-        mats16,
-        head16,
-        vecs16.astype(jnp.float32),
-        patches,
-        saved,
-        back_projected,
-    )
+    back_pooled, grad_head, unused_bias = project_back(pooled, head16, back_projected)
+    grad_mats, grad_vecs = backward(mats16, saved, back_pooled)
     grad_mats, grad_small = reduce(
         lay,
-        grad_mats.astype(jnp.bfloat16).reshape(NMAT, n, lay.rows, D),
+        grad_mats.reshape(NMAT, n, lay.rows, D),
         pack_all(grad_head, grad_vecs, n).astype(jnp.bfloat16),
     )
     grad_head, grad_vecs = unpack_shard(grad_small, n)

time: 1300 us -> 671 us (0.52)
  local copies, waits for them, and re-layouts: 425 us -> 42.2 us
  matrix products: 394 us -> 47.8 us
  Pallas kernels: 287 us -> 526 us
  other arithmetic: 171 us -> 42.1 us
    dot_general x28 -> x18, matrix products: 358 us -> 46.1 us  [dot_rows(): lax.dot_general(a, b, (((0,), (0,)), ((), ())), preferred_element_type=FULL)]
    pallas_call x0 -> x8, Pallas kernels: none -> 239 us  [the longest x1 72.7 us: backward(): call(mlp_back_kernel, steps, [FRAMES, FRAMES, HIDDEN, whole(1, D)] + matr...]
    another operation x27 -> x5, local copies, waits for them, and re-layouts: 111 us -> 2.22 us  [the longest x1 1.1 us: backward(): grad_mats = jnp.stack([product(*pair) for pair in pairs])]
    slice x28 -> x13, local copies, waits for them, and re-layouts: 84 us -> 5.23 us  [the longest x2 2.09 us: backward(): pairs += [(a2, dg[k]) for k in range(4)] + [(e[k], r3) for k in range(4)]]
    concatenate x11 -> x1, local copies, waits for them, and re-layouts: 78 us -> 0.73 us  [backward(): jnp.concatenate([class_grad, time[:, 0], sums3[4:5], sums3[0:2], sums2[6:...]
    reduce_sum x24 -> x3, other arithmetic: 60.2 us -> 2.97 us  [the longest x2 2.02 us: backward(): jnp.sum(part[:, 0], 0, keepdims=True)]
    dot_general x1 -> x0, other arithmetic: 43.7 us -> none  [backward(): jnp.einsum('kcna,cnb->kab', activated, rounded, preferred_element_type=jn...]
    convert_element_type x9 -> x0, local copies, waits for them, and re-layouts: 36.1 us -> none  [the longest x2 8.14 us: project_back(): rounded = cotangent.astype(jnp.bfloat16)]
where the time goes in v2:
time: 671 us; the launch traced here: 667 us
  Pallas kernels  526 us (78%)
  matrix products  47.8 us (7%)
  local copies, waits for them, and re-layouts  42.2 us (6%)
  other arithmetic  42.1 us (6%)
  between operations  8.79 us (1%)
    pallas_call x1, Pallas kernels, reduce(): pl.pallas_call(functools.partial(reduce_kernel, lay), out_shape=(jax.Shap...  135 us
    pallas_call x1, Pallas kernels, gather(): pl.pallas_call(functools.partial(gather_kernel, lay), out_shape=(jax.Shap...  126 us
    pallas_call x1, Pallas kernels, backward(): call(mlp_back_kernel, steps, [FRAMES, FRAMES, HIDDEN, whole(1, D)] + matr...  72.7 us
    dot_general x18, matrix products, dot_rows(): lax.dot_general(a, b, (((0,), (0,)), ((), ())), preferred_element_type=FULL)  46.1 us
    pallas_call x1, Pallas kernels, forward(): call(mlp_kernel, steps, [FRAMES, whole(1, D), FRAMES] + matrices(9, 9) +...  42.6 us
    pallas_call x1, Pallas kernels, forward(): call(space_kernel, steps, [FRAMES, FRAMES] + matrices(4, 5) + [tab, per_f...  28.4 us
    pallas_call x2, Pallas kernels, spread(): pl.pallas_call(functools.partial(spread_kernel, dp, n), out_shape=jax.Sha...  26.5 us
    pallas_call x1, Pallas kernels, backward(): call(time_back_kernel, SP // GROUP, [SLAB] * 4 + [pl.BlockSpec((1, F * GR...  25.6 us

profile of v2, /device:TPU:0, one launch (start us, length us, event | category | flops | bytes accessed | tf_op | source)
XLA Modules:
  0.0 666.8 jit_solution(17655770884005496914)
XLA Ops:
  0.7 4.4 convert_element_type.89.w_ref
  6.1 125.9 %shard_map.254 = (bf16[18,8,96,768]{3,2,1,0:T(8,128)(2,1)}, bf16[8,2,32,768]{3,2,1,0:T(8,128)(2,1)}) custom-call(bf16[18,96,768]{2,1,0:T(8,128)(2,1)} %convert_element_type.89.w_ref, bf16[2,32,768]{2,1,0:T(8,128)(2,1)} %pad_maximum_fusion.1.s_ref), custom_call_target="tpu_custom_call" | custom-call | tf_op jit(solution)/shard_map/pallas_call | solution.py:168
  139.9 15.4 %shard_map.255 = (bf16[8,208,768]{2,1,0:T(8,128)(2,1)}, f32[8,208,768]{2,1,0:T(8,128)}, bf16[8,208,768]{2,1,0:T(8,128)(2,1)}, bf16[8,208,768]{2,1,0:T(8,128)(2,1...) custom-call(bf16[1,8,196,768]{3,2,1,0:T(8,128)(2,1)} %copy.87.p_ref, bf16[18,768,768]{2,1,0:T(8,128)(2,1)} %bitcast.149, ...), custom_call_target="tpu_custom_call" | custom-call | tf_op jit(solution)/shard_map/pallas_call | solution.py:767
  157.2 16.1 %shard_map.256.o_ref = bf16[8,208,768]{2,1,0:T(8,128)(2,1)} custom-call(bf16[8,208,768]{2,1,0:T(8,128)(2,1)} %get-tuple-element.67.q_ref, bf16[8,208,768]{2,1,0:T(8,128)(2,1)} %get-tuple-element.68.k_ref, bf16[8,208,768]{2,1,0:T(8,128)(2,1)} %get-tuple-element.69.v_ref, f32[13,128,128]{2,1,0:T(8,128)} %get-tuple-element.189.fill_ref), custom_call_target="tpu_custom_call" | custom-call | tf_op jit(solution)/shard_map/pallas_call | solution.py:772
  174.0 28.4 %shard_map.257 = (bf16[8,208,768]{2,1,0:T(8,128)(2,1)}, f32[8,208,768]{2,1,0:T(8,128)}, bf16[8,208,768]{2,1,0:T(8,128)(2,1)}, bf16[8,208,768]{2,1,0:T(8,128)(2,1...) custom-call(bf16[8,208,768]{2,1,0:T(8,128)(2,1)} %shard_map.256.o_re, ...), custom_call_target="tpu_custom_call" | custom-call | tf_op jit(solution)/shard_map/pallas_call | solution.py:775
  204.8 42.6 %shard_map.258 = (bf16[8,208,768]{2,1,0:T(8,128)(2,1)}, f32[8,208,768]{2,1,0:T(8,128)}, bf16[8,208,768]{2,1,0:T(8,128)(2,1)}, f32[4,8,208,768]{3,2,1,0:T(8,128)}...) custom-call(bf16[8,208,768]{2,1,0:T(8,128)(2,1)} %get-tuple-element.71.o_ref, ...), custom_call_target="tpu_custom_call" | custom-call | tf_op jit(solution)/shard_map/pallas_call | solution.py:780
  250.2 13.5 %shard_map.259 = f32[32,8,128]{2,1,0:T(8,128)} custom-call(f32[8,128]{1,0:T(8,128)} %pad.29.x_ref), custom_call_target="tpu_custom_call" | custom-call | tf_op jit(solution)/shard_map/pallas_call | solution.py:421
  270.5 72.7 %shard_map.260 = (bf16[8,208,768]{2,1,0:T(8,128)(2,1)}, bf16[4,8,208,768]{3,2,1,0:T(8,128)(2,1)}, f32[8,208,768]{2,1,0:T(8,128)}, bf16[8,208,768]{2,1,0:T(8,128)...) custom-call(f32[8,208,768]{2,1,0:T(8,128)} %get-tuple-element.76.x3_, ...), custom_call_target="tpu_custom_call" | custom-call | tf_op jit(solution)/shard_map/pallas_call | solution.py:797
  345.9 23.0 %shard_map.261 = (bf16[8,208,768]{2,1,0:T(8,128)(2,1)}, bf16[8,208,768]{2,1,0:T(8,128)(2,1)}, bf16[8,208,768]{2,1,0:T(8,128)(2,1)}, f32[8,208,768]{2,1,0:T(8,128...) custom-call(bf16[8,208,768]{2,1,0:T(8,128)(2,1)} %get-tuple-element., ...), custom_call_target="tpu_custom_call" | custom-call | tf_op jit(solution)/shard_map/pallas_call | solution.py:806
  368.9 25.6 %shard_map.262 = (bf16[8,208,768]{2,1,0:T(8,128)(2,1)}, bf16[8,208,768]{2,1,0:T(8,128)(2,1)}, bf16[8,208,768]{2,1,0:T(8,128)(2,1)}) custom-call(bf16[8,208,768]{2,1,0:T(8,128)(2,1)} %get-tuple-element.67.q_ref, bf16[8,208,768]{2,1,0:T(8,128)(2,1)} %get-tuple-element.68.k_ref, bf16[8,208,768]{2,1,0:T(8,128)(2,1)} %get-tuple-element.69.v_ref, ...), custom_call_target="tpu_custom_call" | custom-call | tf_op jit(solution)/shard_map/pallas_call | solution.py:812
  394.6 14.9 %shard_map.263 = (bf16[8,208,768]{2,1,0:T(8,128)(2,1)}, f32[208,768]{1,0:T(8,128)}, f32[8,1,768]{2,1,0:T(1,128)}, f32[16,768]{1,0:T(8,128)}) custom-call(bf16[8,208,768]{2,1,0:T(8,128)(2,1)} %get-tuple-element.90.dq_ref, bf16[8,208,768]{2,1,0:T(8,128)(2,1)} %get-tuple-element.91.dk_ref, bf16[8,208,768]{2,1,0:T(8,128)(2,1)} %get-tuple-element.92.dv_ref, ...), custom_call_target="tpu_custom_call" | custom-call | tf_op jit(solution)/shard_map/pallas_call | solution.py:815
  409.5 4.2 bitcast_convert_fusion.9
  414.9 2.5 bitcast_convert_fusion.8
  418.4 2.5 bitcast_convert_fusion.7
  425.6 2.5 bitcast_convert_fusion.5
  429.2 2.6 bitcast_convert_fusion.4
  440.2 2.5 bitcast_convert_fusion.1
  443.8 2.5 bitcast_convert_fusion
  456.3 2.5 convolution_convert_fusion.5
  459.9 2.5 convolution_convert_fusion.4
  485.6 134.7 %shard_map.264 = (f32[18,96,768]{2,1,0:T(8,128)}, f32[2,32,768]{2,1,0:T(8,128)}) custom-call(bf16[18,8,96,768]{3,2,1,0:T(8,128)(2,1)} %constant_dynamic-update-slice_fusion.g_ref, bf16[2,8,32,768]{3,2,1,0:T(8,128)(2,1)} %pad_maximum_fusion.s_ref), custom_call_target="tpu_custom_call" | custom-call | tf_op jit(solution)/shard_map/pallas_call | solution.py:375
  620.4 4.5 multiply_reduce_fusion
  629.0 13.0 %shard_map.265 = f32[32,8,128]{2,1,0:T(8,128)} custom-call(f32[8,128]{1,0:T(8,128)} %broadcast_in_dim.173.x_ref), custom_call_target="tpu_custom_call" | custom-call | tf_op jit(solution)/shard_map/pallas_call | solution.py:421
  644.4 18.3 %multiply_add_fusion = (f32[18,96,768]{2,1,0:T(8,128)}, f32[18,96,768]{2,1,0:T(8,128)}, f32[18,96,768]{2,1,0:T(8,128)}, f32[18,96,768]{2,1,0:T(8,128)}) fusion(f32[18,96,768]{2,1,0:T(8,128)} %param.21, f32[18,96,768]{2,1,0:T(8,128)} %param.18, f32[18,96,768]{2,1,0:T(8,128)} %get-tuple-element.114, f32[]{:T(128)S(6)} %div.102, f32[18,96,768]{2,1,0:T(8,128)} %param.19, ...), kind=kLoop, calls=%fused_computation.2 | loop fusion | flops 25214976 | bytes 47775748 | tf_op jit(solution)/shard_map/add | solution.py:863
  (218 shorter events, 80.8 us)
Async XLA Ops:
  0.6 4.4 copy-start.8
  0.7 4.7 copy-start.6
  6.1 128.1 %copy-start.4 = (bf16[1,8,196,768]{3,1,2,0:T(8,128)(2,1)S(1)}, bf16[1,8,196,768]{3,1,2,0:T(8,128)(2,1)}, u32[]{:S(2)}) copy-start(bf16[1,8,196,768]{3,1,2,0:T(8,128)(2,1)} %param.15) | copy-start | bytes 7225348
  139.9 15.5 %copy-start.21 = (s32[1,8,196]{2,1,0:T(8,128)S(1)}, s32[1,8,196]{2,1,0:T(8,128)}, u32[]{:S(2)}) copy-start(s32[1,8,196]{2,1,0:T(8,128)} %param.16) | copy-start | bytes 18820
  204.8 60.0 %copy-start.22 = (s32[32]{0:T(128)S(1)}, s32[32]{0:T(128)}, u32[]{:S(2)}) copy-start(s32[32]{0:T(128)} %param.17) | copy-start | bytes 388
  394.6 14.9 %copy-start.27 = (bf16[8,208,768]{2,1,0:T(8,128)(2,1)S(1)}, bf16[8,208,768]{2,1,0:T(8,128)(2,1)}, u32[]{:S(2)}) copy-start(bf16[8,208,768]{2,1,0:T(8,128)(2,1)} %get-tuple-element.75) | copy-start | bytes 7667716
  409.5 5.4 copy-start.3
  409.5 5.4 copy-start.25
  429.2 3.8 copy-start.34
  439.0 4.8 copy-start.28
  439.0 4.8 copy-start.31
  440.2 7.2 %slice-start.3 = ((s8[10223616]{0:T(1024)(128)(4,1)}), s8[4194304]{0:T(1024)(128)(4,1)S(1)}, s32[]{:S(2)}) async-start(s8[10223616]{0:T(1024)(128)(4,1)} %bitcast.186), calls=%async_computation.3 | async-start | bytes 8388608
  440.2 7.2 %slice-start.4 = ((s8[10223616]{0:T(1024)(128)(4,1)}), s8[4194304]{0:T(1024)(128)(4,1)S(1)}, s32[]{:S(2)}) async-start(s8[10223616]{0:T(1024)(128)(4,1)} %bitcast.186), calls=%async_computation.4 | async-start | bytes 8388608
  456.3 7.1 %slice-start = ((s8[10223616]{0:T(1024)(128)(4,1)}), s8[4194304]{0:T(1024)(128)(4,1)S(1)}, s32[]{:S(2)}) async-start(s8[10223616]{0:T(1024)(128)(4,1)} %bitcast.184), calls=%async_computation | async-start | bytes 8388608
  456.3 7.1 %slice-start.1 = ((s8[10223616]{0:T(1024)(128)(4,1)}), s8[4194304]{0:T(1024)(128)(4,1)S(1)}, s32[]{:S(2)}) async-start(s8[10223616]{0:T(1024)(128)(4,1)} %bitcast.184), calls=%async_computation.1 | async-start | bytes 8388608
  620.4 4.5 copy-start.10
  644.3 18.4 %copy-start.7 = (f32[96,256]{1,0:T(8,128)S(1)}, f32[96,256]{1,0:T(8,128)}, u32[]{:S(2)}) copy-start(f32[96,256]{1,0:T(8,128)} %param.22) | copy-start | bytes 294916
  644.3 18.4 %copy-start.11 = (f32[96,256]{1,0:T(8,128)S(1)}, f32[96,256]{1,0:T(8,128)}, u32[]{:S(2)}) copy-start(f32[96,256]{1,0:T(8,128)} %param.25) | copy-start | bytes 294916
  644.3 18.4 %copy-start.12 = (f32[96,256]{1,0:T(8,128)S(1)}, f32[96,256]{1,0:T(8,128)}, u32[]{:S(2)}) copy-start(f32[96,256]{1,0:T(8,128)} %param.23) | copy-start | bytes 294916
  644.3 18.4 %copy-start.13 = (f32[96,256]{1,0:T(8,128)S(1)}, f32[96,256]{1,0:T(8,128)}, u32[]{:S(2)}) copy-start(f32[96,256]{1,0:T(8,128)} %param.24) | copy-start | bytes 294916
  644.3 19.2 %copy-start.9 = (f32[227,96]{0,1:T(8,128)S(1)}, f32[227,96]{0,1:T(8,128)}, u32[]{:S(2)}) copy-start(f32[227,96]{0,1:T(8,128)} %param.26) | copy-start | bytes 261508
  644.3 19.2 %copy-start.14 = (f32[227,96]{0,1:T(8,128)S(1)}, f32[227,96]{0,1:T(8,128)}, u32[]{:S(2)}) copy-start(f32[227,96]{0,1:T(8,128)} %param.29) | copy-start | bytes 261508
  644.3 19.2 %copy-start.15 = (f32[227,96]{0,1:T(8,128)S(1)}, f32[227,96]{0,1:T(8,128)}, u32[]{:S(2)}) copy-start(f32[227,96]{0,1:T(8,128)} %param.27) | copy-start | bytes 261508
  644.3 19.2 %copy-start.16 = (f32[227,96]{0,1:T(8,128)S(1)}, f32[227,96]{0,1:T(8,128)}, u32[]{:S(2)}) copy-start(f32[227,96]{0,1:T(8,128)} %param.28) | copy-start | bytes 261508
  (19 other events, 60.5 us)

commit v3 on v2

--- a/solution.py
+++ b/solution.py
@@ -180,209 +180,6 @@
         ],
         compiler_params=pltpu.CompilerParams(collective_id=0, has_side_effects=True),
     )(shard, small)
-
-
-def reduce_kernel(lay, g_ref, s_ref, og_ref, os_ref, *scratch):
-    i, a, b, y, c = lay.place()
-    A, B, Y = lay.outer, lay.inner, lay.planes
-    greet(lay, i, a, b, y, c)
-    big, little, out_sem = scratch[:20], scratch[20:40], scratch[40]
-    pending = []
-    here = lay.peer(i, y, 1 - c)
-
-    def remote(src, dst, ssem, rsem, dev):
-        copy = pltpu.make_async_remote_copy(
-            src_ref=src, dst_ref=dst, send_sem=ssem, recv_sem=rsem, device_id=dev, device_id_type=MESH
-        )
-        copy.start()
-        pending.append(copy.wait_send)
-
-    def landed(dst, sems, *at):
-        pltpu.make_async_remote_copy(
-            src_ref=dst, dst_ref=dst, send_sem=sems.at[at], recv_sem=sems.at[at], device_id=here, device_id_type=MESH
-        ).wait_recv()
-
-    class Set:
-        def __init__(self, refs, common, split, source, target):
-            (self.g, self.r, self.ys, self.yr, self.xs, self.xr, self.zs, self.zr, self.fin, self.all_) = refs[:10]
-            (self.lsem, self.rs, self.rr, self.yss, self.yrs, self.xss, self.xrs, self.zss, self.zrs, self.fsem) = refs[10:]
-            self.common, self.split = common, split
-            self.source, self.target = source, target
-            self.blocks = self.g.shape[1]
-
-        def slots(self):
-            found = [(v, q) for v in range(1, Y) for q in range(self.split)]
-            return found + [(None, k) for k in range(self.common)] + [(0, q) for q in range(self.split)]
-
-        def slot(self, v, q):
-            return self.slots().index((v, q))
-
-    def big_at(core, v, q):
-        if v is None:
-            return core * lay.half + q
-        return core * lay.half + lay.common + turn(y, v, Y) * lay.split + q
-
-    mats = Set(big, lay.common, lay.split, lambda core, v, q: g_ref.at[big_at(core, v, q)], lambda core, v, q: og_ref.at[big_at(core, v, q)])
-    rest = Set(little, 1, 0, lambda core, v, q: s_ref.at[core], lambda core, v, q: os_ref.at[core])
-
-    work = [(rest, None, 0)] + [(mats, None, k) for k in range(mats.common)] + [(mats, 0, q) for q in range(mats.split)]
-    starts = [(mats, v, q) for v in range(1, Y) for q in range(mats.split)] + work
-    for st, v, q in starts:
-        n = st.slot(v, q)
-        remote(st.source(1 - c, v, q), st.r.at[n], st.rs.at[n], st.rr.at[n], here)
-        pltpu.make_async_copy(st.source(c, v, q), st.g.at[n], st.lsem.at[n]).start()
-
-    def ready(st, v, q):
-        n = st.slot(v, q)
-        pltpu.make_async_copy(st.source(c, v, q), st.g.at[n], st.lsem.at[n]).wait()
-        landed(st.r.at[n], st.rr, n)
-
-    def base(st, n, v, q, j):
-        total = st.g[n, j].astype(jnp.float32) + st.r[n, j].astype(jnp.float32)
-        if v == 0:
-            for w in range(1, Y):
-                total = total + st.yr[w - 1, q, j].astype(jnp.float32)
-        return total
-
-    def pass_on(st, v, q):
-        n = st.slot(v, q)
-        ready(st, v, q)
-
-        @pl.loop(0, st.blocks)
-        def _(j):
-            st.ys[v - 1, q, j] = base(st, n, None, q, j).astype(jnp.bfloat16)
-
-        remote(st.ys.at[v - 1, q], st.yr.at[v - 1, q], st.yss.at[v - 1, q], st.yrs.at[v - 1, q], lay.peer(i, turn(y, v, Y), c))
-
-    def item(st, v, q):
-        return q if v is None else st.common + q
-
-    def cross(st, v, q):
-        n, k = st.slot(v, q), item(st, v, q)
-        ready(st, v, q)
-        if v == 0:
-            for w in range(1, Y):
-                landed(st.yr.at[w - 1, q], st.yrs, w - 1, q)
-        for u in range(1, B):
-            other = turn(b, u, B)
-
-            @pl.loop(0, A)
-            def _(e):
-                st.xs[k, u - 1, e] = base(st, n, v, q, e * B + other).astype(jnp.bfloat16)
-
-            remote(st.xs.at[k, u - 1], st.xr.at[k, u - 1], st.xss.at[k, u - 1], st.xrs.at[k, u - 1], lay.peer(a * B + other, y, c))
-
-    def along(st, v, q):
-        n, k = st.slot(v, q), item(st, v, q)
-        for u in range(1, B):
-            landed(st.xr.at[k, u - 1], st.xrs, k, u - 1)
-
-        def total(e):
-            value = base(st, n, v, q, e * B + b)
-            for u in range(1, B):
-                value = value + st.xr[k, u - 1, e].astype(jnp.float32)
-            return value
-
-        for t in range(1, A):
-            e = turn(a, t, A)
-            st.zs[k, t - 1] = total(e).astype(jnp.bfloat16)
-            remote(st.zs.at[k, t - 1], st.zr.at[k, t - 1], st.zss.at[k, t - 1], st.zrs.at[k, t - 1], lay.peer(e * B + b, y, c))
-        st.fin[k] = total(a)
-
-    def close(st, v, q):
-        k = item(st, v, q)
-        for t in range(1, A):
-            landed(st.zr.at[k, t - 1], st.zrs, k, t - 1)
-        value = st.fin[k]
-        for t in range(1, A):
-            value = value + st.zr[k, t - 1].astype(jnp.float32)
-        st.fin[k] = value
-        if v is None:
-            st.all_[y, k] = value
-            for w in range(1, Y):
-                remote(st.all_.at[y, k], st.all_.at[y, k], st.fsem.at[0, k, w], st.fsem.at[1, k, w], lay.peer(i, turn(y, w, Y), c))
-        else:
-            target = st.target(c, v, q)
-            for w in range(1, Y):
-                remote(st.fin.at[k], target, st.fsem.at[0, k, w], st.fsem.at[1, k, w], lay.peer(i, turn(y, w, Y), c))
-            finish(st, k, target)
-
-    def finish(st, k, target):
-        copy = pltpu.make_async_copy(st.fin.at[k], target, st.fsem.at[2, k, 0])
-        copy.start()
-        pending.append(copy.wait)
-        remote(st.fin.at[k], target, st.fsem.at[3, k, 0], st.fsem.at[4, k, 0], here)
-
-    def merge(st, v, q):
-        k = item(st, v, q)
-        if v is None:
-            for w in range(1, Y):
-                landed(st.all_.at[turn(y, -w, Y), k], st.fsem, 1, k, w)
-            value = st.all_[0, k]
-            for w in range(1, Y):
-                value = value + st.all_[w, k]
-            st.fin[k] = value
-            finish(st, k, st.target(c, v, q))
-        else:
-            for w in range(1, Y):
-                back = st.target(c, -w, q)
-                landed(back, st.fsem, 1, k, w)
-                remote(back, back, st.fsem.at[3, k, w], st.fsem.at[4, k, w], here)
-
-    others = [(mats, v, q) for v in range(1, Y) for q in range(mats.split)]
-    for job in others:
-        pass_on(*job)
-    for step in range(len(work) + 3):
-        if step < len(work):
-            cross(*work[step])
-        if 0 <= step - 1 < len(work):
-            along(*work[step - 1])
-        if 0 <= step - 2 < len(work):
-            close(*work[step - 2])
-        if 0 <= step - 3 < len(work):
-            merge(*work[step - 3])
-    for st, v, q in work:
-        k = item(st, v, q)
-        landed(st.target(1 - c, v, q), st.fsem, 4, k, 0)
-        if v is not None:
-            for w in range(1, Y):
-                landed(st.target(1 - c, -w, q), st.fsem, 4, k, w)
-    for wait in pending:
-        wait()
-
-
-def reduce_scratch(lay, rows, common, split):
-    A, B, Y, n = lay.outer, lay.inner, lay.planes, lay.n
-    slots, kept, passed, K = common + split * Y, max(split, 1), max(Y - 1, 1), common + split
-    half = jnp.bfloat16
-    dma = pltpu.SemaphoreType.DMA
-    width = rows if split else 16
-    depth = n if split else 1
-    crossed, along = max(B - 1, 1), max(A - 1, 1)
-    return [
-        pltpu.VMEM((slots, n, rows, D), half), pltpu.VMEM((slots, n, rows, D), half),
-        pltpu.VMEM((passed, kept, depth, width, D), half), pltpu.VMEM((passed, kept, depth, width, D), half),
-        pltpu.VMEM((K, crossed, A, rows, D), half), pltpu.VMEM((K, crossed, A, rows, D), half),
-        pltpu.VMEM((K, along, rows, D), half), pltpu.VMEM((K, along, rows, D), half),
-        pltpu.VMEM((K, rows, D), jnp.float32), pltpu.VMEM((Y, K if not split else common, rows, D), jnp.float32),
-        dma((slots,)), dma((slots,)), dma((slots,)), dma((passed, kept)), dma((passed, kept)),
-        dma((K, crossed)), dma((K, crossed)), dma((K, along)), dma((K, along)), dma((5, K, Y)),
-    ]
-
-
-def reduce(lay, grads, small):
-    rows, rest = grads.shape[2], small.shape[2]
-    return pl.pallas_call(
-        functools.partial(reduce_kernel, lay),
-        out_shape=(
-            jax.ShapeDtypeStruct((NMAT, rows, D), jnp.float32),
-            jax.ShapeDtypeStruct((2, rest, D), jnp.float32),
-        ),
-        in_specs=[ANY, ANY],
-        out_specs=(ANY, ANY),
-        scratch_shapes=reduce_scratch(lay, rows, lay.common, lay.split) + reduce_scratch(lay, rest, 1, 0) + [pltpu.SemaphoreType.DMA((1,))],
-        compiler_params=pltpu.CompilerParams(collective_id=1, has_side_effects=True, vmem_limit_bytes=58 * 2**20),
-    )(grads, small)
 
 
 def spread_kernel(dp, n, x_ref, o_ref, ssem, rsem):
@@ -745,6 +542,382 @@
 
 def per_frame(*tail):
     return pl.BlockSpec((FB,) + tail, lambda i: (i,) + (0,) * len(tail))
+
+
+class Part:
+    def __init__(self, lay, first, half, split):
+        self.first, self.half, self.split = first, half, split
+        self.common = half - split * lay.planes
+
+    def order(self):
+        return list(range(self.common, self.half)) + list(range(self.common))
+
+
+class Sums:
+    def __init__(self, refs, common, split):
+        (self.g, self.r, self.ys, self.yr, self.xs, self.xr, self.zs, self.zr, self.fin, self.every) = refs[:10]
+        (self.rs, self.rr, self.yss, self.yrs, self.xss, self.xrs, self.zss, self.zrs, self.fsem) = refs[10:]
+        self.common, self.split = common, split
+
+
+SUMS = 19
+
+
+def sums_scratch(lay, rows, common, split):
+    A, B, Y, n = lay.outer, lay.inner, lay.planes, lay.n
+    slots, kept, passed, K = common + split * Y, max(split, 1), max(Y - 1, 1), common + split
+    dma = pltpu.SemaphoreType.DMA
+    width, depth = (rows, n) if split else (16, 1)
+    crossed, along = max(B - 1, 1), max(A - 1, 1)
+    return [
+        pltpu.VMEM((slots, 2, n, rows, D), HALF), pltpu.VMEM((slots, n, rows, D), HALF),
+        pltpu.VMEM((passed, kept, depth, width, D), HALF), pltpu.VMEM((passed, kept, depth, width, D), HALF),
+        pltpu.VMEM((K, crossed, A, rows, D), HALF), pltpu.VMEM((K, crossed, A, rows, D), HALF),
+        pltpu.VMEM((K, along, rows, D), HALF), pltpu.VMEM((K, along, rows, D), HALF),
+        pltpu.VMEM((K, rows, D), FULL), pltpu.VMEM((Y, common, rows, D), FULL),
+        dma((slots,)), dma((slots,)), dma((passed, kept)), dma((passed, kept)),
+        dma((K, crossed)), dma((K, crossed)), dma((K, along)), dma((K, along)), dma((5, K, Y)),
+    ]
+
+
+class Reducer:
+    def __init__(self, lay):
+        self.lay = lay
+        self.i, self.a, self.b, self.y, self.c = lay.place()
+        self.here = lay.peer(self.i, self.y, 1 - self.c)
+        self.pending = []
+        greet(lay, self.i, self.a, self.b, self.y, self.c)
+
+    def remote(self, src, dst, sends, at, recvs, dev, like):
+        pltpu.make_async_remote_copy(
+            src_ref=src, dst_ref=dst, send_sem=sends.at[at], recv_sem=recvs[0].at[recvs[1]], device_id=dev, device_id_type=MESH
+        ).start()
+        self.pending.append((like, sends, at, True))
+
+    def wait_all(self):
+        for make, sems, at, remote in self.pending:
+            like = make()
+            if remote:
+                pltpu.make_async_remote_copy(
+                    src_ref=like, dst_ref=like, send_sem=sems.at[at], recv_sem=sems.at[at], device_id=self.here, device_id_type=MESH
+                ).wait_send()
+            else:
+                pltpu.make_async_copy(like, like, sems.at[at]).wait()
+
+    def landed(self, dst, sems, *at):
+        pltpu.make_async_remote_copy(
+            src_ref=dst, dst_ref=dst, send_sem=sems.at[at], recv_sem=sems.at[at], device_id=self.here, device_id_type=MESH
+        ).wait_recv()
+
+    def slot(self, st, v, q):
+        if v is None:
+            return q
+        return st.common + turn(self.y, v, self.lay.planes) * st.split + q
+
+    def hand(self, st, h):
+        self.remote(st.g.at[h, 1 - self.c], st.r.at[h], st.rs, (h,), (st.rr, (h,)), self.here, lambda: st.r.at[h])
+
+    def base(self, st, v, q, j):
+        n = self.slot(st, v, q)
+        total = st.g[n, self.c, j].astype(FULL) + st.r[n, j].astype(FULL)
+        if v == 0:
+            for w in range(1, self.lay.planes):
+                total = total + st.yr[w - 1, q, j].astype(FULL)
+        return total
+
+    def pass_on(self, st, v, q):
+        n = self.slot(st, v, q)
+        self.landed(st.r.at[n], st.rr, n)
+
+        @pl.loop(0, self.lay.n)
+        def _(j):
+            st.ys[v - 1, q, j] = self.base(st, v, q, j).astype(HALF)
+
+        self.remote(
+            st.ys.at[v - 1, q], st.yr.at[v - 1, q], st.yss, (v - 1, q), (st.yrs, (v - 1, q)),
+            self.lay.peer(self.i, turn(self.y, v, self.lay.planes), self.c), lambda: st.ys.at[v - 1, q],
+        )
+
+    def item(self, st, v, q):
+        return q if v is None else st.common + q
+
+    def cross(self, st, target, v, q):
+        k, n = self.item(st, v, q), self.slot(st, v, q)
+        self.landed(st.r.at[n], st.rr, n)
+        if v == 0:
+            for w in range(1, self.lay.planes):
+                self.landed(st.yr.at[w - 1, q], st.yrs, w - 1, q)
+        for u in range(1, self.lay.inner):
+            other = turn(self.b, u, self.lay.inner)
+
+            @pl.loop(0, self.lay.outer)
+            def _(e):
+                st.xs[k, u - 1, e] = self.base(st, v, q, e * self.lay.inner + other).astype(HALF)
+
+            self.remote(
+                st.xs.at[k, u - 1], st.xr.at[k, u - 1], st.xss, (k, u - 1), (st.xrs, (k, u - 1)),
+                self.lay.peer(self.a * self.lay.inner + other, self.y, self.c), lambda u=u: st.xs.at[k, u - 1],
+            )
+
+    def along(self, st, target, v, q):
+        k = self.item(st, v, q)
+        inner, outer = self.lay.inner, self.lay.outer
+        for u in range(1, inner):
+            self.landed(st.xr.at[k, u - 1], st.xrs, k, u - 1)
+
+        def total(e):
+            value = self.base(st, v, q, e * inner + self.b)
+            for u in range(1, inner):
+                value = value + st.xr[k, u - 1, e].astype(FULL)
+            return value
+
+        for t in range(1, outer):
+            e = turn(self.a, t, outer)
+            st.zs[k, t - 1] = total(e).astype(HALF)
+            self.remote(
+                st.zs.at[k, t - 1], st.zr.at[k, t - 1], st.zss, (k, t - 1), (st.zrs, (k, t - 1)),
+                self.lay.peer(e * inner + self.b, self.y, self.c), lambda t=t: st.zs.at[k, t - 1],
+            )
+        st.fin[k] = total(self.a)
+
+    def close(self, st, target, v, q):
+        k, Y = self.item(st, v, q), self.lay.planes
+        for t in range(1, self.lay.outer):
+            self.landed(st.zr.at[k, t - 1], st.zrs, k, t - 1)
+        value = st.fin[k]
+        for t in range(1, self.lay.outer):
+            value = value + st.zr[k, t - 1].astype(FULL)
+        if v is None:
+            st.every[self.y, k] = value
+            source, landing = st.every.at[self.y, k], st.every.at[self.y, k]
+            like = lambda: st.every.at[0, k]
+        else:
+            st.fin[k] = value
+            source = st.fin.at[k]
+            like = lambda: st.fin.at[k]
+            landing = target(self.c, self.slot(st, v, q))
+        for w in range(1, Y):
+            self.remote(source, landing, st.fsem, (0, k, w), (st.fsem, (1, k, w)), self.lay.peer(self.i, turn(self.y, w, Y), self.c), like)
+        if v is not None:
+            self.finish(st, k, landing)
+
+    def finish(self, st, k, landing):
+        pltpu.make_async_copy(st.fin.at[k], landing, st.fsem.at[2, k, 0]).start()
+        self.pending.append((lambda: st.fin.at[k], st.fsem, (2, k, 0), False))
+        self.remote(st.fin.at[k], landing, st.fsem, (3, k, 0), (st.fsem, (4, k, 0)), self.here, lambda: st.fin.at[k])
+
+    def merge(self, st, target, v, q):
+        k, Y = self.item(st, v, q), self.lay.planes
+        if v is None:
+            for w in range(1, Y):
+                self.landed(st.every.at[turn(self.y, -w, Y), k], st.fsem, 1, k, w)
+            value = st.every[0, k]
+            for w in range(1, Y):
+                value = value + st.every[w, k]
+            st.fin[k] = value
+            self.finish(st, k, target(self.c, q))
+        else:
+            for w in range(1, Y):
+                back = target(self.c, self.slot(st, -w, q))
+                self.landed(back, st.fsem, 1, k, w)
+                self.remote(back, back, st.fsem, (3, k, w), (st.fsem, (4, k, w)), self.here, lambda: target(0, 0))
+
+    def last(self, st, target, v, q):
+        k = self.item(st, v, q)
+        self.landed(target(1 - self.c, self.slot(st, v, q)), st.fsem, 4, k, 0)
+        if v is not None:
+            for w in range(1, self.lay.planes):
+                self.landed(target(1 - self.c, self.slot(st, -w, q)), st.fsem, 4, k, w)
+
+    def progress(self, work, step):
+        for lag, stage in enumerate((self.cross, self.along, self.close, self.merge)):
+            if 0 <= step - lag < len(work):
+                stage(*work[step - lag])
+
+    def done(self, work):
+        for job in work:
+            self.last(*job)
+        self.wait_all()
+
+
+def outer_products(rows, operands, jobs, st, after, a_buf, b_buf, sems):
+    n = st.g.shape[2]
+    lefts, rights, plan = [], [], []
+    for slot, core, left, right in jobs:
+        fresh = [not lefts or lefts[-1] != left, not rights or rights[-1] != right]
+        if fresh[0]:
+            lefts.append(left)
+        if fresh[1]:
+            rights.append(right)
+        plan.append((slot, core, len(lefts) - 1, len(rights) - 1, fresh))
+
+    def load(kind, loads, k):
+        number, block = loads[k]
+        buf = (a_buf, b_buf)[kind]
+        return pltpu.make_async_copy(operands[number].at[pl.ds(block * rows, rows)], buf.at[k % 2], sems.at[kind, k % 2])
+
+    load(0, lefts, 0).start()
+    load(1, rights, 0).start()
+    for slot, core, left, right, fresh in plan:
+        if fresh[0]:
+            load(0, lefts, left).wait()
+        if fresh[1]:
+            load(1, rights, right).wait()
+        if fresh[0] and left + 1 < len(lefts):
+            load(0, lefts, left + 1).start()
+        if fresh[1] and right + 1 < len(rights):
+            load(1, rights, right + 1).start()
+        value = dot_rows(a_buf[left % 2], b_buf[right % 2])
+        st.g[slot, core] = value.reshape(n, -1, D).astype(HALF)
+        if core == 1:
+            after(slot)
+
+
+def product_buffers(rows):
+    return [
+        pltpu.VMEM((2, rows, D), HALF), pltpu.VMEM((2, rows, D), HALF), pltpu.SemaphoreType.DMA((2, 2)),
+    ]
+
+
+def product_jobs(part, pairs):
+    return [(h, core, *pairs[2 * h + core]) for h in part.order() for core in range(2)]
+
+
+def part_work(lay, part, st, target):
+    return [(st, target, None, k) for k in range(part.common)] + [(st, target, 0, q) for q in range(part.split)]
+
+
+def products_and_hand(red, part, st, work, operands, jobs, buffers):
+    passed = [(v, q) for v in range(1, red.lay.planes) for q in range(part.split)]
+    order = part.order()
+    ahead = len(work) - part.common - part.split
+
+    def after(h):
+        red.hand(st, h)
+        place = order.index(h) - (part.half - part.common)
+        if place == 0 or part.common == 0 and h == order[-1]:
+            for v, q in passed:
+                red.pass_on(st, v, q)
+        if place >= 1 - ahead and place + ahead - 1 < steps_beside(part, ahead):
+            red.progress(work, place + ahead - 1)
+
+    outer_products(F * SP, operands, jobs, st, after, *buffers)
+
+
+def steps_beside(part, ahead):
+    return max(part.common + ahead - 1, 0)
+
+
+def early_kernel(lay, part, pairs, *refs):
+    (e_ref, r3_ref, a2_ref, dg_ref, dq_ref, dk_ref, dv_ref, cls_ref, xs_ref, d2_ref, qt_ref, kt_ref, vt_ref, fill_ref, x0_ref, mats_ref, v_ref) = refs[:17]
+    (og_ref, fq_ref, fk_ref, fv_ref, d1_ref, r1_ref, dy_ref, do_ref, tq_ref, tk_ref, tv_ref, rp_ref, sum2_ref, pos_ref, time_ref, sum3_ref) = refs[17:33]
+    red = Reducer(lay)
+    st = Sums(refs[33 : 33 + SUMS], part.common, part.split)
+    w_buf, w_sem = refs[33 + SUMS :]
+    load = pltpu.make_async_copy(mats_ref.at[pl.ds(1, 8)], w_buf, w_sem.at[0])
+    load.start()
+
+    def target(core, h):
+        return og_ref.at[2 * h + core]
+
+    work = part_work(lay, part, st, target)
+    rows = F * SP
+    jobs = product_jobs(part, pairs)
+    pl.run_scoped(lambda *buffers: products_and_hand(red, part, st, work, (e_ref, r3_ref, a2_ref, dg_ref), jobs, buffers), *product_buffers(rows))
+    begun = steps_beside(part, 0)
+    load.wait()
+    ws = [w_buf.at[pl.ds(k, 1)] for k in range(8)]
+
+    steps = F // FB
+
+    def space(dq, dk, dv, xs, d2, fq, fk, fv, d1, r1, dy, do):
+        space_back_kernel(dq, dk, dv, cls_ref, xs, d2, ws[3], ws[4], ws[5], ws[6], ws[7], v_ref, fq, fk, fv, d1, r1, dy, do, sum2_ref)
+        for s in range(steps):
+            @pl.when(pl.program_id(0) == s)
+            def _():
+                red.progress(work, begun + s)
+
+    pltpu.emit_pipeline(space, grid=(steps,), in_specs=[FRAMES] * 5, out_specs=[FRAMES] * 7)(
+        dq_ref, dk_ref, dv_ref, xs_ref, d2_ref, fq_ref, fk_ref, fv_ref, d1_ref, r1_ref, dy_ref, do_ref
+    )
+
+    def time(q, k, v, d, fill, dq, dk, dv):
+        time_back_kernel(q, k, v, d, fill, dq, dk, dv)
+
+        @pl.when(pl.program_id(0) == 6)
+        def _():
+            red.progress(work, begun + steps)
+
+    pltpu.emit_pipeline(time, grid=(SP // GROUP,), in_specs=[SLAB] * 4 + [FILL], out_specs=[SLAB] * 3)(
+        qt_ref, kt_ref, vt_ref, do_ref, fill_ref, tq_ref, tk_ref, tv_ref
+    )
+    red.progress(work, begun + steps + 1)
+
+    def embed(dq, dk, dv, x, d1, r, time):
+        embed_back_kernel(dq, dk, dv, x, d1, ws[0], ws[1], ws[2], v_ref, r, pos_ref, time, sum3_ref)
+
+    pltpu.emit_pipeline(embed, grid=(steps,), in_specs=[FRAMES] * 5, out_specs=[FRAMES, per_frame(1, D)])(
+        tq_ref, tk_ref, tv_ref, x0_ref, d1_ref, rp_ref, time_ref
+    )
+    for s in range(begun + steps + 2, len(work) + 3):
+        red.progress(work, s)
+    red.done(work)
+
+
+FILL = pl.BlockSpec((1, F * GROUP, F * GROUP), lambda i: (i, 0, 0))
+
+
+def early(lay, part, pairs, arrays, cls, table):
+    vmem = pl.BlockSpec(memory_space=pltpu.VMEM)
+    e, r3, a2, dg, dq, dk, dv, xs, d2, qt, kt, vt, fill, x0, mats = arrays
+    two = lambda x: x.reshape(-1, D)
+    full = functools.partial(shape, dtype=FULL)
+    return pl.pallas_call(
+        functools.partial(early_kernel, lay, part, pairs),
+        in_specs=[ANY] * 7 + [vmem] + [ANY] * 8 + [vmem],
+        out_specs=[ANY] * 12 + [vmem, vmem, ANY, vmem],
+        out_shape=[full(2 * part.half, lay.rows, D), ROWS16, ROWS16, ROWS16, ROWS32] + [ROWS16] * 7 + [full(16, D), full(SP, D), full(F, 1, D), full(16, D)],
+        scratch_shapes=sums_scratch(lay, lay.rows, part.common, part.split) + [pltpu.VMEM((8, D, D), HALF), pltpu.SemaphoreType.DMA((1,))],
+        compiler_params=pltpu.CompilerParams(collective_id=1, has_side_effects=True, vmem_limit_bytes=62 * 2**20),
+    )(two(e), two(r3), two(a2), two(dg), dq, dk, dv, cls, xs, d2, qt, kt, vt, fill, x0, mats, table)
+
+
+def late_kernel(lay, part, pairs, count, *refs):
+    s_ref, operands = refs[0], refs[1 : 1 + count]
+    og_ref, os_ref = refs[1 + count : 3 + count]
+    red = Reducer(lay)
+    rest = refs[3 + count :]
+    st = Sums(rest[:SUMS], part.common, part.split)
+    little = Sums(rest[SUMS : 2 * SUMS], 1, 0)
+    small_sem = rest[2 * SUMS]
+    load = pltpu.make_async_copy(s_ref, little.g.at[0], small_sem.at[0])
+    load.start()
+
+    def target(core, h):
+        return og_ref.at[2 * h + core]
+
+    work = part_work(lay, part, st, target)
+    work = [(little, lambda core, h: os_ref.at[core], None, 0)] + work
+    rows = F * SP
+    jobs = product_jobs(part, pairs)
+    load.wait()
+    red.hand(little, 0)
+    pl.run_scoped(lambda *buffers: products_and_hand(red, part, st, work, operands, jobs, buffers), *product_buffers(rows))
+    for s in range(steps_beside(part, 1), len(work) + 3):
+        red.progress(work, s)
+    red.done(work)
+
+
+def late(lay, part, pairs, small, arrays):
+    full = functools.partial(shape, dtype=FULL)
+    return pl.pallas_call(
+        functools.partial(late_kernel, lay, part, pairs, len(arrays)),
+        in_specs=[ANY] * (1 + len(arrays)),
+        out_specs=[ANY, ANY],
+        out_shape=[full(2 * part.half, lay.rows, D), full(2, small.shape[2], D)],
+        scratch_shapes=sums_scratch(lay, lay.rows, part.common, part.split) + sums_scratch(lay, small.shape[2], 1, 0) + [pltpu.SemaphoreType.DMA((1,))],
+        compiler_params=pltpu.CompilerParams(collective_id=4, has_side_effects=True, vmem_limit_bytes=62 * 2**20),
+    )(small, *[x.reshape(-1, D) for x in arrays])
 
 
 def forward(mats, table, patches, mask):
@@ -788,7 +961,7 @@
     return pooled, saved
 
 
-def backward(mats, saved, back_pooled):
+def backward(lay, mats, saved, back_pooled):
     (table, share, space_fill, time_fill, padded, x0, at, qt, kt, vt, ot, yt, xs, as_, qs, ks, vs, of, x2, a2, g, e, x3) = saved
     tab = whole(*table.shape)
     steps = F // FB
@@ -803,28 +976,11 @@
     )(x3, x2, g, top, *[mats] * 9, table, share, qs, ks, vs, column)
     cls = jnp.concatenate([jnp.sum(part[:, 0], 0, keepdims=True) for part in (cq, ck, cv)], 0)
     cls = cls.astype(HALF).astype(FULL) / F
-    fq, fk, fv, d1, r1, dy, do, sums2 = call(
-        space_back_kernel, steps,
-        [FRAMES] * 3 + [whole(3, D), FRAMES, FRAMES] + matrices(4, 5) + [tab],
-        [FRAMES] * 7 + [summed(16)],
-        [ROWS16] * 3 + [ROWS32] + [ROWS16] * 3 + [shape(16, D, dtype=FULL)],
-    )(dq, dk, dv, cls, xs, d2, *[mats] * 5, table)
-    tq, tk, tv = call(
-        time_back_kernel, SP // GROUP, [SLAB] * 4 + [pl.BlockSpec((1, F * GROUP, F * GROUP), lambda i: (i, 0, 0))], [SLAB] * 3, [ROWS16] * 3,
-    )(qt, kt, vt, do, time_fill)
-    rp, pos, time, sums3 = call(
-        embed_back_kernel, steps,
-        [FRAMES] * 5 + matrices(1, 3) + [tab],
-        [FRAMES, summed(SP), per_frame(1, D), summed(16)],
-        [ROWS16, shape(SP, D, dtype=FULL), shape(F, 1, D, dtype=FULL), shape(16, D, dtype=FULL)],
-    )(tq, tk, tv, x0, d1, *[mats] * 3, table)
-
-    def product(a, b):
-        return dot_rows(a.reshape(-1, D), b.reshape(-1, D)).astype(HALF)
-
-    pairs = [(padded, rp), (at, tq), (at, tk), (at, tv), (ot, dy), (yt, r1), (as_, fq), (as_, fk), (as_, fv), (of, r2)]
-    pairs += [(a2, dg[k]) for k in range(4)] + [(e[k], r3) for k in range(4)]
-    grad_mats = jnp.stack([product(*pair) for pair in pairs])
+    first = Part(lay, 10, 4, 1 if lay.planes <= 4 else 0)
+    pairs = [((2, 0), (3, k)) for k in range(4)] + [((0, k), (1, 0)) for k in range(4)]
+    upper, fq, fk, fv, d1, r1, dy, do, tq, tk, tv, rp, sums2, pos, time, sums3 = early(
+        lay, first, pairs, (e, r3, a2, dg, dq, dk, dv, xs, d2, qt, kt, vt, time_fill, x0, mats), cls, table
+    )
     class_grad = sums2[4:5]
     grad_vecs = jnp.concatenate(
         [
@@ -833,7 +989,16 @@
         ],
         0,
     )
-    return grad_mats, grad_vecs
+    second = Part(lay, 0, 5, 1 if lay.planes <= 4 else 0)
+    operands = (padded, rp, at, tq, tk, tv, ot, dy, yt, r1, as_, fq, fk, fv, of, r2)
+    pairs = [(0, 1), (2, 3), (2, 4), (2, 5), (6, 7), (8, 9), (10, 11), (10, 12), (10, 13), (14, 15)]
+    pairs = [((left, 0), (right, 0)) for left, right in pairs]
+
+    def finish(small):
+        lower, rest = late(lay, second, pairs, small, operands)
+        return jnp.concatenate([lower, upper], 0), rest
+
+    return finish, grad_vecs
 
 
 def project(inputs, weight):
@@ -955,12 +1120,9 @@
     back_unit = lax.dynamic_slice_in_dim(back_gathered, offset, clip_count, 0)
     (back_projected,) = unit_back(back_unit)
     back_pooled, grad_head, unused_bias = project_back(pooled, head16, back_projected)
-    grad_mats, grad_vecs = backward(mats16, saved, back_pooled)
-    grad_mats, grad_small = reduce(
-        lay,
-        grad_mats.reshape(NMAT, n, lay.rows, D),
-        pack_all(grad_head, grad_vecs, n).astype(jnp.bfloat16),
-    )
+    finish, grad_vecs = backward(lay, mats16, saved, back_pooled)
+    small = pack_all(grad_head, grad_vecs, n).astype(jnp.bfloat16)
+    grad_mats, grad_small = finish(small)
     grad_head, grad_vecs = unpack_shard(grad_small, n)
     partial_squares = (
         jnp.sum(grad_mats * grad_mats)

time: 671 us -> 639 us (0.952)
  matrix products: 47.8 us -> 1.71 us
  Pallas kernels: 526 us -> 557 us
  local copies, waits for them, and re-layouts: 42.2 us -> 25.6 us
    dot_general x18 -> x0, matrix products: 46.1 us -> none  [dot_rows(): lax.dot_general(a, b, (((0,), (0,)), ((), ())), preferred_element_type=FULL)]
    pallas_call x4 -> x2, Pallas kernels: 198 us -> 231 us  [the longest x1 127 us: early(): pl.pallas_call(functools.partial(early_kernel, lay, part, pairs), in_spec...]
    unnamed x107 -> x39, local copies, waits for them, and re-layouts: 22.6 us -> 7.09 us
where the time goes in v3:
time: 639 us; the launch traced here: 634 us
  Pallas kernels  557 us (87%)
  other arithmetic  41.4 us (6%)
  local copies, waits for them, and re-layouts  25.6 us (4%)
  between operations  8.48 us (1%)
    pallas_call x1, Pallas kernels, early(): pl.pallas_call(functools.partial(early_kernel, lay, part, pairs), in_spec...  127 us
    pallas_call x1, Pallas kernels, gather(): pl.pallas_call(functools.partial(gather_kernel, lay), out_shape=(jax.Shap...  126 us
    pallas_call x1, Pallas kernels, late(): pl.pallas_call(functools.partial(late_kernel, lay, part, pairs, len(array...  104 us
    pallas_call x1, Pallas kernels, backward(): call(mlp_back_kernel, steps, [FRAMES, FRAMES, HIDDEN, whole(1, D)] + matr...  72.7 us
    pallas_call x1, Pallas kernels, forward(): call(mlp_kernel, steps, [FRAMES, whole(1, D), FRAMES] + matrices(9, 9) +...  42.6 us
    pallas_call x1, Pallas kernels, forward(): call(space_kernel, steps, [FRAMES, FRAMES] + matrices(4, 5) + [tab, per_f...  28.4 us
    pallas_call x2, Pallas kernels, spread(): pl.pallas_call(functools.partial(spread_kernel, dp, n), out_shape=jax.Sha...  24.5 us
    add x3, other arithmetic, adamw_step(): average = AVERAGE_KEEP * average + (1.0 - AVERAGE_KEEP) * weight  20 us

profile of v3, /device:TPU:0, one launch (start us, length us, event | category | flops | bytes accessed | tf_op | source)
XLA Modules:
  0.0 634.2 jit_solution(8772696060045291929)
XLA Ops:
  0.7 4.4 convert_element_type.35.w_ref
  6.1 125.9 %shard_map.254 = (bf16[18,8,96,768]{3,2,1,0:T(8,128)(2,1)}, bf16[8,2,32,768]{3,2,1,0:T(8,128)(2,1)}) custom-call(bf16[18,96,768]{2,1,0:T(8,128)(2,1)} %convert_element_type.35.w_ref, bf16[2,32,768]{2,1,0:T(8,128)(2,1)} %pad_maximum_fusion.1.s_ref), custom_call_target="tpu_custom_call" | custom-call | tf_op jit(solution)/shard_map/pallas_call | solution.py:168
  132.0 1.9 fusion.34
  134.2 1.9 copy.87.p_ref
  136.1 1.5 reshape_squeeze.9
  140.9 15.5 %shard_map.255 = (bf16[8,208,768]{2,1,0:T(8,128)(2,1)}, f32[8,208,768]{2,1,0:T(8,128)}, bf16[8,208,768]{2,1,0:T(8,128)(2,1)}, bf16[8,208,768]{2,1,0:T(8,128)(2,1...) custom-call(bf16[1,8,196,768]{3,2,1,0:T(8,128)(2,1)} %copy.87.p_ref, bf16[18,768,768]{2,1,0:T(8,128)(2,1)} %bitcast.85, ...), custom_call_target="tpu_custom_call" | custom-call | tf_op jit(solution)/shard_map/pallas_call | solution.py:940
  156.7 1.5 broadcast_select_fusion
  158.2 16.1 %shard_map.256.o_ref = bf16[8,208,768]{2,1,0:T(8,128)(2,1)} custom-call(bf16[8,208,768]{2,1,0:T(8,128)(2,1)} %get-tuple-element.66.q_ref.refs_10_, bf16[8,208,768]{2,1,0:T(8,128)(2,1)} %get-tuple-element.67.k_ref.refs_11_, bf16[8,208,768]{2,1,0:T(8,128)(2,1)} %get-tuple-element.68.v_ref.refs_12_, f32[13,128,128]{2,1,0:T(8,128)} %get-tuple-element.179.fill_ref), custom_call_target="tpu_custom_call" | custom-call | tf_op jit(solution)/shard_map/pallas_call | solution.py:945
  175.0 28.4 %shard_map.257 = (bf16[8,208,768]{2,1,0:T(8,128)(2,1)}, f32[8,208,768]{2,1,0:T(8,128)}, bf16[8,208,768]{2,1,0:T(8,128)(2,1)}, bf16[8,208,768]{2,1,0:T(8,128)(2,1...) custom-call(bf16[8,208,768]{2,1,0:T(8,128)(2,1)} %shard_map.256.o_re, ...), custom_call_target="tpu_custom_call" | custom-call | tf_op jit(solution)/shard_map/pallas_call | solution.py:948
  205.8 42.6 %shard_map.258 = (bf16[8,208,768]{2,1,0:T(8,128)(2,1)}, f32[8,208,768]{2,1,0:T(8,128)}, bf16[8,208,768]{2,1,0:T(8,128)(2,1)}, f32[4,8,208,768]{3,2,1,0:T(8,128)}...) custom-call(bf16[8,208,768]{2,1,0:T(8,128)(2,1)} %get-tuple-element.70.o_ref, ...), custom_call_target="tpu_custom_call" | custom-call | tf_op jit(solution)/shard_map/pallas_call | solution.py:953
  251.3 13.5 %shard_map.259 = f32[32,8,128]{2,1,0:T(8,128)} custom-call(f32[8,128]{1,0:T(8,128)} %pad.29.x_ref), custom_call_target="tpu_custom_call" | custom-call | tf_op jit(solution)/shard_map/pallas_call | solution.py:218
  269.8 1.2 broadcast_in_dim.168.fill_ref
  271.0 72.7 %shard_map.260 = (bf16[8,208,768]{2,1,0:T(8,128)(2,1)}, bf16[4,8,208,768]{3,2,1,0:T(8,128)(2,1)}, f32[8,208,768]{2,1,0:T(8,128)}, bf16[8,208,768]{2,1,0:T(8,128)...) custom-call(f32[8,208,768]{2,1,0:T(8,128)} %get-tuple-element.75.x3_, ...), custom_call_target="tpu_custom_call" | custom-call | tf_op jit(solution)/shard_map/pallas_call | solution.py:970
  343.7 1.1 slice_reduce_fusion
  344.8 1.0 slice_reduce_fusion.2
  346.4 127.3 %shard_map.261 = (f32[8,96,768]{2,1,0:T(8,128)}, bf16[8,208,768]{2,1,0:T(8,128)(2,1)}, bf16[8,208,768]{2,1,0:T(8,128)(2,1)}, bf16[8,208,768]{2,1,0:T(8,128)(2,1)...) custom-call(bf16[6656,768]{1,0:T(8,128)(2,1)} %bitcast.114, ...), custom_call_target="tpu_custom_call" | custom-call | tf_op jit(solution)/shard_map/pallas_call | solution.py:875
  477.0 1.1 slice.194
  483.1 103.9 %shard_map.262 = (f32[10,96,768]{2,1,0:T(8,128)}, f32[2,32,768]{2,1,0:T(8,128)}) custom-call(bf16[2,8,32,768]{3,2,1,0:T(8,128)(2,1)} %pad_maximum_fusion.refs_0_, bf16[1664,768]{1,0:T(8,128)(2,1)} %bitcast.118, bf16[1664,768]{1,0:T(8,128)(2,1)} %bitcast.133, bf16[1664,768]{1,0:T(8,128)(2,1)} %bitcast.119, bf16[1664,768]{1,0:T(8,128)(2,1)} %bitcast.130, ...), custom_call_target="tpu_custom_call" | custom-call | tf_op jit(solution)/shard_map/pallas_call | solution.py:913
  587.0 2.3 constant_dynamic-update-slice_fusion.1
  589.8 2.4 copy-done
  592.2 2.0 multiply_reduce_fusion
  598.3 11.1 %shard_map.263 = f32[32,8,128]{2,1,0:T(8,128)} custom-call(f32[8,128]{1,0:T(8,128)} %broadcast_in_dim.173.x_ref), custom_call_target="tpu_custom_call" | custom-call | tf_op jit(solution)/shard_map/pallas_call | solution.py:218
  609.3 1.5 slice_reduce_fusion.4
  611.7 18.4 %multiply_add_fusion = (f32[18,96,768]{2,1,0:T(8,128)}, f32[18,96,768]{2,1,0:T(8,128)}, f32[18,96,768]{2,1,0:T(8,128)}, f32[18,96,768]{2,1,0:T(8,128)}) fusion(f32[18,96,768]{2,1,0:T(8,128)} %param.21, f32[18,96,768]{2,1,0:T(8,128)} %param.18, f32[18,96,768]{2,1,0:T(8,128)} %copy-done, f32[]{:T(128)S(6)} %div.102, f32[18,96,768]{2,1,0:T(8,128)} %param.19, ...), kind=kLoop, calls=%fused_computation.2 | loop fusion | flops 25214976 | bytes 47775748 | tf_op jit(solution)/shard_map/add | solution.py:1028
  (126 shorter events, 26.6 us)
Async XLA Ops:
  0.6 4.4 copy-start.5
  0.7 4.7 copy-start.3
  5.1 129.1 %copy-start.1 = (bf16[1,8,196,768]{3,1,2,0:T(8,128)(2,1)S(1)}, bf16[1,8,196,768]{3,1,2,0:T(8,128)(2,1)}, u32[]{:S(2)}) copy-start(bf16[1,8,196,768]{3,1,2,0:T(8,128)(2,1)} %param.15) | copy-start | bytes 7225348
  140.9 15.5 %copy-start.15 = (s32[1,8,196]{2,1,0:T(8,128)S(1)}, s32[1,8,196]{2,1,0:T(8,128)}, u32[]{:S(2)}) copy-start(s32[1,8,196]{2,1,0:T(8,128)} %param.16) | copy-start | bytes 18820
  205.8 60.0 %copy-start.16 = (s32[32]{0:T(128)S(1)}, s32[32]{0:T(128)}, u32[]{:S(2)}) copy-start(s32[32]{0:T(128)} %param.17) | copy-start | bytes 388
  346.4 130.5 %copy-start.14 = (f32[16,768]{1,0:T(8,128)S(1)}, f32[16,768]{1,0:T(8,128)}, u32[]{:S(2)}) copy-start(f32[16,768]{1,0:T(8,128)} %get-tuple-element.94) | copy-start | bytes 147460
  587.0 2.6 copy-start.2
  589.3 4.9 copy-start.7
  589.8 2.4 copy-start
  611.6 18.5 %copy-start.4 = (f32[96,256]{1,0:T(8,128)S(1)}, f32[96,256]{1,0:T(8,128)}, u32[]{:S(2)}) copy-start(f32[96,256]{1,0:T(8,128)} %param.22) | copy-start | bytes 294916
  611.6 18.5 %copy-start.8 = (f32[96,256]{1,0:T(8,128)S(1)}, f32[96,256]{1,0:T(8,128)}, u32[]{:S(2)}) copy-start(f32[96,256]{1,0:T(8,128)} %param.25) | copy-start | bytes 294916
  611.6 18.5 %copy-start.9 = (f32[96,256]{1,0:T(8,128)S(1)}, f32[96,256]{1,0:T(8,128)}, u32[]{:S(2)}) copy-start(f32[96,256]{1,0:T(8,128)} %param.23) | copy-start | bytes 294916
  611.6 18.5 %copy-start.10 = (f32[96,256]{1,0:T(8,128)S(1)}, f32[96,256]{1,0:T(8,128)}, u32[]{:S(2)}) copy-start(f32[96,256]{1,0:T(8,128)} %param.24) | copy-start | bytes 294916
  611.7 19.3 %copy-start.6 = (f32[227,96]{0,1:T(8,128)S(1)}, f32[227,96]{0,1:T(8,128)}, u32[]{:S(2)}) copy-start(f32[227,96]{0,1:T(8,128)} %param.26) | copy-start | bytes 261508
  611.7 19.3 %copy-start.11 = (f32[227,96]{0,1:T(8,128)S(1)}, f32[227,96]{0,1:T(8,128)}, u32[]{:S(2)}) copy-start(f32[227,96]{0,1:T(8,128)} %param.29) | copy-start | bytes 261508
  611.7 19.2 %copy-start.12 = (f32[227,96]{0,1:T(8,128)S(1)}, f32[227,96]{0,1:T(8,128)}, u32[]{:S(2)}) copy-start(f32[227,96]{0,1:T(8,128)} %param.27) | copy-start | bytes 261508
  611.7 19.2 %copy-start.13 = (f32[227,96]{0,1:T(8,128)S(1)}, f32[227,96]{0,1:T(8,128)}, u32[]{:S(2)}) copy-start(f32[227,96]{0,1:T(8,128)} %param.28) | copy-start | bytes 261508

commit v4 on v3

--- a/solution.py
+++ b/solution.py
@@ -69,117 +69,6 @@
     for other in others:
         pl.semaphore_signal(barrier, inc=1, device_id=other, device_id_type=MESH)
     pl.semaphore_wait(barrier, len(others))
-
-
-def gather_kernel(lay, w_ref, s_ref, ow_ref, os_ref, own_sem, zs, zr, xs, xr, ys, yr, cs, cr, small):
-    i, a, b, y, c = lay.place()
-    A, B = lay.outer, lay.inner
-    greet(lay, i, a, b, y, c)
-    pending = []
-
-    def remote(src, dst, ssem, rsem, dev):
-        copy = pltpu.make_async_remote_copy(
-            src_ref=src, dst_ref=dst, send_sem=ssem, recv_sem=rsem, device_id=dev, device_id_type=MESH
-        )
-        copy.start()
-        pending.append(copy)
-        return copy
-
-    def landed(dst, ssem, rsem, dev):
-        pltpu.make_async_remote_copy(
-            src_ref=dst, dst_ref=dst, send_sem=ssem, recv_sem=rsem, device_id=dev, device_id_type=MESH
-        ).wait_recv()
-
-    K = lay.handled
-    here = lay.peer(i, y, 1 - c)
-    local_small = pltpu.make_async_copy(s_ref, os_ref.at[i], own_sem.at[0])
-    local_small.start()
-    for k in [-1] + list(range(lay.common, K)) + list(range(lay.common)):
-        src = s_ref if k < 0 else w_ref.at[lay.matrix(c, y, k)]
-        dst = os_ref.at[i] if k < 0 else ow_ref.at[lay.matrix(c, y, k), i]
-        for t in range(1, A):
-            remote(src, dst, zs.at[k + 1, t], zr.at[k + 1, t], lay.peer(turn(a, t, A) * B + b, y, c))
-        for u in range(1, B):
-            remote(src, dst, xs.at[k + 1, u, 0], xr.at[k + 1, u, 0], lay.peer(a * B + turn(b, u, B), y, c))
-    locals_ = []
-    for first, count in ((lay.matrix(c, y, 0), lay.common), (lay.matrix(c, y, lay.common), lay.split)):
-        if count:
-            span = pl.ds(first, count)
-            locals_.append(pltpu.make_async_copy(w_ref.at[span], ow_ref.at[span, i], own_sem.at[1 + len(locals_)]))
-            locals_[-1].start()
-    order = [-1] + list(range(lay.common, K)) + list(range(lay.common))
-
-    def at(k, j):
-        return os_ref.at[j] if k < 0 else ow_ref.at[lay.matrix(c, y, k), j]
-
-    def cross(k):
-        for t in range(1, A):
-            j = turn(a, -t, A) * B + b
-            landed(at(k, j), zs.at[k + 1, t], zr.at[k + 1, t], here)
-            for u in range(1, B):
-                remote(at(k, j), at(k, j), xs.at[k + 1, u, t], xr.at[k + 1, u, t], lay.peer(a * B + turn(b, u, B), y, c))
-
-    def share(k):
-        for u in range(1, B):
-            for t in range(A):
-                j = turn(a, -t, A) * B + turn(b, -u, B)
-                landed(at(k, j), xs.at[k + 1, u, t], xr.at[k + 1, u, t], here)
-        if k >= 0:
-            m = lay.matrix(c, y, k)
-            if k >= lay.common:
-                for v in range(1, lay.planes):
-                    q = k - lay.common
-                    remote(ow_ref.at[m], ow_ref.at[m], ys.at[q, v], yr.at[q, v], lay.peer(i, turn(y, v, lay.planes), c))
-            remote(ow_ref.at[m], ow_ref.at[m], cs.at[k], cr.at[k], here)
-
-    for step in range(len(order) + 1):
-        if step < len(order):
-            cross(order[step])
-        if step == 2:
-            for local in locals_:
-                local.wait()
-        if step >= 1:
-            share(order[step - 1])
-    slot = K
-    for v in range(1, lay.planes):
-        for q in range(lay.split):
-            m = lay.matrix(c, turn(y, -v, lay.planes), lay.common + q)
-            landed(ow_ref.at[m], ys.at[q, v], yr.at[q, v], here)
-            remote(ow_ref.at[m], ow_ref.at[m], cs.at[slot], cr.at[slot], here)
-            slot += 1
-    slot = K
-    for k in range(K):
-        m = lay.matrix(1 - c, y, k)
-        landed(ow_ref.at[m], cs.at[k], cr.at[k], here)
-    for v in range(1, lay.planes):
-        for q in range(lay.split):
-            m = lay.matrix(1 - c, turn(y, -v, lay.planes), lay.common + q)
-            landed(ow_ref.at[m], cs.at[slot], cr.at[slot], here)
-            slot += 1
-    local_small.wait()
-    for copy in pending:
-        copy.wait_send()
-
-
-def gather(lay, shard, small):
-    A, B, K = lay.outer, lay.inner, lay.handled
-    dma = pltpu.SemaphoreType.DMA
-    kept = max(lay.split, 1)
-    return pl.pallas_call(
-        functools.partial(gather_kernel, lay),
-        out_shape=(
-            jax.ShapeDtypeStruct((NMAT, lay.n) + shard.shape[1:], shard.dtype),
-            jax.ShapeDtypeStruct((lay.n,) + small.shape, small.dtype),
-        ),
-        in_specs=[ANY, ANY],
-        out_specs=(ANY, ANY),
-        scratch_shapes=[
-            dma((3,)), dma((K + 1, A)), dma((K + 1, A)), dma((K + 1, B, A)), dma((K + 1, B, A)),
-            dma((kept, lay.planes)), dma((kept, lay.planes)), dma((lay.half,)), dma((lay.half,)),
-            dma((1,)),
-        ],
-        compiler_params=pltpu.CompilerParams(collective_id=0, has_side_effects=True),
-    )(shard, small)
 
 
 def spread_kernel(dp, n, x_ref, o_ref, ssem, rsem):
@@ -576,7 +465,7 @@
         pltpu.VMEM((K, along, rows, D), HALF), pltpu.VMEM((K, along, rows, D), HALF),
         pltpu.VMEM((K, rows, D), FULL), pltpu.VMEM((Y, common, rows, D), FULL),
         dma((slots,)), dma((slots,)), dma((passed, kept)), dma((passed, kept)),
-        dma((K, crossed)), dma((K, crossed)), dma((K, along)), dma((K, along)), dma((5, K, Y)),
+        dma((K, crossed, A)), dma((K, crossed, A)), dma((K, along)), dma((K, along)), dma((5, K, Y)),
     ]
 
 
@@ -647,38 +536,34 @@
         if v == 0:
             for w in range(1, self.lay.planes):
                 self.landed(st.yr.at[w - 1, q], st.yrs, w - 1, q)
-        for u in range(1, self.lay.inner):
-            other = turn(self.b, u, self.lay.inner)
-
-            @pl.loop(0, self.lay.outer)
-            def _(e):
-                st.xs[k, u - 1, e] = self.base(st, v, q, e * self.lay.inner + other).astype(HALF)
-
-            self.remote(
-                st.xs.at[k, u - 1], st.xr.at[k, u - 1], st.xss, (k, u - 1), (st.xrs, (k, u - 1)),
-                self.lay.peer(self.a * self.lay.inner + other, self.y, self.c), lambda u=u: st.xs.at[k, u - 1],
-            )
+        outer, inner = self.lay.outer, self.lay.inner
+        for t in list(range(1, outer)) + [0]:
+            e = turn(self.a, t, outer)
+            for u in range(1, inner):
+                other = turn(self.b, u, inner)
+                st.xs[k, u - 1, e] = self.base(st, v, q, e * inner + other).astype(HALF)
+                self.remote(
+                    st.xs.at[k, u - 1, e], st.xr.at[k, u - 1, e], st.xss, (k, u - 1, t), (st.xrs, (k, u - 1, t)),
+                    self.lay.peer(self.a * inner + other, self.y, self.c), lambda u=u: st.xs.at[k, u - 1, 0],
+                )
 
     def along(self, st, target, v, q):
         k = self.item(st, v, q)
         inner, outer = self.lay.inner, self.lay.outer
-        for u in range(1, inner):
-            self.landed(st.xr.at[k, u - 1], st.xrs, k, u - 1)
-
-        def total(e):
+        for t in list(range(1, outer)) + [0]:
+            e = turn(self.a, t, outer)
             value = self.base(st, v, q, e * inner + self.b)
             for u in range(1, inner):
+                self.landed(st.xr.at[k, u - 1, e], st.xrs, k, u - 1, t)
                 value = value + st.xr[k, u - 1, e].astype(FULL)
-            return value
-
-        for t in range(1, outer):
-            e = turn(self.a, t, outer)
-            st.zs[k, t - 1] = total(e).astype(HALF)
+            if t == 0:
+                st.fin[k] = value
+                continue
+            st.zs[k, t - 1] = value.astype(HALF)
             self.remote(
                 st.zs.at[k, t - 1], st.zr.at[k, t - 1], st.zss, (k, t - 1), (st.zrs, (k, t - 1)),
                 self.lay.peer(e * inner + self.b, self.y, self.c), lambda t=t: st.zs.at[k, t - 1],
             )
-        st.fin[k] = total(self.a)
 
     def close(self, st, target, v, q):
         k, Y = self.item(st, v, q), self.lay.planes
@@ -832,8 +717,8 @@
 
     def space(dq, dk, dv, xs, d2, fq, fk, fv, d1, r1, dy, do):
         space_back_kernel(dq, dk, dv, cls_ref, xs, d2, ws[3], ws[4], ws[5], ws[6], ws[7], v_ref, fq, fk, fv, d1, r1, dy, do, sum2_ref)
-        for s in range(steps):
-            @pl.when(pl.program_id(0) == s)
+        for s, place in enumerate((1, 3)):
+            @pl.when(pl.program_id(0) == place)
             def _():
                 red.progress(work, begun + s)
 
@@ -844,22 +729,26 @@
     def time(q, k, v, d, fill, dq, dk, dv):
         time_back_kernel(q, k, v, d, fill, dq, dk, dv)
 
-        @pl.when(pl.program_id(0) == 6)
-        def _():
-            red.progress(work, begun + steps)
+        for s, place in enumerate((6, 12)):
+            @pl.when(pl.program_id(0) == place)
+            def _():
+                red.progress(work, begun + 2 + s)
 
     pltpu.emit_pipeline(time, grid=(SP // GROUP,), in_specs=[SLAB] * 4 + [FILL], out_specs=[SLAB] * 3)(
         qt_ref, kt_ref, vt_ref, do_ref, fill_ref, tq_ref, tk_ref, tv_ref
     )
-    red.progress(work, begun + steps + 1)
 
     def embed(dq, dk, dv, x, d1, r, time):
         embed_back_kernel(dq, dk, dv, x, d1, ws[0], ws[1], ws[2], v_ref, r, pos_ref, time, sum3_ref)
 
+        @pl.when(pl.program_id(0) == 3)
+        def _():
+            red.progress(work, begun + 4)
+
     pltpu.emit_pipeline(embed, grid=(steps,), in_specs=[FRAMES] * 5, out_specs=[FRAMES, per_frame(1, D)])(
         tq_ref, tk_ref, tv_ref, x0_ref, d1_ref, rp_ref, time_ref
     )
-    for s in range(begun + steps + 2, len(work) + 3):
+    for s in range(begun + 5, len(work) + 3):
         red.progress(work, s)
     red.done(work)
 
@@ -920,7 +809,234 @@
     )(small, *[x.reshape(-1, D) for x in arrays])
 
 
-def forward(mats, table, patches, mask):
+def front_kernel(lay, w_ref, s_ref, p_ref, tfill_ref, sfill_ref, *refs):
+    (ow_ref, os_ref, pad_ref, x0_ref, at_ref, qt_ref, kt_ref, vt_ref, ot_ref, yt_ref, xs_ref, as_ref, qs_ref, ks_ref, vs_ref, mix_ref, cls_ref, v_ref) = refs[:18]
+    (w_buf, piece, pos_buf, time_buf, own, zs, zr, xs, xr, ys, yr, cs, cr, wsem) = refs[18:]
+    i, a, b, y, c = lay.place()
+    A, B, Y, K = lay.outer, lay.inner, lay.planes, lay.handled
+    greet(lay, i, a, b, y, c)
+    here = lay.peer(i, y, 1 - c)
+    pending = []
+
+    def remote(src, dst, sends, at, recvs, dev, like):
+        pltpu.make_async_remote_copy(
+            src_ref=src, dst_ref=dst, send_sem=sends.at[at], recv_sem=recvs.at[at], device_id=dev, device_id_type=MESH
+        ).start()
+        pending.append((like, sends, at))
+
+    def landed(dst, sems, *at):
+        pltpu.make_async_remote_copy(
+            src_ref=dst, dst_ref=dst, send_sem=sems.at[at], recv_sem=sems.at[at], device_id=here, device_id_type=MESH
+        ).wait_recv()
+
+    def matrix_of(core, k, v=0):
+        h = k if k < lay.common else lay.common + turn(y, v, Y) * lay.split + (k - lay.common)
+        return 2 * h + core
+
+    def source(k):
+        return s_ref.at[c] if k < 0 else w_ref.at[matrix_of(c, k)]
+
+    def at(k, j):
+        return os_ref.at[c, j] if k < 0 else ow_ref.at[matrix_of(c, k), j]
+
+    def like(k):
+        return (lambda: s_ref.at[0]) if k < 0 else (lambda: w_ref.at[0])
+
+    order = [-1] + list(range(K))
+
+    def local(k):
+        if k < 0:
+            return pltpu.make_async_copy(s_ref.at[c], os_ref.at[c, i], own.at[0])
+        m = 2 * k + c
+        return pltpu.make_async_copy(w_ref.at[m], ow_ref.at[m, i], own.at[k + 1])
+
+    for k in order:
+        for t in range(1, A):
+            remote(source(k), at(k, i), zs, (k + 1, t), zr, lay.peer(turn(a, t, A) * B + b, y, c), like(k))
+    for k in range(-1, lay.half):
+        local(k).start()
+
+    def over(k, j, t, u):
+        if k >= lay.common:
+            for v in range(1, Y):
+                remote(at(k, j), at(k, j), ys, (k - lay.common, v, t, u), yr, lay.peer(i, turn(y, v, Y), c), like(k))
+
+    def cross(k):
+        for u in range(1, B):
+            remote(source(k), at(k, i), xs, (k + 1, u, 0), xr, lay.peer(a * B + turn(b, u, B), y, c), like(k))
+        for t in range(1, A):
+            j = turn(a, -t, A) * B + b
+            landed(at(k, j), zr, k + 1, t)
+            for u in range(1, B):
+                remote(at(k, j), at(k, j), xs, (k + 1, u, t), xr, lay.peer(a * B + turn(b, u, B), y, c), like(k))
+            over(k, j, t, 0)
+
+    def share(k):
+        for t in range(A):
+            for u in range(1, B):
+                j = turn(a, -t, A) * B + turn(b, -u, B)
+                landed(at(k, j), xr, k + 1, u, t)
+                over(k, j, t, u)
+        if k < 0:
+            local(k).wait()
+            remote(os_ref.at[c], os_ref.at[c], cs, (0,), cr, here, lambda: os_ref.at[0])
+        else:
+            if k < lay.common:
+                local(k).wait()
+            else:
+                own_wait(k, 0)
+            m = matrix_of(c, k)
+            remote(ow_ref.at[m], ow_ref.at[m], cs, (k + 1,), cr, here, lambda: ow_ref.at[0])
+
+    def own_wait(k, v):
+        m = matrix_of(c, k, v)
+        pltpu.make_async_copy(w_ref.at[m], ow_ref.at[m, i], own.at[lax.div(m, 2) + 1]).wait()
+
+    def slot(q, v):
+        return K + 1 + (v - 1) * lay.split + q
+
+    def from_planes():
+        for v in range(1, Y):
+            for q in range(lay.split):
+                k = lay.common + q
+                m = matrix_of(c, k, -v)
+                for t in range(A):
+                    for u in range(B):
+                        if t or u:
+                            j = turn(a, -t, A) * B + turn(b, -u, B)
+                            landed(ow_ref.at[m, j], yr, q, v, t, u)
+                own_wait(k, -v)
+                remote(ow_ref.at[m], ow_ref.at[m], cs, (slot(q, v),), cr, here, lambda: ow_ref.at[0])
+
+    def paired(k, v=0):
+        if k < 0:
+            landed(os_ref.at[1 - c], cr, 0)
+        else:
+            landed(ow_ref.at[matrix_of(1 - c, k, v)], cr, k + 1 if v == 0 else slot(k - lay.common, -v))
+
+    def fetch(first, count):
+        span = pl.ds(first, count)
+        return pltpu.make_async_copy(ow_ref.at[span], w_buf.at[span], wsem.at[first])
+
+    begun = 0
+    for step in range(4):
+        cross(order[step])
+        if step:
+            share(order[step - 1])
+        begun = step + 1
+    paired(-1)
+    paired(0)
+    paired(1)
+    fetch(0, 4).start()
+    table = pltpu.make_async_copy(os_ref.at[0], piece, wsem.at[lay.half])
+    table.start()
+    v_ref[...] = jnp.zeros_like(v_ref)
+    table.wait()
+    for j in range(lay.n):
+        lane = min(lay.rows * j // 128 * 128, D - 256)
+        v_ref[: piece.shape[1], lane : lane + 256] += piece[j].astype(FULL)
+    pos_buf[...] = v_ref[31 : 31 + SP, :]
+    for f in range(F):
+        time_buf[f] = v_ref[1 + f : 2 + f, :]
+    fetch(0, 4).wait()
+    ws = [Weight(w_buf.at[k]) for k in range(9)]
+    steps = F // FB
+
+    def advance(step):
+        if step < len(order):
+            cross(order[step])
+        if step - 1 < len(order):
+            share(order[step - 1])
+
+    def embed(p, *outs):
+        now = pl.program_id(0)
+        embed_kernel(p, *ws[:4], v_ref, pos_buf, time_buf.at[pl.ds(now * FB, FB)], *outs)
+        for s, place in enumerate((1, 3)):
+            @pl.when(now == place)
+            def _():
+                advance(begun + s)
+
+    pltpu.emit_pipeline(embed, grid=(steps,), in_specs=[pl.BlockSpec((1, FB, S, D), lambda i: (0, i, 0, 0))], out_specs=[FRAMES] * 6)(
+        p_ref, pad_ref, x0_ref, at_ref, qt_ref, kt_ref, vt_ref
+    )
+
+    def time(q, k, v, fill, o):
+        time_kernel(q, k, v, fill, o)
+        for s, place in enumerate((5, 11)):
+            @pl.when(pl.program_id(0) == place)
+            def _():
+                advance(begun + 2 + s)
+
+    pltpu.emit_pipeline(time, grid=(SP // GROUP,), in_specs=[SLAB] * 3 + [FILL], out_specs=[SLAB])(
+        qt_ref, kt_ref, vt_ref, tfill_ref, ot_ref
+    )
+    for k in range(2, 5):
+        paired(k)
+    fetch(4, 5).start()
+    fetch(4, 5).wait()
+
+    def space(o, x, fill, *outs):
+        space_kernel(o, x, *ws[4:9], v_ref, fill, *outs)
+
+        @pl.when(pl.program_id(0) == 0)
+        def _():
+            advance(begun + 4)
+
+    pltpu.emit_pipeline(space, grid=(steps,), in_specs=[FRAMES, FRAMES, per_frame(1, SP)], out_specs=[FRAMES] * 7 + [per_frame(8, D)])(
+        ot_ref, x0_ref, sfill_ref, yt_ref, xs_ref, as_ref, qs_ref, ks_ref, vs_ref, mix_ref, cls_ref
+    )
+    for step in range(begun + 5, len(order) + 1):
+        advance(step)
+    from_planes()
+    for k in range(5, K):
+        paired(k)
+    for v in range(1, Y):
+        for q in range(lay.split):
+            paired(lay.common + q, -v)
+    for make, sems, at_ in pending:
+        ref = make()
+        pltpu.make_async_remote_copy(
+            src_ref=ref, dst_ref=ref, send_sem=sems.at[at_], recv_sem=sems.at[at_], device_id=here, device_id_type=MESH
+        ).wait_send()
+
+
+class Weight:
+    def __init__(self, ref):
+        self.ref = ref
+
+    def __getitem__(self, unused):
+        value = self.ref[...]
+        if value.shape[1] % 16:
+            return value.astype(FULL).reshape(D, D).astype(HALF)
+        return value.reshape(D, D)
+
+
+def front(lay, shard, small, patches, time_fill, space_fill):
+    A, B, K, Y = lay.outer, lay.inner, lay.handled, lay.planes
+    dma = pltpu.SemaphoreType.DMA
+    kept = max(lay.split, 1)
+    vmem = pl.BlockSpec(memory_space=pltpu.VMEM)
+    full = functools.partial(shape, dtype=FULL)
+    slots = K + 1 + max(Y - 1, 0) * lay.split
+    return pl.pallas_call(
+        functools.partial(front_kernel, lay),
+        in_specs=[ANY] * 5,
+        out_specs=[ANY] * 17 + [vmem],
+        out_shape=[
+            shape(NMAT, lay.n, lay.rows, D), shape(2, lay.n, *small.shape[1:]),
+            ROWS16, ROWS32, ROWS16, ROWS16, ROWS16, ROWS16, ROWS16, ROWS16, ROWS32, ROWS16, ROWS16, ROWS16, ROWS16, ROWS16,
+            full(F, 8, D), full(256, D),
+        ],
+        scratch_shapes=[
+            pltpu.VMEM((9, lay.n, lay.rows, D), HALF), pltpu.VMEM((lay.n,) + small.shape[1:], HALF), pltpu.VMEM((SP, D), FULL), pltpu.VMEM((F, 1, D), FULL),
+            dma((lay.half + 1,)), dma((K + 1, A)), dma((K + 1, A)), dma((K + 1, B, A)), dma((K + 1, B, A)),
+            dma((kept, Y, A, B)), dma((kept, Y, A, B)), dma((slots,)), dma((slots,)), dma((lay.half + 1,)),
+        ],
+        compiler_params=pltpu.CompilerParams(collective_id=0, has_side_effects=True, vmem_limit_bytes=60 * 2**20),
+    )(shard, small, patches, time_fill, space_fill)
+
+
+def forward(lay, shard, small, patches, mask):
     alive = jnp.pad(mask[0] > 0, ((0, 0), (0, SP - S)))
     kept = jnp.where(alive, 0.0, MASKED).astype(FULL)
     places = jnp.arange(SP)[None]
@@ -930,25 +1046,14 @@
     same = spot[:, None] == spot[None]
     time_fill = jnp.where(same[None], time_keys[:, None, :], NEVER)
     time_fill_back = jnp.where(same[None], time_keys[:, :, None], NEVER)
-    table = jnp.pad(table, ((0, -table.shape[0] % 8), (0, 0)))
-    pos = jnp.pad(table[31 : 31 + S], ((0, SP - S), (0, 0)))
-    time = table[1 : 1 + F][:, None]
     one = jnp.where(places[0] < S, 1.0, jnp.where(places[0] == S, 1.0 / F, 0.0)).astype(FULL)
     share = jnp.broadcast_to(jnp.tile(one, FB)[:, None], (FB * SP, 1))
+    mats, rest, padded, x0, at, qt, kt, vt, ot, yt, xs, as_, qs, ks, vs, os_, cls, table = front(
+        lay, shard, small, patches, time_fill, space_fill[:, None]
+    )
+    mats = mats.reshape(NMAT, D, D)
     tab = whole(*table.shape)
     steps = F // FB
-    padded, x0, at, qt, kt, vt = call(
-        embed_kernel, steps,
-        [pl.BlockSpec((1, FB, S, D), lambda i: (0, i, 0, 0))] + matrices(0, 4) + [tab, whole(SP, D), per_frame(1, D)],
-        [FRAMES] * 6, [ROWS16, ROWS32] + [ROWS16] * 4,
-    )(patches, *[mats] * 4, table, pos, time)
-    ot = call(
-        time_kernel, SP // GROUP, [SLAB] * 3 + [pl.BlockSpec((1, F * GROUP, F * GROUP), lambda i: (i, 0, 0))], SLAB, ROWS16,
-    )(qt, kt, vt, time_fill)
-    yt, xs, as_, qs, ks, vs, os_, cls = call(
-        space_kernel, steps, [FRAMES, FRAMES] + matrices(4, 5) + [tab, per_frame(1, SP)],
-        [FRAMES] * 7 + [per_frame(8, D)], [ROWS16, ROWS32] + [ROWS16] * 5 + [shape(F, 8, D, dtype=FULL)],
-    )(ot, x0, *[mats] * 5, table, space_fill[:, None])
     cls = jnp.mean(cls[:, 0], 0, keepdims=True)
     of, x2, a2, g, e, x3, pool = call(
         mlp_kernel, steps,
@@ -957,8 +1062,9 @@
         [ROWS16, ROWS32, ROWS16, HIDDEN32, HIDDEN16, ROWS32, shape(8, D, dtype=FULL)],
     )(os_, cls, xs, *[mats] * 9, table, share)
     pooled = (pool[:1] / (F * S + 1)).astype(HALF)
+    head = rest[1][:, : lay.rows].reshape(D, -1)
     saved = (table, share, space_fill, time_fill_back, padded, x0, at, qt, kt, vt, ot, yt, xs, as_, qs, ks, vs, of, x2, a2, g, e, x3)
-    return pooled, saved
+    return pooled, mats, head, saved
 
 
 def backward(lay, mats, saved, back_pooled):
@@ -1029,21 +1135,12 @@
     return (weight, first, second, average)
 
 
-def pack(head, vecs):
-    rows = head.shape[0] // 3
-    first = jnp.concatenate([head[:rows], head[rows : 2 * rows], head[2 * rows :]], 1)
-    tall = jnp.pad(vecs, ((0, D // 3 - vecs.shape[0]), (0, 0)))
-    second = tall.reshape(D // head.shape[0], rows, head.shape[0]).transpose(1, 0, 2).reshape(rows, D)
-    fill = -rows % 16
-    return jnp.pad(jnp.stack([first, second]), ((0, 0), (0, fill), (0, 0)))
-
-
-def unpack(blocks, rows):
-    n = blocks.shape[0]
-    kept = blocks[:, :, : rows // 3]
-    head = kept[:, 0].reshape(n, rows // 3, 3, D // 3).transpose(0, 2, 1, 3).reshape(D, D // 3)
-    vecs = kept[:, 1].reshape(n, rows // 3, n, rows).transpose(2, 1, 0, 3).reshape(D // 3, D)
-    return head, vecs[:NVEC]
+def pack(lay, head, vecs):
+    first = lay.rows * lax.axis_index("fsdp")
+    lane = first - jnp.minimum(first // 128 * 128, D - 256)
+    tall = -(-NVEC // 16) * 16
+    moved = lax.dynamic_update_slice(jnp.zeros((tall, 256), HALF), vecs, (0, lane))
+    return jnp.stack([moved, jnp.pad(head, ((0, tall - head.shape[0]), (0, 0)))])
 
 
 def pack_all(head, vecs, n):
@@ -1082,14 +1179,13 @@
     vector_average,
 ):
     n = lay.n
-    gathered_mats, gathered_small = gather(
+    pooled, mats16, head16, saved = forward(
         lay,
         matrices.astype(jnp.bfloat16),
-        pack(head_weight.astype(jnp.bfloat16), vectors.astype(jnp.bfloat16)),
-    )
-    mats16 = gathered_mats.reshape(NMAT, D, D)
-    head16, vecs16 = unpack(gathered_small, lay.rows)
-    pooled, saved = forward(mats16, vecs16.astype(jnp.float32), patches, patch_keep_mask)
+        pack(lay, head_weight.astype(jnp.bfloat16), vectors.astype(jnp.bfloat16)),
+        patches,
+        patch_keep_mask,
+    )
     projected = project(pooled, head16)
     unit_length_lines, unit_back = jax.vjp(normalize, projected)
     clip_count, width = unit_length_lines.shape
@@ -1160,7 +1256,8 @@
 
 
 def solution(mesh):
-    lay = Layout(mesh.shape["dp"], mesh.shape["fsdp"], 2)
+    planes = mesh.shape["dp"] // 2
+    lay = Layout(mesh.shape["dp"], mesh.shape["fsdp"], 2 if planes == 2 else 0)
     placed = (
         P(("dp", "fsdp"), None, None, None),
         P(("dp", "fsdp"), None, None),

time: 639 us -> 599 us (0.937)
  Pallas kernels: 557 us -> 517 us
    pallas_call x1, Pallas kernels: 127 us -> 105 us  [early(): pl.pallas_call(functools.partial(early_kernel, lay, part, pairs), in_spec...]
    pallas_call x4 -> x1, Pallas kernels: 186 us -> 166 us  [front(): pl.pallas_call(functools.partial(front_kernel, lay), in_specs=[ANY] * 5,...]
where the time goes in v4:
time: 599 us; the launch traced here: 589 us
  Pallas kernels  517 us (86%)
  other arithmetic  41.5 us (7%)
  local copies, waits for them, and re-layouts  20.8 us (3%)
  between operations  8.47 us (1%)
    pallas_call x1, Pallas kernels, front(): pl.pallas_call(functools.partial(front_kernel, lay), in_specs=[ANY] * 5,...  166 us
    pallas_call x1, Pallas kernels, early(): pl.pallas_call(functools.partial(early_kernel, lay, part, pairs), in_spec...  105 us
    pallas_call x1, Pallas kernels, late(): pl.pallas_call(functools.partial(late_kernel, lay, part, pairs, len(array...  102 us
    pallas_call x1, Pallas kernels, backward(): call(mlp_back_kernel, steps, [FRAMES, FRAMES, HIDDEN, whole(1, D)] + matr...  72.8 us
    pallas_call x1, Pallas kernels, forward(): call(mlp_kernel, steps, [FRAMES, whole(1, D), FRAMES] + matrices(9, 9) +...  42.2 us
    pallas_call x2, Pallas kernels, spread(): pl.pallas_call(functools.partial(spread_kernel, dp, n), out_shape=jax.Sha...  29.7 us
    add x3, other arithmetic, adamw_step(): average = AVERAGE_KEEP * average + (1.0 - AVERAGE_KEEP) * weight  19.9 us

profile of v4, /device:TPU:0, one launch (start us, length us, event | category | flops | bytes accessed | tf_op | source)
XLA Modules:
  0.0 589.4 jit_solution(1185568922751764741)
XLA Ops:
  0.7 4.5 convert_element_type.28.w_ref
  6.9 1.9 copy.76.p_ref
  9.1 1.5 broadcast_select_fusion
  11.2 165.7 %shard_map.254 = (bf16[18,8,96,768]{3,2,1,0:T(8,128)(2,1)}, bf16[2,8,240,256]{3,2,1,0:T(8,128)(2,1)}, bf16[8,208,768]{2,1,0:T(8,128)(2,1)}, f32[8,208,768]{2,1,0...) custom-call(bf16[18,96,768]{2,1,0:T(8,128)(2,1)} %convert_element_ty, ...), custom_call_target="tpu_custom_call" | custom-call | tf_op jit(solution)/shard_map/pallas_call | solution.py:1021
  177.0 1.3 slice_bitcast_fusion
  178.3 1.0 slice_reduce_fusion.3
  180.7 42.2 %shard_map.255 = (bf16[8,208,768]{2,1,0:T(8,128)(2,1)}, f32[8,208,768]{2,1,0:T(8,128)}, bf16[8,208,768]{2,1,0:T(8,128)(2,1)}, f32[4,8,208,768]{3,2,1,0:T(8,128)}...) custom-call(bf16[8,208,768]{2,1,0:T(8,128)(2,1)} %get-tuple-element.66.o_ref, ...), custom_call_target="tpu_custom_call" | custom-call | tf_op jit(solution)/shard_map/pallas_call | solution.py:1058
  225.8 18.5 %shard_map.256 = f32[32,8,128]{2,1,0:T(8,128)} custom-call(f32[8,128]{1,0:T(8,128)} %pad.19.x_ref), custom_call_target="tpu_custom_call" | custom-call | tf_op jit(solution)/shard_map/pallas_call | solution.py:107
  244.2 0.9 slice.104
  249.3 1.2 broadcast_in_dim.168.fill_ref
  250.4 72.8 %shard_map.257 = (bf16[8,208,768]{2,1,0:T(8,128)(2,1)}, bf16[4,8,208,768]{3,2,1,0:T(8,128)(2,1)}, f32[8,208,768]{2,1,0:T(8,128)}, bf16[8,208,768]{2,1,0:T(8,128)...) custom-call(f32[8,208,768]{2,1,0:T(8,128)} %get-tuple-element.74.x3_, ...), custom_call_target="tpu_custom_call" | custom-call | tf_op jit(solution)/shard_map/pallas_call | solution.py:1076
  323.3 1.1 slice_reduce_fusion
  324.4 1.0 slice_reduce_fusion.2
  326.0 104.5 %shard_map.258 = (f32[8,96,768]{2,1,0:T(8,128)}, bf16[8,208,768]{2,1,0:T(8,128)(2,1)}, bf16[8,208,768]{2,1,0:T(8,128)(2,1)}, bf16[8,208,768]{2,1,0:T(8,128)(2,1)...) custom-call(bf16[6656,768]{1,0:T(8,128)(2,1)} %bitcast.94, ...), custom_call_target="tpu_custom_call" | custom-call | tf_op jit(solution)/shard_map/pallas_call | solution.py:764
  433.7 1.1 slice.162
  434.9 1.1 concatenate.15
  439.1 0.9 pad_maximum_fusion.refs_0_
  440.1 102.0 %shard_map.259 = (f32[10,96,768]{2,1,0:T(8,128)}, f32[2,32,768]{2,1,0:T(8,128)}) custom-call(bf16[2,8,32,768]{3,2,1,0:T(8,128)(2,1)} %pad_maximum_fusion.refs_0_, bf16[1664,768]{1,0:T(8,128)(2,1)} %bitcast.98, bf16[1664,768]{1,0:T(8,128)(2,1)} %bitcast.113, bf16[1664,768]{1,0:T(8,128)(2,1)} %bitcast.99, bf16[1664,768]{1,0:T(8,128)(2,1)} %bitcast.110, ...), custom_call_target="tpu_custom_call" | custom-call | tf_op jit(solution)/shard_map/pallas_call | solution.py:802
  542.1 2.3 constant_dynamic-update-slice_fusion.1
  545.0 2.4 copy-done
  547.3 2.0 multiply_reduce_fusion
  553.4 11.2 %shard_map.260 = f32[32,8,128]{2,1,0:T(8,128)} custom-call(f32[8,128]{1,0:T(8,128)} %broadcast_in_dim.173.x_ref), custom_call_target="tpu_custom_call" | custom-call | tf_op jit(solution)/shard_map/pallas_call | solution.py:107
  564.6 1.5 slice_reduce_fusion.4
  567.0 18.3 %multiply_add_fusion = (f32[18,96,768]{2,1,0:T(8,128)}, f32[18,96,768]{2,1,0:T(8,128)}, f32[18,96,768]{2,1,0:T(8,128)}, f32[18,96,768]{2,1,0:T(8,128)}) fusion(f32[18,96,768]{2,1,0:T(8,128)} %param.21, f32[18,96,768]{2,1,0:T(8,128)} %param.18, f32[18,96,768]{2,1,0:T(8,128)} %copy-done, f32[]{:T(128)S(6)} %div.113, f32[18,96,768]{2,1,0:T(8,128)} %param.19, ...), kind=kLoop, calls=%fused_computation.2 | loop fusion | flops 25214976 | bytes 47775748 | tf_op jit(solution)/shard_map/add | solution.py:1134
  (110 shorter events, 20.1 us)
Async XLA Ops:
  0.6 4.6 copy-start.3
  0.7 4.6 copy-start.5
  0.7 6.2 %copy-start.1 = (bf16[1,8,196,768]{3,1,2,0:T(8,128)(2,1)S(1)}, bf16[1,8,196,768]{3,1,2,0:T(8,128)(2,1)}, u32[]{:S(2)}) copy-start(bf16[1,8,196,768]{3,1,2,0:T(8,128)(2,1)} %param.15) | copy-start | bytes 7225348
  0.7 8.1 %copy-start.15 = (s32[1,8,196]{2,1,0:T(8,128)S(1)}, s32[1,8,196]{2,1,0:T(8,128)}, u32[]{:S(2)}) copy-start(s32[1,8,196]{2,1,0:T(8,128)} %param.16) | copy-start | bytes 18820
  180.7 64.6 %copy-start.16 = (s32[32]{0:T(128)S(1)}, s32[32]{0:T(128)}, u32[]{:S(2)}) copy-start(s32[32]{0:T(128)} %param.17) | copy-start | bytes 388
  326.0 107.7 %copy-start.14 = (f32[16,768]{1,0:T(8,128)S(1)}, f32[16,768]{1,0:T(8,128)}, u32[]{:S(2)}) copy-start(f32[16,768]{1,0:T(8,128)} %get-tuple-element.97) | copy-start | bytes 147460
  542.1 2.6 copy-start.2
  544.4 4.9 copy-start.7
  544.9 2.4 copy-start
  566.9 18.4 %copy-start.4 = (f32[96,256]{1,0:T(8,128)S(1)}, f32[96,256]{1,0:T(8,128)}, u32[]{:S(2)}) copy-start(f32[96,256]{1,0:T(8,128)} %param.22) | copy-start | bytes 294916
  566.9 18.4 %copy-start.8 = (f32[96,256]{1,0:T(8,128)S(1)}, f32[96,256]{1,0:T(8,128)}, u32[]{:S(2)}) copy-start(f32[96,256]{1,0:T(8,128)} %param.25) | copy-start | bytes 294916
  566.9 18.4 %copy-start.9 = (f32[96,256]{1,0:T(8,128)S(1)}, f32[96,256]{1,0:T(8,128)}, u32[]{:S(2)}) copy-start(f32[96,256]{1,0:T(8,128)} %param.23) | copy-start | bytes 294916
  566.9 18.4 %copy-start.10 = (f32[96,256]{1,0:T(8,128)S(1)}, f32[96,256]{1,0:T(8,128)}, u32[]{:S(2)}) copy-start(f32[96,256]{1,0:T(8,128)} %param.24) | copy-start | bytes 294916
  566.9 19.2 %copy-start.6 = (f32[227,96]{0,1:T(8,128)S(1)}, f32[227,96]{0,1:T(8,128)}, u32[]{:S(2)}) copy-start(f32[227,96]{0,1:T(8,128)} %param.26) | copy-start | bytes 261508
  566.9 19.2 %copy-start.11 = (f32[227,96]{0,1:T(8,128)S(1)}, f32[227,96]{0,1:T(8,128)}, u32[]{:S(2)}) copy-start(f32[227,96]{0,1:T(8,128)} %param.29) | copy-start | bytes 261508
  566.9 19.2 %copy-start.12 = (f32[227,96]{0,1:T(8,128)S(1)}, f32[227,96]{0,1:T(8,128)}, u32[]{:S(2)}) copy-start(f32[227,96]{0,1:T(8,128)} %param.27) | copy-start | bytes 261508
  567.0 19.2 %copy-start.13 = (f32[227,96]{0,1:T(8,128)S(1)}, f32[227,96]{0,1:T(8,128)}, u32[]{:S(2)}) copy-start(f32[227,96]{0,1:T(8,128)} %param.28) | copy-start | bytes 261508

commit v5 on v4

--- a/solution.py
+++ b/solution.py
@@ -163,12 +163,8 @@
 
 
 def gelu(x):
-    return x * normal_cdf(x)[0]
-
-
-def gelu_slope(x):
     below, bell = normal_cdf(x)
-    return below + x * bell * 0.3989422804014327
+    return x * below, below + x * bell * 0.3989422804014327
 
 
 def column_sum(x):
@@ -289,8 +285,9 @@
     x3 = x2 + v_ref[21:22]
     for k in range(4):
         g = dot(a, (u0, u1, u2, u3)[k][0]) + v_ref[17 + k : 18 + k]
-        g_ref[k] = g.reshape(FB, SP, D)
-        e = gelu(g).astype(HALF)
+        e, slope = gelu(g)
+        g_ref[k] = slope.reshape(FB, SP, D)
+        e = e.astype(HALF)
         e_ref[k] = e.reshape(FB, SP, D)
         x3 = x3 + dot(e, (e0, e1, e2, e3)[k][0])
     x3_ref[...] = x3.reshape(FB, SP, D)
@@ -308,7 +305,7 @@
     sums.append(column_sum(r3))
     back = None
     for k in range(4):
-        dg = (dot_back(r3, (e0, e1, e2, e3)[k][0]) * gelu_slope(flat(g_ref.at[k]))).astype(HALF)
+        dg = (dot_back(r3, (e0, e1, e2, e3)[k][0]) * flat(g_ref.at[k])).astype(HALF)
         dg_ref[k] = dg.reshape(FB, SP, D)
         sums.append(column_sum(dg))
         part = dot_back(dg, (u0, u1, u2, u3)[k][0])
@@ -469,13 +466,35 @@
     ]
 
 
+def other_device(lay, me, t):
+    j = lax.rem(me + t, lay.dp * lay.n)
+    return {"fsdp": lax.rem(j, lay.n), "dp": lax.div(j, lay.n)}
+
+
+def greet_all(lay, me):
+    barrier = pltpu.get_barrier_semaphore()
+
+    @pl.loop(1, lay.dp * lay.n)
+    def _(t):
+        pl.semaphore_signal(barrier, inc=1, device_id=other_device(lay, me, t), device_id_type=MESH)
+
+    pl.semaphore_wait(barrier, lay.dp * lay.n - 1)
+
+
 class Reducer:
-    def __init__(self, lay):
+    def __init__(self, lay, squares, everyone):
         self.lay = lay
+        self.squares = squares
         self.i, self.a, self.b, self.y, self.c = lay.place()
         self.here = lay.peer(self.i, self.y, 1 - self.c)
         self.pending = []
-        greet(lay, self.i, self.a, self.b, self.y, self.c)
+        if everyone:
+            greet_all(lay, lax.axis_index("dp") * lay.n + self.i)
+        else:
+            greet(lay, self.i, self.a, self.b, self.y, self.c)
+
+    def square(self, value, share):
+        self.squares[...] += jnp.sum((value * value).reshape(-1, 8, D), 0) * share
 
     def remote(self, src, dst, sends, at, recvs, dev, like):
         pltpu.make_async_remote_copy(
@@ -578,6 +597,7 @@
             like = lambda: st.every.at[0, k]
         else:
             st.fin[k] = value
+            self.square(value, 1.0)
             source = st.fin.at[k]
             like = lambda: st.fin.at[k]
             landing = target(self.c, self.slot(st, v, q))
@@ -600,6 +620,7 @@
             for w in range(1, Y):
                 value = value + st.every[w, k]
             st.fin[k] = value
+            self.square(value, 1.0 / Y)
             self.finish(st, k, target(self.c, q))
         else:
             for w in range(1, Y):
@@ -695,15 +716,16 @@
 
 def early_kernel(lay, part, pairs, *refs):
     (e_ref, r3_ref, a2_ref, dg_ref, dq_ref, dk_ref, dv_ref, cls_ref, xs_ref, d2_ref, qt_ref, kt_ref, vt_ref, fill_ref, x0_ref, mats_ref, v_ref) = refs[:17]
-    (og_ref, fq_ref, fk_ref, fv_ref, d1_ref, r1_ref, dy_ref, do_ref, tq_ref, tk_ref, tv_ref, rp_ref, sum2_ref, pos_ref, time_ref, sum3_ref) = refs[17:33]
-    red = Reducer(lay)
-    st = Sums(refs[33 : 33 + SUMS], part.common, part.split)
-    w_buf, w_sem = refs[33 + SUMS :]
+    (og_ref, fq_ref, fk_ref, fv_ref, d1_ref, r1_ref, dy_ref, do_ref, tq_ref, tk_ref, tv_ref, rp_ref, sum2_ref, pos_ref, time_ref, sum3_ref, sq_ref) = refs[17:34]
+    red = Reducer(lay, sq_ref, False)
+    sq_ref[...] = jnp.zeros_like(sq_ref)
+    st = Sums(refs[34 : 34 + SUMS], part.common, part.split)
+    w_buf, w_sem = refs[34 + SUMS :]
     load = pltpu.make_async_copy(mats_ref.at[pl.ds(1, 8)], w_buf, w_sem.at[0])
     load.start()
 
     def target(core, h):
-        return og_ref.at[2 * h + core]
+        return og_ref.at[part.first + 2 * h + core]
 
     work = part_work(lay, part, st, target)
     rows = F * SP
@@ -764,18 +786,20 @@
     return pl.pallas_call(
         functools.partial(early_kernel, lay, part, pairs),
         in_specs=[ANY] * 7 + [vmem] + [ANY] * 8 + [vmem],
-        out_specs=[ANY] * 12 + [vmem, vmem, ANY, vmem],
-        out_shape=[full(2 * part.half, lay.rows, D), ROWS16, ROWS16, ROWS16, ROWS32] + [ROWS16] * 7 + [full(16, D), full(SP, D), full(F, 1, D), full(16, D)],
+        out_specs=[ANY] * 12 + [vmem, vmem, ANY, vmem, vmem],
+        out_shape=[full(NMAT, lay.rows, D), ROWS16, ROWS16, ROWS16, ROWS32] + [ROWS16] * 7 + [full(16, D), full(SP, D), full(F, 1, D), full(16, D), full(8, D)],
         scratch_shapes=sums_scratch(lay, lay.rows, part.common, part.split) + [pltpu.VMEM((8, D, D), HALF), pltpu.SemaphoreType.DMA((1,))],
         compiler_params=pltpu.CompilerParams(collective_id=1, has_side_effects=True, vmem_limit_bytes=62 * 2**20),
     )(two(e), two(r3), two(a2), two(dg), dq, dk, dv, cls, xs, d2, qt, kt, vt, fill, x0, mats, table)
 
 
 def late_kernel(lay, part, pairs, count, *refs):
-    s_ref, operands = refs[0], refs[1 : 1 + count]
-    og_ref, os_ref = refs[1 + count : 3 + count]
-    red = Reducer(lay)
-    rest = refs[3 + count :]
+    s_ref, sq_ref, operands = refs[0], refs[1], refs[3 : 3 + count]
+    og_ref, os_ref, tiles_ref = refs[3 + count : 6 + count]
+    rest = refs[6 + count : -4]
+    squares, tile, tile_sent, tile_come = refs[-4:]
+    red = Reducer(lay, squares, True)
+    squares[...] = sq_ref[...]
     st = Sums(rest[:SUMS], part.common, part.split)
     little = Sums(rest[SUMS : 2 * SUMS], 1, 0)
     small_sem = rest[2 * SUMS]
@@ -783,7 +807,7 @@
     load.start()
 
     def target(core, h):
-        return og_ref.at[2 * h + core]
+        return og_ref.at[part.first + 2 * h + core]
 
     work = part_work(lay, part, st, target)
     work = [(little, lambda core, h: os_ref.at[core], None, 0)] + work
@@ -794,19 +818,48 @@
     pl.run_scoped(lambda *buffers: products_and_hand(red, part, st, work, operands, jobs, buffers), *product_buffers(rows))
     for s in range(steps_beside(part, 1), len(work) + 3):
         red.progress(work, s)
+    tile[...] = sum(squares[:, e * 128 : e * 128 + 128] for e in range(D // 128))
+    me, total = lax.axis_index("dp") * lay.n + red.i, lay.dp * lay.n
+
+    def swap(t, place):
+        return pltpu.make_async_remote_copy(
+            src_ref=tile, dst_ref=tiles_ref.at[place], send_sem=tile_sent.at[t], recv_sem=tile_come.at[t],
+            device_id=other_device(lay, me, t), device_id_type=MESH,
+        )
+
+    @pl.loop(1, total)
+    def _(t):
+        swap(t, me).start()
+
+    tiles_ref[me] = tile[...]
     red.done(work)
 
-
-def late(lay, part, pairs, small, arrays):
+    @pl.loop(1, total)
+    def _(t):
+        swap(t, lax.rem(me - t + total, total)).wait()
+
+
+def late(lay, part, pairs, small, squares, sums, arrays):
     full = functools.partial(shape, dtype=FULL)
+    vmem = pl.BlockSpec(memory_space=pltpu.VMEM)
+    everyone = lay.dp * lay.n
+    dma = pltpu.SemaphoreType.DMA
     return pl.pallas_call(
         functools.partial(late_kernel, lay, part, pairs, len(arrays)),
-        in_specs=[ANY] * (1 + len(arrays)),
-        out_specs=[ANY, ANY],
-        out_shape=[full(2 * part.half, lay.rows, D), full(2, small.shape[2], D)],
-        scratch_shapes=sums_scratch(lay, lay.rows, part.common, part.split) + sums_scratch(lay, small.shape[2], 1, 0) + [pltpu.SemaphoreType.DMA((1,))],
+        in_specs=[ANY, vmem] + [ANY] * (1 + len(arrays)),
+        out_specs=[ANY, ANY, vmem],
+        out_shape=[full(NMAT, lay.rows, D), full(2, small.shape[2], D), full(everyone, 8, 128)],
+        scratch_shapes=sums_scratch(lay, lay.rows, part.common, part.split) + sums_scratch(lay, small.shape[2], 1, 0)
+        + [dma((1,)), pltpu.VMEM((8, D), FULL), pltpu.VMEM((8, 128), FULL), dma((everyone,)), dma((everyone,))],
+        input_output_aliases={2: 0},
         compiler_params=pltpu.CompilerParams(collective_id=4, has_side_effects=True, vmem_limit_bytes=62 * 2**20),
-    )(small, *[x.reshape(-1, D) for x in arrays])
+    )(small, squares, sums, *[x.reshape(-1, D) for x in arrays])
+
+
+AHEAD = 1
+IN_EMBED = (2,)
+IN_TIME = (4, 12)
+IN_SPACE = (0, 2)
 
 
 def front_kernel(lay, w_ref, s_ref, p_ref, tfill_ref, sfill_ref, *refs):
@@ -830,7 +883,7 @@
         ).wait_recv()
 
     def matrix_of(core, k, v=0):
-        h = k if k < lay.common else lay.common + turn(y, v, Y) * lay.split + (k - lay.common)
+        h = k * Y + turn(y, v, Y) if k < lay.split else lay.split * (Y - 1) + k
         return 2 * h + core
 
     def source(k):
@@ -850,20 +903,30 @@
         m = 2 * k + c
         return pltpu.make_async_copy(w_ref.at[m], ow_ref.at[m, i], own.at[k + 1])
 
+    def send_along(step):
+        if step < len(order):
+            k = order[step]
+            for t in range(1, A):
+                remote(source(k), at(k, i), zs, (k + 1, t), zr, lay.peer(turn(a, t, A) * B + b, y, c), like(k))
+
+    def send_over(k):
+        for u in range(1, B):
+            remote(source(k), at(k, i), xs, (k + 1, u, 0), xr, lay.peer(a * B + turn(b, u, B), y, c), like(k))
+
+    for step in range(AHEAD):
+        send_along(step)
     for k in order:
-        for t in range(1, A):
-            remote(source(k), at(k, i), zs, (k + 1, t), zr, lay.peer(turn(a, t, A) * B + b, y, c), like(k))
+        send_over(k)
     for k in range(-1, lay.half):
         local(k).start()
 
     def over(k, j, t, u):
-        if k >= lay.common:
+        if 0 <= k < lay.split:
             for v in range(1, Y):
-                remote(at(k, j), at(k, j), ys, (k - lay.common, v, t, u), yr, lay.peer(i, turn(y, v, Y), c), like(k))
+                remote(at(k, j), at(k, j), ys, (k, v, t, u), yr, lay.peer(i, turn(y, v, Y), c), like(k))
 
     def cross(k):
-        for u in range(1, B):
-            remote(source(k), at(k, i), xs, (k + 1, u, 0), xr, lay.peer(a * B + turn(b, u, B), y, c), like(k))
+        send_along(order.index(k) + AHEAD)
         for t in range(1, A):
             j = turn(a, -t, A) * B + b
             landed(at(k, j), zr, k + 1, t)
@@ -881,10 +944,7 @@
             local(k).wait()
             remote(os_ref.at[c], os_ref.at[c], cs, (0,), cr, here, lambda: os_ref.at[0])
         else:
-            if k < lay.common:
-                local(k).wait()
-            else:
-                own_wait(k, 0)
+            own_wait(k, 0)
             m = matrix_of(c, k)
             remote(ow_ref.at[m], ow_ref.at[m], cs, (k + 1,), cr, here, lambda: ow_ref.at[0])
 
@@ -895,38 +955,50 @@
     def slot(q, v):
         return K + 1 + (v - 1) * lay.split + q
 
-    def from_planes():
+    def from_planes(k):
+        if k in closed or not 0 <= k < lay.split:
+            return
+        closed.append(k)
         for v in range(1, Y):
-            for q in range(lay.split):
-                k = lay.common + q
-                m = matrix_of(c, k, -v)
-                for t in range(A):
-                    for u in range(B):
-                        if t or u:
-                            j = turn(a, -t, A) * B + turn(b, -u, B)
-                            landed(ow_ref.at[m, j], yr, q, v, t, u)
-                own_wait(k, -v)
-                remote(ow_ref.at[m], ow_ref.at[m], cs, (slot(q, v),), cr, here, lambda: ow_ref.at[0])
-
-    def paired(k, v=0):
+            m = matrix_of(c, k, -v)
+            for t in range(A):
+                for u in range(B):
+                    if t or u:
+                        j = turn(a, -t, A) * B + turn(b, -u, B)
+                        landed(ow_ref.at[m, j], yr, k, v, t, u)
+            own_wait(k, -v)
+            remote(ow_ref.at[m], ow_ref.at[m], cs, (slot(k, v),), cr, here, lambda: ow_ref.at[0])
+
+    def paired(k):
         if k < 0:
             landed(os_ref.at[1 - c], cr, 0)
         else:
-            landed(ow_ref.at[matrix_of(1 - c, k, v)], cr, k + 1 if v == 0 else slot(k - lay.common, -v))
+            landed(ow_ref.at[matrix_of(1 - c, k)], cr, k + 1)
+            if k < lay.split:
+                for v in range(1, Y):
+                    landed(ow_ref.at[matrix_of(1 - c, k, -v)], cr, slot(k, v))
 
     def fetch(first, count):
         span = pl.ds(first, count)
         return pltpu.make_async_copy(ow_ref.at[span], w_buf.at[span], wsem.at[first])
 
-    begun = 0
-    for step in range(4):
-        cross(order[step])
-        if step:
+    closed = []
+
+    def advance(step):
+        if step < len(order):
+            cross(order[step])
+        if 0 <= step - 1 < len(order):
             share(order[step - 1])
-        begun = step + 1
-    paired(-1)
-    paired(0)
-    paired(1)
+        if 0 <= step - 2 < len(order):
+            from_planes(order[step - 2])
+
+    first, second = (1, 3) if lay.split else (2, 5)
+    begun = first + 2
+    for step in range(begun):
+        advance(step)
+    from_planes(first - 1)
+    for k in range(-1, first):
+        paired(k)
     fetch(0, 4).start()
     table = pltpu.make_async_copy(os_ref.at[0], piece, wsem.at[lay.half])
     table.start()
@@ -934,7 +1006,8 @@
     table.wait()
     for j in range(lay.n):
         lane = min(lay.rows * j // 128 * 128, D - 256)
-        v_ref[: piece.shape[1], lane : lane + 256] += piece[j].astype(FULL)
+        wide = jnp.concatenate([piece[j].astype(FULL), jnp.zeros(piece.shape[1:], FULL)], 1)
+        v_ref[: piece.shape[1], lane : lane + 256] += pltpu.roll(wide, lay.rows * j - lane, 1)
     pos_buf[...] = v_ref[31 : 31 + SP, :]
     for f in range(F):
         time_buf[f] = v_ref[1 + f : 2 + f, :]
@@ -942,16 +1015,10 @@
     ws = [Weight(w_buf.at[k]) for k in range(9)]
     steps = F // FB
 
-    def advance(step):
-        if step < len(order):
-            cross(order[step])
-        if step - 1 < len(order):
-            share(order[step - 1])
-
     def embed(p, *outs):
         now = pl.program_id(0)
         embed_kernel(p, *ws[:4], v_ref, pos_buf, time_buf.at[pl.ds(now * FB, FB)], *outs)
-        for s, place in enumerate((1, 3)):
+        for s, place in enumerate(IN_EMBED):
             @pl.when(now == place)
             def _():
                 advance(begun + s)
@@ -962,15 +1029,20 @@
 
     def time(q, k, v, fill, o):
         time_kernel(q, k, v, fill, o)
-        for s, place in enumerate((5, 11)):
+        for s, place in enumerate(IN_TIME):
             @pl.when(pl.program_id(0) == place)
             def _():
-                advance(begun + 2 + s)
+                advance(begun + len(IN_EMBED) + s)
 
     pltpu.emit_pipeline(time, grid=(SP // GROUP,), in_specs=[SLAB] * 3 + [FILL], out_specs=[SLAB])(
         qt_ref, kt_ref, vt_ref, tfill_ref, ot_ref
     )
-    for k in range(2, 5):
+    done = begun + len(IN_EMBED) + len(IN_TIME)
+    for step in range(done, second + 2):
+        advance(step)
+    done = max(done, second + 2)
+    for k in range(first, second):
+        from_planes(k)
         paired(k)
     fetch(4, 5).start()
     fetch(4, 5).wait()
@@ -978,21 +1050,18 @@
     def space(o, x, fill, *outs):
         space_kernel(o, x, *ws[4:9], v_ref, fill, *outs)
 
-        @pl.when(pl.program_id(0) == 0)
-        def _():
-            advance(begun + 4)
+        for s, place in enumerate(IN_SPACE):
+            @pl.when(pl.program_id(0) == place)
+            def _():
+                advance(done + s)
 
     pltpu.emit_pipeline(space, grid=(steps,), in_specs=[FRAMES, FRAMES, per_frame(1, SP)], out_specs=[FRAMES] * 7 + [per_frame(8, D)])(
         ot_ref, x0_ref, sfill_ref, yt_ref, xs_ref, as_ref, qs_ref, ks_ref, vs_ref, mix_ref, cls_ref
     )
-    for step in range(begun + 5, len(order) + 1):
+    for step in range(done + len(IN_SPACE), len(order) + 1):
         advance(step)
-    from_planes()
-    for k in range(5, K):
+    for k in range(second, K):
         paired(k)
-    for v in range(1, Y):
-        for q in range(lay.split):
-            paired(lay.common + q, -v)
     for make, sems, at_ in pending:
         ref = make()
         pltpu.make_async_remote_copy(
@@ -1062,7 +1131,7 @@
         [ROWS16, ROWS32, ROWS16, HIDDEN32, HIDDEN16, ROWS32, shape(8, D, dtype=FULL)],
     )(os_, cls, xs, *[mats] * 9, table, share)
     pooled = (pool[:1] / (F * S + 1)).astype(HALF)
-    head = rest[1][:, : lay.rows].reshape(D, -1)
+    head = rest[1][:, : 2 * lay.rows].reshape(lay.n, 2, lay.rows, 128).transpose(0, 2, 1, 3).reshape(D, 256)
     saved = (table, share, space_fill, time_fill_back, padded, x0, at, qt, kt, vt, ot, yt, xs, as_, qs, ks, vs, of, x2, a2, g, e, x3)
     return pooled, mats, head, saved
 
@@ -1084,7 +1153,7 @@
     cls = cls.astype(HALF).astype(FULL) / F
     first = Part(lay, 10, 4, 1 if lay.planes <= 4 else 0)
     pairs = [((2, 0), (3, k)) for k in range(4)] + [((0, k), (1, 0)) for k in range(4)]
-    upper, fq, fk, fv, d1, r1, dy, do, tq, tk, tv, rp, sums2, pos, time, sums3 = early(
+    upper, fq, fk, fv, d1, r1, dy, do, tq, tk, tv, rp, sums2, pos, time, sums3, squares = early(
         lay, first, pairs, (e, r3, a2, dg, dq, dk, dv, xs, d2, qt, kt, vt, time_fill, x0, mats), cls, table
     )
     class_grad = sums2[4:5]
@@ -1101,8 +1170,7 @@
     pairs = [((left, 0), (right, 0)) for left, right in pairs]
 
     def finish(small):
-        lower, rest = late(lay, second, pairs, small, operands)
-        return jnp.concatenate([lower, upper], 0), rest
+        return late(lay, second, pairs, small, squares, upper, operands)
 
     return finish, grad_vecs
 
@@ -1136,11 +1204,10 @@
 
 
 def pack(lay, head, vecs):
-    first = lay.rows * lax.axis_index("fsdp")
-    lane = first - jnp.minimum(first // 128 * 128, D - 256)
     tall = -(-NVEC // 16) * 16
-    moved = lax.dynamic_update_slice(jnp.zeros((tall, 256), HALF), vecs, (0, lane))
-    return jnp.stack([moved, jnp.pad(head, ((0, tall - head.shape[0]), (0, 0)))])
+    first = jnp.pad(vecs, ((0, tall - NVEC), (0, 128 - lay.rows)))
+    second = jnp.concatenate([head[:, :128], head[:, 128:]], 0)
+    return jnp.stack([first, jnp.pad(second, ((0, tall - second.shape[0]), (0, 0)))])
 
 
 def pack_all(head, vecs, n):
@@ -1218,15 +1285,9 @@
     back_pooled, grad_head, unused_bias = project_back(pooled, head16, back_projected)
     finish, grad_vecs = backward(lay, mats16, saved, back_pooled)
     small = pack_all(grad_head, grad_vecs, n).astype(jnp.bfloat16)
-    grad_mats, grad_small = finish(small)
+    grad_mats, grad_small, tiles = finish(small)
+    squared_norm = jnp.sum(tiles)
     grad_head, grad_vecs = unpack_shard(grad_small, n)
-    partial_squares = (
-        jnp.sum(grad_mats * grad_mats)
-        + jnp.sum(grad_head * grad_head)
-        + jnp.sum(grad_vecs * grad_vecs)
-    )
-    squares = spread(lay.dp, n, jnp.broadcast_to(partial_squares, (8, 128)), 3)
-    squared_norm = jnp.sum(squares[:, 0, 0]) / lay.dp
     factor = CLIP_AT / jnp.maximum(jnp.sqrt(squared_norm), CLIP_AT)
     mats_out = adamw_step(
         matrices, matrix_first, matrix_second, matrix_average, grad_mats, factor, RATE

time: 599 us -> 551 us (0.920)
  Pallas kernels: 517 us -> 481 us
  local copies, waits for them, and re-layouts: 20.8 us -> 14 us
    pallas_call x1, Pallas kernels: 166 us -> 141 us  [front(): pl.pallas_call(functools.partial(front_kernel, lay), in_specs=[ANY] * 5,...]
    pallas_call x2 -> x1, Pallas kernels: 29.7 us -> 16.8 us  [spread(): pl.pallas_call(functools.partial(spread_kernel, dp, n), out_shape=jax.Sha...]
    pallas_call x1, Pallas kernels: 72.8 us -> 61.5 us  [backward(): call(mlp_back_kernel, steps, [FRAMES, FRAMES, HIDDEN, whole(1, D)] + matr...]
    pallas_call x1, Pallas kernels: 102 us -> 111 us  [late(): pl.pallas_call(functools.partial(late_kernel, lay, part, pairs, len(array...]
where the time goes in v5:
time: 551 us; the launch traced here: 541 us
  Pallas kernels  481 us (87%)
  other arithmetic  39.2 us (7%)
  local copies, waits for them, and re-layouts  14 us (3%)
    pallas_call x1, Pallas kernels, front(): pl.pallas_call(functools.partial(front_kernel, lay), in_specs=[ANY] * 5,...  141 us
    pallas_call x1, Pallas kernels, late(): pl.pallas_call(functools.partial(late_kernel, lay, part, pairs, len(array...  111 us
    pallas_call x1, Pallas kernels, early(): pl.pallas_call(functools.partial(early_kernel, lay, part, pairs), in_spec...  106 us
    pallas_call x1, Pallas kernels, backward(): call(mlp_back_kernel, steps, [FRAMES, FRAMES, HIDDEN, whole(1, D)] + matr...  61.5 us
    pallas_call x1, Pallas kernels, forward(): call(mlp_kernel, steps, [FRAMES, whole(1, D), FRAMES] + matrices(9, 9) +...  45 us
    add x3, other arithmetic, adamw_step(): average = AVERAGE_KEEP * average + (1.0 - AVERAGE_KEEP) * weight  20 us
    pallas_call x1, Pallas kernels, spread(): pl.pallas_call(functools.partial(spread_kernel, dp, n), out_shape=jax.Sha...  16.8 us

profile of v5, /device:TPU:0, one launch (start us, length us, event | category | flops | bytes accessed | tf_op | source)
XLA Modules:
  0.0 541.3 jit_solution(12414394981180770976)
XLA Ops:
  0.7 4.5 convert_element_type.30.w_ref
  6.1 1.9 copy.79.p_ref
  8.3 1.6 broadcast_select_fusion
  10.5 141.3 %shard_map.254 = (bf16[18,8,96,768]{3,2,1,0:T(8,128)(2,1)}, bf16[2,8,240,128]{3,2,1,0:T(8,128)(2,1)}, bf16[8,208,768]{2,1,0:T(8,128)(2,1)}, f32[8,208,768]{2,1,0...) custom-call(bf16[18,96,768]{2,1,0:T(8,128)(2,1)} %convert_element_ty, ...), custom_call_target="tpu_custom_call" | custom-call | tf_op jit(solution)/shard_map/pallas_call | solution.py:1090
  151.8 1.1 slice_bitcast_fusion
  153.2 1.0 slice_reduce_fusion.3
  154.8 0.9 broadcast_in_dim_tile.6.share_ref
  155.7 45.0 %shard_map.255 = (bf16[8,208,768]{2,1,0:T(8,128)(2,1)}, f32[8,208,768]{2,1,0:T(8,128)}, bf16[8,208,768]{2,1,0:T(8,128)(2,1)}, f32[4,8,208,768]{3,2,1,0:T(8,128)}...) custom-call(bf16[8,208,768]{2,1,0:T(8,128)(2,1)} %get-tuple-element.68.o_ref, ...), custom_call_target="tpu_custom_call" | custom-call | tf_op jit(solution)/shard_map/pallas_call | solution.py:1127
  200.7 0.9 fusion.5
  203.6 16.8 %shard_map.256 = f32[32,8,128]{2,1,0:T(8,128)} custom-call(f32[8,128]{1,0:T(8,128)} %pad.24.x_ref), custom_call_target="tpu_custom_call" | custom-call | tf_op jit(solution)/shard_map/pallas_call | solution.py:107
  220.3 0.9 slice.109
  225.4 1.2 broadcast_in_dim.161.fill_ref
  226.6 61.5 %shard_map.257 = (bf16[8,208,768]{2,1,0:T(8,128)(2,1)}, bf16[4,8,208,768]{3,2,1,0:T(8,128)(2,1)}, f32[8,208,768]{2,1,0:T(8,128)}, bf16[8,208,768]{2,1,0:T(8,128)...) custom-call(f32[8,208,768]{2,1,0:T(8,128)} %get-tuple-element.76.x3_, ...), custom_call_target="tpu_custom_call" | custom-call | tf_op jit(solution)/shard_map/pallas_call | solution.py:1145
  288.0 1.0 slice_reduce_fusion
  289.0 1.0 slice_reduce_fusion.1
  290.0 1.0 slice_reduce_fusion.2
  291.6 105.9 %shard_map.258 = (f32[18,96,768]{2,1,0:T(8,128)}, bf16[8,208,768]{2,1,0:T(8,128)(2,1)}, bf16[8,208,768]{2,1,0:T(8,128)(2,1)}, bf16[8,208,768]{2,1,0:T(8,128)(2,1...) custom-call(bf16[6656,768]{1,0:T(8,128)(2,1)} %bitcast.99, ...), custom_call_target="tpu_custom_call" | custom-call | tf_op jit(solution)/shard_map/pallas_call | solution.py:786
  399.0 0.8 convert.81
  399.8 0.8 convert.82
  400.7 1.1 slice.167
  405.7 0.9 pad_maximum_fusion.refs_0_
  406.7 110.5 %shard_map.259 = (f32[18,96,768]{2,1,0:T(8,128)}, f32[2,32,768]{2,1,0:T(8,128)}, f32[32,8,128]{2,1,0:T(8,128)}) custom-call(bf16[2,8,32,768]{3,2,1,0:T(8,128)(2,1)} %pad_maximum_fusion.refs_0_, f32[8,768]{1,0:T(8,128)} %get-tuple-element.101.refs_1_, f32[18,96,768]{2,1,0:T(8,128)} %get-tuple-element.102.refs_2_, ...), custom_call_target="tpu_custom_call", output_to_operand_aliasing={{0}: (2, {})} | custom-call | tf_op jit(solution)/shard_map/pallas_call | solution.py:847
  517.2 1.5 reduce_sum.103
  519.6 18.4 %multiply_add_fusion = (f32[18,96,768]{2,1,0:T(8,128)}, f32[18,96,768]{2,1,0:T(8,128)}, f32[18,96,768]{2,1,0:T(8,128)}, f32[18,96,768]{2,1,0:T(8,128)}) fusion(f32[18,96,768]{2,1,0:T(8,128)} %param.21, f32[18,96,768]{2,1,0:T(8,128)} %param.18, f32[18,96,768]{2,1,0:T(8,128)} %get-tuple-element.120, f32[]{:T(128)S(6)} %div.98, f32[18,96,768]{2,1,0:T(8,128)} %param.19, ...), kind=kLoop, calls=%fused_computation.2 | loop fusion | flops 25214976 | bytes 47775748 | tf_op jit(solution)/shard_map/add | solution.py:1202
  (101 shorter events, 14.6 us)
Async XLA Ops:
  0.6 4.6 copy-start.1
  0.7 4.6 copy-start.3
  0.7 5.4 copy-start
  0.7 7.3 %copy-start.13 = (s32[1,8,196]{2,1,0:T(8,128)S(1)}, s32[1,8,196]{2,1,0:T(8,128)}, u32[]{:S(2)}) copy-start(s32[1,8,196]{2,1,0:T(8,128)} %param.16) | copy-start | bytes 18820
  155.7 65.7 %copy-start.14 = (s32[32]{0:T(128)S(1)}, s32[32]{0:T(128)}, u32[]{:S(2)}) copy-start(s32[32]{0:T(128)} %param.17) | copy-start | bytes 388
  291.6 109.1 %copy-start.12 = (f32[16,768]{1,0:T(8,128)S(1)}, f32[16,768]{1,0:T(8,128)}, u32[]{:S(2)}) copy-start(f32[16,768]{1,0:T(8,128)} %get-tuple-element.99) | copy-start | bytes 147460
  519.5 18.5 %copy-start.5 = (f32[2,32,768]{2,1,0:T(8,128)S(1)}, f32[2,32,768]{2,1,0:T(8,128)}, u32[]{:S(2)}) copy-start(f32[2,32,768]{2,1,0:T(8,128)} %get-tuple-element.121) | copy-start | bytes 589828
  519.5 18.6 %copy-start.2 = (f32[96,256]{1,0:T(8,128)S(1)}, f32[96,256]{1,0:T(8,128)}, u32[]{:S(2)}) copy-start(f32[96,256]{1,0:T(8,128)} %param.22) | copy-start | bytes 294916
  519.5 18.6 %copy-start.6 = (f32[96,256]{1,0:T(8,128)S(1)}, f32[96,256]{1,0:T(8,128)}, u32[]{:S(2)}) copy-start(f32[96,256]{1,0:T(8,128)} %param.25) | copy-start | bytes 294916
  519.5 18.6 %copy-start.7 = (f32[96,256]{1,0:T(8,128)S(1)}, f32[96,256]{1,0:T(8,128)}, u32[]{:S(2)}) copy-start(f32[96,256]{1,0:T(8,128)} %param.23) | copy-start | bytes 294916
  519.5 18.6 %copy-start.8 = (f32[96,256]{1,0:T(8,128)S(1)}, f32[96,256]{1,0:T(8,128)}, u32[]{:S(2)}) copy-start(f32[96,256]{1,0:T(8,128)} %param.24) | copy-start | bytes 294916
  519.5 19.6 %copy-start.4 = (f32[227,96]{0,1:T(8,128)S(1)}, f32[227,96]{0,1:T(8,128)}, u32[]{:S(2)}) copy-start(f32[227,96]{0,1:T(8,128)} %param.26) | copy-start | bytes 261508
  519.5 19.6 %copy-start.9 = (f32[227,96]{0,1:T(8,128)S(1)}, f32[227,96]{0,1:T(8,128)}, u32[]{:S(2)}) copy-start(f32[227,96]{0,1:T(8,128)} %param.29) | copy-start | bytes 261508
  519.5 19.6 %copy-start.10 = (f32[227,96]{0,1:T(8,128)S(1)}, f32[227,96]{0,1:T(8,128)}, u32[]{:S(2)}) copy-start(f32[227,96]{0,1:T(8,128)} %param.27) | copy-start | bytes 261508
  519.6 19.6 %copy-start.11 = (f32[227,96]{0,1:T(8,128)S(1)}, f32[227,96]{0,1:T(8,128)}, u32[]{:S(2)}) copy-start(f32[227,96]{0,1:T(8,128)} %param.28) | copy-start | bytes 261508

commit v6 on v5

--- a/solution.py
+++ b/solution.py
@@ -178,6 +178,11 @@
 
 def row_of(rows):
     return lax.rem(lax.broadcasted_iota(jnp.int32, (rows, 1), 0), SP)
+
+
+def row_share(rows):
+    place = row_of(rows)
+    return jnp.where(place < S, 1.0, jnp.where(place == S, 1.0 / F, 0.0))
 
 
 def first_step():
@@ -274,9 +279,10 @@
             cls_ref[f, :, lanes] = mixed[S : S + 8]
 
 
-def mlp_kernel(o_ref, cls_ref, xs_ref, wp_ref, u0, u1, u2, u3, e0, e1, e2, e3, v_ref, share_ref, of_ref, x2_ref, a_ref, g_ref, e_ref, x3_ref, pool_ref):
+def mlp_kernel(o_ref, cls_ref, xs_ref, wp_ref, u0, u1, u2, u3, e0, e1, e2, e3, v_ref, of_ref, x2_ref, a_ref, g_ref, e_ref, x3_ref, pool_ref):
     rows = FB * SP
-    o = jnp.where(row_of(rows) == S, cls_ref[...], flat(o_ref).astype(FULL)).astype(HALF)
+    middle = sum(cls_ref[f, 0:1, :] for f in range(F)) * (1.0 / F)
+    o = jnp.where(row_of(rows) == S, middle, flat(o_ref).astype(FULL)).astype(HALF)
     of_ref[...] = o.reshape(FB, SP, D)
     x2 = flat(xs_ref) + dot(o, wp_ref[0]) + v_ref[16:17]
     x2_ref[...] = x2.reshape(FB, SP, D)
@@ -291,13 +297,13 @@
         e_ref[k] = e.reshape(FB, SP, D)
         x3 = x3 + dot(e, (e0, e1, e2, e3)[k][0])
     x3_ref[...] = x3.reshape(FB, SP, D)
-    final = norm(x3, v_ref[28:29], v_ref[29:30]) * share_ref[...]
+    final = norm(x3, v_ref[28:29], v_ref[29:30]) * row_share(FB * SP)
     add_rows(pool_ref, [column_sum(final)])
 
 
-def mlp_back_kernel(x3_ref, x2_ref, g_ref, d_ref, wp_ref, u0, u1, u2, u3, e0, e1, e2, e3, v_ref, share_ref, q_ref, k_ref, b_ref, fill_ref,
+def mlp_back_kernel(x3_ref, x2_ref, g_ref, d_ref, wp_ref, u0, u1, u2, u3, e0, e1, e2, e3, v_ref, q_ref, k_ref, b_ref, fill_ref,
                     r3_ref, dg_ref, d2_ref, r2_ref, dq_ref, dk_ref, dv_ref, cq_ref, ck_ref, cv_ref, sum_ref, do_ref):
-    top = d_ref[0:1] * share_ref[...]
+    top = d_ref[0:1] * row_share(FB * SP)
     d3, unit = norm_back(flat(x3_ref), v_ref[28:29], top)
     sums = [column_sum(unit), column_sum(top)]
     r3 = d3.astype(HALF)
@@ -329,12 +335,13 @@
 
 
 def space_back_kernel(dq_ref, dk_ref, dv_ref, cls_ref, xs_ref, d2_ref, w0, w1, w2, w3, w4, v_ref, fq_ref, fk_ref, fv_ref, d1_ref, r1_ref, dy_ref, do_ref, sum_ref):
-    rows = FB * SP
+    frames = xs_ref.shape[0]
+    rows = frames * SP
     is_class = row_of(rows) == S
     grads = []
     for k, (ref, out) in enumerate(zip((dq_ref, dk_ref, dv_ref), (fq_ref, fk_ref, fv_ref))):
         grad = jnp.where(is_class, cls_ref[k : k + 1], flat(ref).astype(FULL)).astype(HALF)
-        out[...] = grad.reshape(FB, SP, D)
+        out[...] = grad.reshape(frames, SP, D)
         grads.append(grad)
     back = dot_back(grads[0], w2[0]) + dot_back(grads[1], w3[0]) + dot_back(grads[2], w4[0])
     d, unit = norm_back(flat(xs_ref), v_ref[24:25], back)
@@ -343,14 +350,14 @@
     kept = jnp.where(is_class, d, 0.0)
     sums.append(column_sum(kept))
     d = d - kept
-    d1_ref[...] = d.reshape(FB, SP, D)
+    d1_ref[...] = d.reshape(frames, SP, D)
     r1 = d.astype(HALF)
-    r1_ref[...] = r1.reshape(FB, SP, D)
+    r1_ref[...] = r1.reshape(frames, SP, D)
     sums.append(column_sum(r1))
     dy = dot_back(r1, w1[0]).astype(HALF)
-    dy_ref[...] = dy.reshape(FB, SP, D)
+    dy_ref[...] = dy.reshape(frames, SP, D)
     sums.append(column_sum(dy))
-    do_ref[...] = dot_back(dy, w0[0]).astype(HALF).reshape(FB, SP, D)
+    do_ref[...] = dot_back(dy, w0[0]).astype(HALF).reshape(frames, SP, D)
     add_rows(sum_ref, sums)
 
 
@@ -715,12 +722,15 @@
 
 
 def early_kernel(lay, part, pairs, *refs):
-    (e_ref, r3_ref, a2_ref, dg_ref, dq_ref, dk_ref, dv_ref, cls_ref, xs_ref, d2_ref, qt_ref, kt_ref, vt_ref, fill_ref, x0_ref, mats_ref, v_ref) = refs[:17]
-    (og_ref, fq_ref, fk_ref, fv_ref, d1_ref, r1_ref, dy_ref, do_ref, tq_ref, tk_ref, tv_ref, rp_ref, sum2_ref, pos_ref, time_ref, sum3_ref, sq_ref) = refs[17:34]
+    (e_ref, r3_ref, a2_ref, dg_ref, dq_ref, dk_ref, dv_ref, cq_ref, ck_ref, cv_ref, sum1_ref, xs_ref, d2_ref, qt_ref, kt_ref, vt_ref, fill_ref, x0_ref, mats_ref, v_ref) = refs[:20]
+    (og_ref, fq_ref, fk_ref, fv_ref, d1_ref, r1_ref, dy_ref, do_ref, tq_ref, tk_ref, tv_ref, rp_ref, vec_ref, sq_ref) = refs[20:34]
     red = Reducer(lay, sq_ref, False)
     sq_ref[...] = jnp.zeros_like(sq_ref)
     st = Sums(refs[34 : 34 + SUMS], part.common, part.split)
-    w_buf, w_sem = refs[34 + SUMS :]
+    w_buf, w_sem, cls_ref, sum2_ref, pos_ref, time_ref, sum3_ref = refs[34 + SUMS :]
+    for k, ref in enumerate((cq_ref, ck_ref, cv_ref)):
+        total = sum(ref[f, 0:1, :] for f in range(F))
+        cls_ref[k : k + 1, :] = total.astype(HALF).astype(FULL) * (1.0 / F)
     load = pltpu.make_async_copy(mats_ref.at[pl.ds(1, 8)], w_buf, w_sem.at[0])
     load.start()
 
@@ -760,16 +770,26 @@
         qt_ref, kt_ref, vt_ref, do_ref, fill_ref, tq_ref, tk_ref, tv_ref
     )
 
-    def embed(dq, dk, dv, x, d1, r, time):
-        embed_back_kernel(dq, dk, dv, x, d1, ws[0], ws[1], ws[2], v_ref, r, pos_ref, time, sum3_ref)
+    def embed(dq, dk, dv, x, d1, r):
+        place = time_ref.at[pl.ds(pl.program_id(0) * FB, FB)]
+        embed_back_kernel(dq, dk, dv, x, d1, ws[0], ws[1], ws[2], v_ref, r, pos_ref, place, sum3_ref)
 
         @pl.when(pl.program_id(0) == 3)
         def _():
             red.progress(work, begun + 4)
 
-    pltpu.emit_pipeline(embed, grid=(steps,), in_specs=[FRAMES] * 5, out_specs=[FRAMES, per_frame(1, D)])(
-        tq_ref, tk_ref, tv_ref, x0_ref, d1_ref, rp_ref, time_ref
-    )
+    pltpu.emit_pipeline(embed, grid=(steps,), in_specs=[FRAMES] * 5, out_specs=[FRAMES])(
+        tq_ref, tk_ref, tv_ref, x0_ref, d1_ref, rp_ref
+    )
+    vec_ref[...] = jnp.zeros_like(vec_ref)
+    for row, ref, first, count in (
+        (0, sum2_ref, 4, 1), (9, sum3_ref, 4, 1), (10, sum3_ref, 0, 2), (12, sum2_ref, 6, 1), (13, sum2_ref, 5, 1), (14, sum2_ref, 0, 2),
+        (16, sum1_ref, 9, 1), (17, sum1_ref, 3, 4), (21, sum1_ref, 2, 1), (22, sum3_ref, 2, 2), (24, sum2_ref, 2, 2), (26, sum1_ref, 7, 2),
+        (28, sum1_ref, 0, 2), (30, sum2_ref, 4, 1), (31, pos_ref, 0, S),
+    ):
+        vec_ref[row : row + count, :] = ref[first : first + count, :]
+    for f in range(F):
+        vec_ref[1 + f : 2 + f, :] = time_ref[f]
     for s in range(begun + 5, len(work) + 3):
         red.progress(work, s)
     red.done(work)
@@ -778,19 +798,20 @@
 FILL = pl.BlockSpec((1, F * GROUP, F * GROUP), lambda i: (i, 0, 0))
 
 
-def early(lay, part, pairs, arrays, cls, table):
+def early(lay, part, pairs, arrays, classes, table):
     vmem = pl.BlockSpec(memory_space=pltpu.VMEM)
     e, r3, a2, dg, dq, dk, dv, xs, d2, qt, kt, vt, fill, x0, mats = arrays
     two = lambda x: x.reshape(-1, D)
     full = functools.partial(shape, dtype=FULL)
     return pl.pallas_call(
         functools.partial(early_kernel, lay, part, pairs),
-        in_specs=[ANY] * 7 + [vmem] + [ANY] * 8 + [vmem],
-        out_specs=[ANY] * 12 + [vmem, vmem, ANY, vmem, vmem],
-        out_shape=[full(NMAT, lay.rows, D), ROWS16, ROWS16, ROWS16, ROWS32] + [ROWS16] * 7 + [full(16, D), full(SP, D), full(F, 1, D), full(16, D), full(8, D)],
-        scratch_shapes=sums_scratch(lay, lay.rows, part.common, part.split) + [pltpu.VMEM((8, D, D), HALF), pltpu.SemaphoreType.DMA((1,))],
+        in_specs=[ANY] * 7 + [vmem] * 4 + [ANY] * 8 + [vmem],
+        out_specs=[ANY] * 12 + [vmem, vmem],
+        out_shape=[full(NMAT, lay.rows, D), ROWS16, ROWS16, ROWS16, ROWS32] + [ROWS16] * 7 + [full(D // 3, D), full(8, D)],
+        scratch_shapes=sums_scratch(lay, lay.rows, part.common, part.split) + [pltpu.VMEM((8, D, D), HALF), pltpu.SemaphoreType.DMA((1,))]
+        + [pltpu.VMEM(dims, FULL) for dims in ((8, D), (16, D), (SP, D), (F, 1, D), (16, D))],
         compiler_params=pltpu.CompilerParams(collective_id=1, has_side_effects=True, vmem_limit_bytes=62 * 2**20),
-    )(two(e), two(r3), two(a2), two(dg), dq, dk, dv, cls, xs, d2, qt, kt, vt, fill, x0, mats, table)
+    )(two(e), two(r3), two(a2), two(dg), dq, dk, dv, *classes, xs, d2, qt, kt, vt, fill, x0, mats, table)
 
 
 def late_kernel(lay, part, pairs, count, *refs):
@@ -887,7 +908,7 @@
         return 2 * h + core
 
     def source(k):
-        return s_ref.at[c] if k < 0 else w_ref.at[matrix_of(c, k)]
+        return s_ref.at[c] if k < 0 else w_ref.at[lax.div(matrix_of(c, k), 2)]
 
     def at(k, j):
         return os_ref.at[c, j] if k < 0 else ow_ref.at[matrix_of(c, k), j]
@@ -900,8 +921,7 @@
     def local(k):
         if k < 0:
             return pltpu.make_async_copy(s_ref.at[c], os_ref.at[c, i], own.at[0])
-        m = 2 * k + c
-        return pltpu.make_async_copy(w_ref.at[m], ow_ref.at[m, i], own.at[k + 1])
+        return pltpu.make_async_copy(w_ref.at[k], ow_ref.at[2 * k + c, i], own.at[k + 1])
 
     def send_along(step):
         if step < len(order):
@@ -950,7 +970,7 @@
 
     def own_wait(k, v):
         m = matrix_of(c, k, v)
-        pltpu.make_async_copy(w_ref.at[m], ow_ref.at[m, i], own.at[lax.div(m, 2) + 1]).wait()
+        pltpu.make_async_copy(w_ref.at[lax.div(m, 2)], ow_ref.at[m, i], own.at[lax.div(m, 2) + 1]).wait()
 
     def slot(q, v):
         return K + 1 + (v - 1) * lay.split + q
@@ -1115,54 +1135,41 @@
     same = spot[:, None] == spot[None]
     time_fill = jnp.where(same[None], time_keys[:, None, :], NEVER)
     time_fill_back = jnp.where(same[None], time_keys[:, :, None], NEVER)
-    one = jnp.where(places[0] < S, 1.0, jnp.where(places[0] == S, 1.0 / F, 0.0)).astype(FULL)
-    share = jnp.broadcast_to(jnp.tile(one, FB)[:, None], (FB * SP, 1))
     mats, rest, padded, x0, at, qt, kt, vt, ot, yt, xs, as_, qs, ks, vs, os_, cls, table = front(
         lay, shard, small, patches, time_fill, space_fill[:, None]
     )
     mats = mats.reshape(NMAT, D, D)
     tab = whole(*table.shape)
     steps = F // FB
-    cls = jnp.mean(cls[:, 0], 0, keepdims=True)
     of, x2, a2, g, e, x3, pool = call(
         mlp_kernel, steps,
-        [FRAMES, whole(1, D), FRAMES] + matrices(9, 9) + [tab, whole(FB * SP, 1)],
+        [FRAMES, whole(F, 8, D), FRAMES] + matrices(9, 9) + [tab],
         [FRAMES] * 3 + [HIDDEN] * 2 + [FRAMES, summed(8)],
         [ROWS16, ROWS32, ROWS16, HIDDEN32, HIDDEN16, ROWS32, shape(8, D, dtype=FULL)],
-    )(os_, cls, xs, *[mats] * 9, table, share)
+    )(os_, cls, xs, *[mats] * 9, table)
     pooled = (pool[:1] / (F * S + 1)).astype(HALF)
     head = rest[1][:, : 2 * lay.rows].reshape(lay.n, 2, lay.rows, 128).transpose(0, 2, 1, 3).reshape(D, 256)
-    saved = (table, share, space_fill, time_fill_back, padded, x0, at, qt, kt, vt, ot, yt, xs, as_, qs, ks, vs, of, x2, a2, g, e, x3)
+    saved = (table, space_fill, time_fill_back, padded, x0, at, qt, kt, vt, ot, yt, xs, as_, qs, ks, vs, of, x2, a2, g, e, x3)
     return pooled, mats, head, saved
 
 
 def backward(lay, mats, saved, back_pooled):
-    (table, share, space_fill, time_fill, padded, x0, at, qt, kt, vt, ot, yt, xs, as_, qs, ks, vs, of, x2, a2, g, e, x3) = saved
+    (table, space_fill, time_fill, padded, x0, at, qt, kt, vt, ot, yt, xs, as_, qs, ks, vs, of, x2, a2, g, e, x3) = saved
     tab = whole(*table.shape)
     steps = F // FB
     top = back_pooled / (F * S + 1)
     column = jnp.broadcast_to(space_fill[:, :, None], (F, SP, 128))
     r3, dg, d2, r2, dq, dk, dv, cq, ck, cv, sums1 = call(
         mlp_back_kernel, steps,
-        [FRAMES, FRAMES, HIDDEN, whole(1, D)] + matrices(9, 9) + [tab, whole(FB * SP, 1), FRAMES, FRAMES, FRAMES, per_frame(SP, 128)],
+        [FRAMES, FRAMES, HIDDEN, whole(1, D)] + matrices(9, 9) + [tab, FRAMES, FRAMES, FRAMES, per_frame(SP, 128)],
         [FRAMES, HIDDEN] + [FRAMES] * 5 + [per_frame(8, D)] * 3 + [summed(16)],
         [ROWS16, HIDDEN16, ROWS32] + [ROWS16] * 4 + [shape(F, 8, D, dtype=FULL)] * 3 + [shape(16, D, dtype=FULL)],
         [pltpu.VMEM((FB, SP, D), HALF)],
-    )(x3, x2, g, top, *[mats] * 9, table, share, qs, ks, vs, column)
-    cls = jnp.concatenate([jnp.sum(part[:, 0], 0, keepdims=True) for part in (cq, ck, cv)], 0)
-    cls = cls.astype(HALF).astype(FULL) / F
+    )(x3, x2, g, top, *[mats] * 9, table, qs, ks, vs, column)
     first = Part(lay, 10, 4, 1 if lay.planes <= 4 else 0)
     pairs = [((2, 0), (3, k)) for k in range(4)] + [((0, k), (1, 0)) for k in range(4)]
-    upper, fq, fk, fv, d1, r1, dy, do, tq, tk, tv, rp, sums2, pos, time, sums3, squares = early(
-        lay, first, pairs, (e, r3, a2, dg, dq, dk, dv, xs, d2, qt, kt, vt, time_fill, x0, mats), cls, table
-    )
-    class_grad = sums2[4:5]
-    grad_vecs = jnp.concatenate(
-        [
-            class_grad, time[:, 0], sums3[4:5], sums3[0:2], sums2[6:7], sums2[5:6], sums2[0:2], sums1[9:10], sums1[3:7], sums1[2:3],
-            sums3[2:4], sums2[2:4], sums1[7:9], sums1[0:2], class_grad, pos[:S],
-        ],
-        0,
+    upper, fq, fk, fv, d1, r1, dy, do, tq, tk, tv, rp, grad_vecs, squares = early(
+        lay, first, pairs, (e, r3, a2, dg, dq, dk, dv, xs, d2, qt, kt, vt, time_fill, x0, mats), (cq, ck, cv, sums1), table
     )
     second = Part(lay, 0, 5, 1 if lay.planes <= 4 else 0)
     operands = (padded, rp, at, tq, tk, tv, ot, dy, yt, r1, as_, fq, fk, fv, of, r2)
@@ -1201,6 +1208,11 @@
     weight = weight - rate * (first_hat / (jnp.sqrt(second_hat) + ADAM_EPSILON) + DECAY * weight)
     average = AVERAGE_KEEP * average + (1.0 - AVERAGE_KEEP) * weight
     return (weight, first, second, average)
+
+
+def own_matrices(lay, matrices):
+    pairs = matrices.reshape(NMAT // 2, 2, lay.rows, D)
+    return lax.dynamic_index_in_dim(pairs, lax.rem(lax.axis_index("dp"), 2), 1, keepdims=False)
 
 
 def pack(lay, head, vecs):
@@ -1248,7 +1260,7 @@
     n = lay.n
     pooled, mats16, head16, saved = forward(
         lay,
-        matrices.astype(jnp.bfloat16),
+        own_matrices(lay, matrices).astype(jnp.bfloat16),
         pack(lay, head_weight.astype(jnp.bfloat16), vectors.astype(jnp.bfloat16)),
         patches,
         patch_keep_mask,

time: 551 us -> 541 us (0.982)
  other arithmetic: 39.2 us -> 30.9 us
where the time goes in v6:
time: 541 us; the launch traced here: 532 us
  Pallas kernels  481 us (89%)
  other arithmetic  30.9 us (6%)
  local copies, waits for them, and re-layouts  12.9 us (2%)
    pallas_call x1, Pallas kernels, front(): pl.pallas_call(functools.partial(front_kernel, lay), in_specs=[ANY] * 5,...  141 us
    pallas_call x1, Pallas kernels, late(): pl.pallas_call(functools.partial(late_kernel, lay, part, pairs, len(array...  111 us
    pallas_call x1, Pallas kernels, early(): pl.pallas_call(functools.partial(early_kernel, lay, part, pairs), in_spec...  106 us
    pallas_call x1, Pallas kernels, backward(): call(mlp_back_kernel, steps, [FRAMES, FRAMES, HIDDEN, whole(1, D)] + matr...  61.6 us
    pallas_call x1, Pallas kernels, forward(): call(mlp_kernel, steps, [FRAMES, whole(F, 8, D), FRAMES] + matrices(9, 9)...  44.5 us
    add x3, other arithmetic, adamw_step(): average = AVERAGE_KEEP * average + (1.0 - AVERAGE_KEEP) * weight  20 us
    pallas_call x1, Pallas kernels, spread(): pl.pallas_call(functools.partial(spread_kernel, dp, n), out_shape=jax.Sha...  16.9 us

profile of v6, /device:TPU:0, one launch (start us, length us, event | category | flops | bytes accessed | tf_op | source)
XLA Modules:
  0.0 531.8 jit_solution(9897546125608899743)
XLA Ops:
  0.7 3.1 fusion.1.w_ref
  3.8 0.9 convert_element_type.29
  4.7 0.9 convert_element_type.28
  5.7 0.7 pad_maximum_fusion.1.s_ref
  6.4 1.9 copy.78.p_ref
  8.6 1.6 broadcast_select_fusion
  10.8 141.2 %shard_map.254 = (bf16[18,8,96,768]{3,2,1,0:T(8,128)(2,1)}, bf16[2,8,240,128]{3,2,1,0:T(8,128)(2,1)}, bf16[8,208,768]{2,1,0:T(8,128)(2,1)}, f32[8,208,768]{2,1,0...) custom-call(bf16[9,96,768]{2,1,0:T(8,128)(2,1)} %fusion.1.w_ref, ...), custom_call_target="tpu_custom_call" | custom-call | tf_op jit(solution)/shard_map/pallas_call | solution.py:1110
  152.0 1.1 slice_bitcast_fusion
  153.4 44.5 %shard_map.255 = (bf16[8,208,768]{2,1,0:T(8,128)(2,1)}, f32[8,208,768]{2,1,0:T(8,128)}, bf16[8,208,768]{2,1,0:T(8,128)(2,1)}, f32[4,8,208,768]{3,2,1,0:T(8,128)}...) custom-call(bf16[8,208,768]{2,1,0:T(8,128)(2,1)} %get-tuple-element.65.o_ref, ...), custom_call_target="tpu_custom_call" | custom-call | tf_op jit(solution)/shard_map/pallas_call | solution.py:1144
  197.9 0.9 fusion.6
  198.8 0.6 multiply_reduce_fusion.1
  200.8 16.9 %shard_map.256 = f32[32,8,128]{2,1,0:T(8,128)} custom-call(f32[8,128]{1,0:T(8,128)} %pad.19.x_ref), custom_call_target="tpu_custom_call" | custom-call | tf_op jit(solution)/shard_map/pallas_call | solution.py:107
  217.7 0.9 slice.41
  222.7 1.2 broadcast_in_dim.136.fill_ref
  223.9 61.6 %shard_map.257 = (bf16[8,208,768]{2,1,0:T(8,128)(2,1)}, bf16[4,8,208,768]{3,2,1,0:T(8,128)(2,1)}, f32[8,208,768]{2,1,0:T(8,128)}, bf16[8,208,768]{2,1,0:T(8,128)...) custom-call(f32[8,208,768]{2,1,0:T(8,128)} %get-tuple-element.73.x3_, ...), custom_call_target="tpu_custom_call" | custom-call | tf_op jit(solution)/shard_map/pallas_call | solution.py:1162
  285.5 106.3 %shard_map.258 = (f32[18,96,768]{2,1,0:T(8,128)}, bf16[8,208,768]{2,1,0:T(8,128)(2,1)}, bf16[8,208,768]{2,1,0:T(8,128)(2,1)}, bf16[8,208,768]{2,1,0:T(8,128)(2,1...) custom-call(bf16[6656,768]{1,0:T(8,128)(2,1)} %bitcast.103, ...), custom_call_target="tpu_custom_call" | custom-call | tf_op jit(solution)/shard_map/pallas_call | solution.py:806
  391.9 1.2 convert.22
  394.4 0.8 convert_reduce_fusion
  396.2 0.9 pad_maximum_fusion.refs_0_
  397.1 110.5 %shard_map.259 = (f32[18,96,768]{2,1,0:T(8,128)}, f32[2,32,768]{2,1,0:T(8,128)}, f32[32,8,128]{2,1,0:T(8,128)}) custom-call(bf16[2,8,32,768]{3,2,1,0:T(8,128)(2,1)} %pad_maximum_fusion.refs_0_, f32[8,768]{1,0:T(8,128)} %get-tuple-element.95.refs_1_, f32[18,96,768]{2,1,0:T(8,128)} %get-tuple-element.96.refs_2_, ...), custom_call_target="tpu_custom_call", output_to_operand_aliasing={{0}: (2, {})} | custom-call | tf_op jit(solution)/shard_map/pallas_call | solution.py:868
  507.6 1.5 reduce_sum.63
  510.0 18.4 %multiply_add_fusion = (f32[18,96,768]{2,1,0:T(8,128)}, f32[18,96,768]{2,1,0:T(8,128)}, f32[18,96,768]{2,1,0:T(8,128)}, f32[18,96,768]{2,1,0:T(8,128)}) fusion(f32[18,96,768]{2,1,0:T(8,128)} %param.21, f32[18,96,768]{2,1,0:T(8,128)} %param.18, f32[18,96,768]{2,1,0:T(8,128)} %get-tuple-element.114, f32[]{:T(128)S(6)} %div.79, f32[18,96,768]{2,1,0:T(8,128)} %param.19, ...), kind=kLoop, calls=%fused_computation.2 | loop fusion | flops 25214976 | bytes 47775748 | tf_op jit(solution)/shard_map/add | solution.py:1209
  528.5 0.8 multiply_add_fusion.4
  529.6 0.8 multiply_add_fusion.2
  (67 shorter events, 7.3 us)
Async XLA Ops:
  0.6 5.8 %copy-start = (bf16[1,8,196,768]{3,1,2,0:T(8,128)(2,1)S(1)}, bf16[1,8,196,768]{3,1,2,0:T(8,128)(2,1)}, u32[]{:S(2)}) copy-start(bf16[1,8,196,768]{3,1,2,0:T(8,128)(2,1)} %param.15) | copy-start | bytes 7225348
  0.7 7.7 %copy-start.10 = (s32[1,8,196]{2,1,0:T(8,128)S(1)}, s32[1,8,196]{2,1,0:T(8,128)}, u32[]{:S(2)}) copy-start(s32[1,8,196]{2,1,0:T(8,128)} %param.16) | copy-start | bytes 18820
  153.4 65.4 %copy-start.11 = (s32[32]{0:T(128)S(1)}, s32[32]{0:T(128)}, u32[]{:S(2)}) copy-start(s32[32]{0:T(128)} %param.17) | copy-start | bytes 388
  509.9 18.5 %copy-start.3 = (f32[2,32,768]{2,1,0:T(8,128)S(1)}, f32[2,32,768]{2,1,0:T(8,128)}, u32[]{:S(2)}) copy-start(f32[2,32,768]{2,1,0:T(8,128)} %get-tuple-element.115) | copy-start | bytes 589828
  509.9 18.6 %copy-start.1 = (f32[96,256]{1,0:T(8,128)S(1)}, f32[96,256]{1,0:T(8,128)}, u32[]{:S(2)}) copy-start(f32[96,256]{1,0:T(8,128)} %param.22) | copy-start | bytes 294916
  509.9 18.6 %copy-start.4 = (f32[96,256]{1,0:T(8,128)S(1)}, f32[96,256]{1,0:T(8,128)}, u32[]{:S(2)}) copy-start(f32[96,256]{1,0:T(8,128)} %param.25) | copy-start | bytes 294916
  510.0 18.6 %copy-start.5 = (f32[96,256]{1,0:T(8,128)S(1)}, f32[96,256]{1,0:T(8,128)}, u32[]{:S(2)}) copy-start(f32[96,256]{1,0:T(8,128)} %param.23) | copy-start | bytes 294916
  510.0 18.6 %copy-start.6 = (f32[96,256]{1,0:T(8,128)S(1)}, f32[96,256]{1,0:T(8,128)}, u32[]{:S(2)}) copy-start(f32[96,256]{1,0:T(8,128)} %param.24) | copy-start | bytes 294916
  510.0 19.6 %copy-start.2 = (f32[227,96]{0,1:T(8,128)S(1)}, f32[227,96]{0,1:T(8,128)}, u32[]{:S(2)}) copy-start(f32[227,96]{0,1:T(8,128)} %param.26) | copy-start | bytes 261508
  510.0 19.6 %copy-start.7 = (f32[227,96]{0,1:T(8,128)S(1)}, f32[227,96]{0,1:T(8,128)}, u32[]{:S(2)}) copy-start(f32[227,96]{0,1:T(8,128)} %param.29) | copy-start | bytes 261508
  510.0 19.6 %copy-start.8 = (f32[227,96]{0,1:T(8,128)S(1)}, f32[227,96]{0,1:T(8,128)}, u32[]{:S(2)}) copy-start(f32[227,96]{0,1:T(8,128)} %param.27) | copy-start | bytes 261508
  510.0 19.6 %copy-start.9 = (f32[227,96]{0,1:T(8,128)S(1)}, f32[227,96]{0,1:T(8,128)}, u32[]{:S(2)}) copy-start(f32[227,96]{0,1:T(8,128)} %param.28) | copy-start | bytes 261508

commit v7 on v6

--- a/solution.py
+++ b/solution.py
@@ -878,8 +878,8 @@
 
 
 AHEAD = 1
-IN_EMBED = (2,)
-IN_TIME = (4, 12)
+IN_EMBED = (0, 3)
+IN_TIME = (6, 12)
 IN_SPACE = (0, 2)
 
 

time: 541 us -> 542 us (level)
  no operation moved by 1% of the time
where the time goes in v7:
time: 542 us; the launch traced here: 533 us
  Pallas kernels  482 us (89%)
  other arithmetic  30.9 us (6%)
  local copies, waits for them, and re-layouts  12.9 us (2%)
    pallas_call x1, Pallas kernels, front(): pl.pallas_call(functools.partial(front_kernel, lay), in_specs=[ANY] * 5,...  137 us
    pallas_call x1, Pallas kernels, late(): pl.pallas_call(functools.partial(late_kernel, lay, part, pairs, len(array...  110 us
    pallas_call x1, Pallas kernels, early(): pl.pallas_call(functools.partial(early_kernel, lay, part, pairs), in_spec...  107 us
    pallas_call x1, Pallas kernels, backward(): call(mlp_back_kernel, steps, [FRAMES, FRAMES, HIDDEN, whole(1, D)] + matr...  61.6 us
    pallas_call x1, Pallas kernels, forward(): call(mlp_kernel, steps, [FRAMES, whole(F, 8, D), FRAMES] + matrices(9, 9)...  44.5 us
    pallas_call x1, Pallas kernels, spread(): pl.pallas_call(functools.partial(spread_kernel, dp, n), out_shape=jax.Sha...  22.2 us
    add x3, other arithmetic, adamw_step(): average = AVERAGE_KEEP * average + (1.0 - AVERAGE_KEEP) * weight  20 us

profile of v7, /device:TPU:0, one launch (start us, length us, event | category | flops | bytes accessed | tf_op | source)
XLA Modules:
  0.0 532.5 jit_solution(8121379706070721180)
XLA Ops:
  0.7 3.1 fusion.1.w_ref
  3.8 0.9 convert_element_type.29
  4.7 0.9 convert_element_type.28
  5.7 0.7 pad_maximum_fusion.1.s_ref
  6.4 1.9 copy.78.p_ref
  8.6 1.6 broadcast_select_fusion
  10.8 136.6 %shard_map.254 = (bf16[18,8,96,768]{3,2,1,0:T(8,128)(2,1)}, bf16[2,8,240,128]{3,2,1,0:T(8,128)(2,1)}, bf16[8,208,768]{2,1,0:T(8,128)(2,1)}, f32[8,208,768]{2,1,0...) custom-call(bf16[9,96,768]{2,1,0:T(8,128)(2,1)} %fusion.1.w_ref, ...), custom_call_target="tpu_custom_call" | custom-call | tf_op jit(solution)/shard_map/pallas_call | solution.py:1110
  147.4 1.1 slice_bitcast_fusion
  148.9 44.5 %shard_map.255 = (bf16[8,208,768]{2,1,0:T(8,128)(2,1)}, f32[8,208,768]{2,1,0:T(8,128)}, bf16[8,208,768]{2,1,0:T(8,128)(2,1)}, f32[4,8,208,768]{3,2,1,0:T(8,128)}...) custom-call(bf16[8,208,768]{2,1,0:T(8,128)(2,1)} %get-tuple-element.65.o_ref, ...), custom_call_target="tpu_custom_call" | custom-call | tf_op jit(solution)/shard_map/pallas_call | solution.py:1144
  193.4 0.9 fusion.6
  194.3 0.6 multiply_reduce_fusion.1
  196.2 22.2 %shard_map.256 = f32[32,8,128]{2,1,0:T(8,128)} custom-call(f32[8,128]{1,0:T(8,128)} %pad.19.x_ref), custom_call_target="tpu_custom_call" | custom-call | tf_op jit(solution)/shard_map/pallas_call | solution.py:107
  218.5 0.9 slice.41
  223.5 1.2 broadcast_in_dim.136.fill_ref
  224.7 61.6 %shard_map.257 = (bf16[8,208,768]{2,1,0:T(8,128)(2,1)}, bf16[4,8,208,768]{3,2,1,0:T(8,128)(2,1)}, f32[8,208,768]{2,1,0:T(8,128)}, bf16[8,208,768]{2,1,0:T(8,128)...) custom-call(f32[8,208,768]{2,1,0:T(8,128)} %get-tuple-element.73.x3_, ...), custom_call_target="tpu_custom_call" | custom-call | tf_op jit(solution)/shard_map/pallas_call | solution.py:1162
  286.3 106.9 %shard_map.258 = (f32[18,96,768]{2,1,0:T(8,128)}, bf16[8,208,768]{2,1,0:T(8,128)(2,1)}, bf16[8,208,768]{2,1,0:T(8,128)(2,1)}, bf16[8,208,768]{2,1,0:T(8,128)(2,1...) custom-call(bf16[6656,768]{1,0:T(8,128)(2,1)} %bitcast.103, ...), custom_call_target="tpu_custom_call" | custom-call | tf_op jit(solution)/shard_map/pallas_call | solution.py:806
  393.2 1.2 convert.22
  395.7 0.8 convert_reduce_fusion
  397.5 0.9 pad_maximum_fusion.refs_0_
  398.5 109.9 %shard_map.259 = (f32[18,96,768]{2,1,0:T(8,128)}, f32[2,32,768]{2,1,0:T(8,128)}, f32[32,8,128]{2,1,0:T(8,128)}) custom-call(bf16[2,8,32,768]{3,2,1,0:T(8,128)(2,1)} %pad_maximum_fusion.refs_0_, f32[8,768]{1,0:T(8,128)} %get-tuple-element.95.refs_1_, f32[18,96,768]{2,1,0:T(8,128)} %get-tuple-element.96.refs_2_, ...), custom_call_target="tpu_custom_call", output_to_operand_aliasing={{0}: (2, {})} | custom-call | tf_op jit(solution)/shard_map/pallas_call | solution.py:868
  508.4 1.5 reduce_sum.63
  510.8 18.4 %multiply_add_fusion = (f32[18,96,768]{2,1,0:T(8,128)}, f32[18,96,768]{2,1,0:T(8,128)}, f32[18,96,768]{2,1,0:T(8,128)}, f32[18,96,768]{2,1,0:T(8,128)}) fusion(f32[18,96,768]{2,1,0:T(8,128)} %param.21, f32[18,96,768]{2,1,0:T(8,128)} %param.18, f32[18,96,768]{2,1,0:T(8,128)} %get-tuple-element.114, f32[]{:T(128)S(6)} %div.79, f32[18,96,768]{2,1,0:T(8,128)} %param.19, ...), kind=kLoop, calls=%fused_computation.2 | loop fusion | flops 25214976 | bytes 47775748 | tf_op jit(solution)/shard_map/add | solution.py:1209
  529.3 0.8 multiply_add_fusion.4
  530.4 0.8 multiply_add_fusion.2
  (67 shorter events, 7.3 us)
Async XLA Ops:
  0.6 5.8 %copy-start = (bf16[1,8,196,768]{3,1,2,0:T(8,128)(2,1)S(1)}, bf16[1,8,196,768]{3,1,2,0:T(8,128)(2,1)}, u32[]{:S(2)}) copy-start(bf16[1,8,196,768]{3,1,2,0:T(8,128)(2,1)} %param.15) | copy-start | bytes 7225348
  0.7 7.7 %copy-start.10 = (s32[1,8,196]{2,1,0:T(8,128)S(1)}, s32[1,8,196]{2,1,0:T(8,128)}, u32[]{:S(2)}) copy-start(s32[1,8,196]{2,1,0:T(8,128)} %param.16) | copy-start | bytes 18820
  148.9 70.7 %copy-start.11 = (s32[32]{0:T(128)S(1)}, s32[32]{0:T(128)}, u32[]{:S(2)}) copy-start(s32[32]{0:T(128)} %param.17) | copy-start | bytes 388
  510.7 18.5 %copy-start.3 = (f32[2,32,768]{2,1,0:T(8,128)S(1)}, f32[2,32,768]{2,1,0:T(8,128)}, u32[]{:S(2)}) copy-start(f32[2,32,768]{2,1,0:T(8,128)} %get-tuple-element.115) | copy-start | bytes 589828
  510.7 18.6 %copy-start.1 = (f32[96,256]{1,0:T(8,128)S(1)}, f32[96,256]{1,0:T(8,128)}, u32[]{:S(2)}) copy-start(f32[96,256]{1,0:T(8,128)} %param.22) | copy-start | bytes 294916
  510.7 18.6 %copy-start.4 = (f32[96,256]{1,0:T(8,128)S(1)}, f32[96,256]{1,0:T(8,128)}, u32[]{:S(2)}) copy-start(f32[96,256]{1,0:T(8,128)} %param.25) | copy-start | bytes 294916
  510.7 18.6 %copy-start.5 = (f32[96,256]{1,0:T(8,128)S(1)}, f32[96,256]{1,0:T(8,128)}, u32[]{:S(2)}) copy-start(f32[96,256]{1,0:T(8,128)} %param.23) | copy-start | bytes 294916
  510.7 18.6 %copy-start.6 = (f32[96,256]{1,0:T(8,128)S(1)}, f32[96,256]{1,0:T(8,128)}, u32[]{:S(2)}) copy-start(f32[96,256]{1,0:T(8,128)} %param.24) | copy-start | bytes 294916
  510.7 19.6 %copy-start.2 = (f32[227,96]{0,1:T(8,128)S(1)}, f32[227,96]{0,1:T(8,128)}, u32[]{:S(2)}) copy-start(f32[227,96]{0,1:T(8,128)} %param.26) | copy-start | bytes 261508
  510.7 19.6 %copy-start.7 = (f32[227,96]{0,1:T(8,128)S(1)}, f32[227,96]{0,1:T(8,128)}, u32[]{:S(2)}) copy-start(f32[227,96]{0,1:T(8,128)} %param.29) | copy-start | bytes 261508
  510.7 19.6 %copy-start.8 = (f32[227,96]{0,1:T(8,128)S(1)}, f32[227,96]{0,1:T(8,128)}, u32[]{:S(2)}) copy-start(f32[227,96]{0,1:T(8,128)} %param.27) | copy-start | bytes 261508
  510.8 19.6 %copy-start.9 = (f32[227,96]{0,1:T(8,128)S(1)}, f32[227,96]{0,1:T(8,128)}, u32[]{:S(2)}) copy-start(f32[227,96]{0,1:T(8,128)} %param.28) | copy-start | bytes 261508
